TPU v7x, 128 devices: a whole 4x4x4 slice. The times are simulated.
128 devices in a mesh: dp: 8 (over y, x_lo), tensor: 16 (over z, x_hi, core).
Axes of the slice: x: 4 (x_hi: 2, x_lo: 2; x = x_hi * 2 + x_lo), y: 4, z: 4, core: 2. Of those that a mesh axis runs over, the one named last changes fastest.
Arguments:
- hidden: bfloat16 [8, 2048, 1024], P('dp', 'tensor'), may hold values from -6 to 6
- seg_ids: int32 [8, 2048], P('dp'), may hold values from 0 to 7, never falling along the last dimension, each value on 1 to 800 neighbouring positions
- key_mask: int32 [8, 2048], P('dp'), may hold values 0 or 1
- routes: int32 [8, 2048, 8], P('dp'), may hold values from 0 to 31, all different within a row; in each aligned block of 2048 rows (0 to 2047, 2048 to 4095, ..., all dimensions but the last counted through in order) at most 1024 rows name the same one
- gain_attn: bfloat16 [1024], P(('dp', 'tensor')), may hold values from 0.5 to 1.5
- w_query: bfloat16 [1024, 1024], P('dp', 'tensor'), may hold values from -0.1875 to 0.1875
- w_keyval: bfloat16 [1024, 1024], P(('dp', 'tensor')), may hold values from -0.1875 to 0.1875
- w_out: bfloat16 [1024, 1024], P(None, ('dp', 'tensor')), may hold values from -0.5 to 0.5
- gain_mlp: bfloat16 [1024], P(('dp', 'tensor')), may hold values from 0.5 to 1.5
- w_router: bfloat16 [1024, 32], P(('dp', 'tensor')), may hold values from -0.09375 to 0.09375
- w_gate_up: bfloat16 [32, 1024, 1024], P('tensor', 'dp'), may hold values from -0.1875 to 0.1875
- w_down: bfloat16 [32, 512, 1024], P('tensor', None, 'dp'), may hold values from -0.5 to 0.5
- cotangent: bfloat16 [8, 2048, 1024], P('dp', 'tensor'), may hold values from -6 to 6
Outputs:
- output: bfloat16 [8, 2048, 1024], P('dp', 'tensor')
- grad_hidden: bfloat16 [8, 2048, 1024], P('dp', 'tensor')
- grad_gain_attn: float32 [1024], P(('dp', 'tensor'))
- grad_query: float32 [1024, 1024], P('dp', 'tensor')
- grad_keyval: float32 [1024, 1024], P(('dp', 'tensor'))
- grad_out: float32 [1024, 1024], P(None, ('dp', 'tensor'))
- grad_gain_mlp: float32 [1024], P(('dp', 'tensor'))
- grad_router: float32 [1024, 32], P(('dp', 'tensor'))
- grad_gate_up: float32 [32, 1024, 1024], P('tensor', 'dp')
- grad_down: float32 [32, 512, 1024], P('tensor', None, 'dp')
Inputs may be any that keep to these rules, and one draw needn't show every extreme that they name: `routes`: in each sequence no expert is named by more than 1024 tokens, a bound that some block reaches; a token names 8 different experts. `seg_ids`: document numbers never fall along a sequence; a document has at most 800 tokens and some document exactly 800.
All inputs are finite; a program needn't handle non-finite values. No bound on the sum of `key_mask` on one device may be relied on, other than what follows from the above.
Results may differ from a plain program's by a relative error of at most 0.025.
Values may be sent and summed in bfloat16 or wider, within the bound.
A program may use at most 192 MiB of HBM per device.

v0:
```python
import math

import jax
import jax.numpy as jnp
from jax import lax
from jax.sharding import PartitionSpec as P

HEADS = 16
HEAD = 64
KV_HEADS = 8
DOC_MOST = 800


def gather_turned(arrays, axis, dims):
    turned = [jnp.moveaxis(a, dim, 0) for a, dim in zip(arrays, dims)]
    both = jnp.concatenate([t.reshape(len(t), -1) for t in turned], axis=1)
    whole, at, finished = (lax.all_gather(both, axis, axis=0, tiled=True), 0, [])
    for t, dim in zip(turned, dims):
        slab = whole[:, at : at + t[0].size].reshape(-1, *t.shape[1:])
        finished.append(jnp.moveaxis(slab, 0, dim))
        at += t[0].size
    return tuple(finished)


def in_blocks(value, dim, count):
    dims = value.shape
    pieces = value.reshape(*dims[:dim], count, dims[dim] // count, *dims[dim + 1 :])
    return jnp.moveaxis(pieces, dim, 0)


def sum_packed(arrays, axis, dims):
    count = lax.axis_size(axis)
    pieces = [in_blocks(a, dim, count) for a, dim in zip(arrays, dims)]
    lines = jnp.concatenate([b.reshape(count, -1) for b in pieces], axis=1)
    rows = max(16, -(-lines.shape[1] // 1024) * 8)
    lines = jnp.pad(lines, ((0, 0), (0, rows * 128 - lines.shape[1]))).reshape(-1, 128)
    line, at, finished = (lax.psum_scatter(lines, axis, tiled=True).reshape(-1), 0, [])
    for b in pieces:
        part = b[0]
        finished.append(line[at : at + part.size].reshape(part.shape))
        at += part.size
    return tuple(finished)


def matmul(left, right):
    return jnp.dot(left, right, preferred_element_type=jnp.float32)


def contract_rows(left, right):
    return lax.dot_general(
        left, right, (((0,), (0,)), ((), ())), preferred_element_type=jnp.float32
    )


def times_transposed(left, right):
    return lax.dot_general(
        left, right, (((1,), (1,)), ((), ())), preferred_element_type=jnp.float32
    )


def split_float(values):
    upper = values.astype(jnp.bfloat16)
    lower = (values - upper.astype(jnp.float32)).astype(jnp.bfloat16)
    return (upper, lower)


def rope_tables(length, width):
    half = width // 2
    freqs = jnp.exp(jnp.arange(half, dtype=jnp.float32) * (-2.0 * math.log(10000.0) / width))
    angles = jnp.arange(length, dtype=jnp.float32)[:, None] * freqs[None, :]
    return (jnp.cos(angles), jnp.sin(angles))


def rotate(values, cosine, sine):
    length = values.shape[0]
    half = cosine.shape[1]
    shaped = values.reshape(length, -1, 2 * half)
    first = shaped[:, :, :half]
    second = shaped[:, :, half:]
    cos_three = cosine[:, None, :]
    sin_three = sine[:, None, :]
    turned = jnp.concatenate(
        [first * cos_three - second * sin_three, second * cos_three + first * sin_three], axis=-1
    )
    return turned.reshape(length, -1)


def unrotate(grads, cosine, sine):
    length = grads.shape[0]
    half = cosine.shape[1]
    shaped = grads.reshape(length, -1, 2 * half)
    first = shaped[:, :, :half]
    second = shaped[:, :, half:]
    cos_three = cosine[:, None, :]
    sin_three = sine[:, None, :]
    turned = jnp.concatenate(
        [first * cos_three + second * sin_three, second * cos_three - first * sin_three], axis=-1
    )
    return turned.reshape(length, -1)


def block_geometry(length):
    rows = min(512, length)
    reach = (DOC_MOST + 127) // 128 * 128
    window = min(length, rows + reach)
    return (rows, reach, window)


def block_scores(head_query, head_key, segment, live_keys, start, first_key, rows, window):
    scale = 1.0 / math.sqrt(head_query.shape[1])
    query_block = lax.dynamic_slice_in_dim(head_query, start, rows, 0)
    key_block = lax.dynamic_slice_in_dim(head_key, first_key, window, 0)
    query_places = start + jnp.arange(rows, dtype=jnp.int32)
    key_places = first_key + jnp.arange(window, dtype=jnp.int32)
    same_doc = (
        lax.dynamic_slice_in_dim(segment, start, rows, 0)[:, None]
        == lax.dynamic_slice_in_dim(segment, first_key, window, 0)[None, :]
    )
    live_key = lax.dynamic_slice_in_dim(live_keys, first_key, window, 0)[None, :] == 1
    diagonal = key_places[None, :] == query_places[:, None]
    allowed = same_doc & (key_places[None, :] <= query_places[:, None]) & (live_key | diagonal)
    raw = times_transposed(query_block, key_block)
    return (jnp.where(allowed, raw * scale, -1000000000.0), query_block, key_block)


def head_forward(head_query, head_key, head_value, segment, live_keys, length):
    rows, reach, window = block_geometry(length)
    width = head_query.shape[1]

    def one_block(index):
        start = index * rows
        first_key = jnp.clip(start - reach, 0, length - window)
        scores, query_block, key_block = block_scores(
            head_query, head_key, segment, live_keys, start, first_key, rows, window
        )
        value_block = lax.dynamic_slice_in_dim(head_value, first_key, window, 0)
        top = jnp.max(scores, -1)
        weights = jnp.exp(scores - top[:, None])
        totals = jnp.sum(weights, -1)
        probs = weights / totals[:, None]
        block_out = matmul(probs.astype(jnp.bfloat16), value_block).astype(jnp.bfloat16)
        return (block_out, top, totals)

    outs, tops, totals = lax.map(one_block, jnp.arange(length // rows, dtype=jnp.int32))
    return (outs.reshape(length, width), tops.reshape(length), totals.reshape(length))


def head_backward(
    head_query, head_key, head_value, head_grad, tops, totals, segment, live_keys, length
):
    rows, reach, window = block_geometry(length)
    width = head_query.shape[1]
    scale = 1.0 / math.sqrt(width)

    def one_block(carry, index):
        key_sum, value_sum = carry
        start = index * rows
        first_key = jnp.clip(start - reach, 0, length - window)
        scores, query_block, key_block = block_scores(
            head_query, head_key, segment, live_keys, start, first_key, rows, window
        )
        value_block = lax.dynamic_slice_in_dim(head_value, first_key, window, 0)
        grad_block = lax.dynamic_slice_in_dim(head_grad, start, rows, 0)
        top_block = lax.dynamic_slice_in_dim(tops, start, rows, 0)
        total_block = lax.dynamic_slice_in_dim(totals, start, rows, 0)
        probs = jnp.exp(scores - top_block[:, None]) / total_block[:, None]
        probs_low = probs.astype(jnp.bfloat16)
        value_grad = contract_rows(probs_low, grad_block)
        prob_grad = times_transposed(grad_block, value_block)
        row_total = jnp.sum(probs * prob_grad, -1)
        score_grad = (scale * (probs * (prob_grad - row_total[:, None]))).astype(jnp.bfloat16)
        query_grad = matmul(score_grad, key_block)
        key_grad = contract_rows(score_grad, query_block)
        key_sum = lax.dynamic_update_slice_in_dim(
            key_sum,
            lax.dynamic_slice_in_dim(key_sum, first_key, window, 0) + key_grad,
            first_key,
            0,
        )
        value_sum = lax.dynamic_update_slice_in_dim(
            value_sum,
            lax.dynamic_slice_in_dim(value_sum, first_key, window, 0) + value_grad,
            first_key,
            0,
        )
        return ((key_sum, value_sum), query_grad)

    empty = jnp.zeros((length, width), jnp.float32)
    sums, query_grads = lax.scan(
        one_block, (empty, empty), jnp.arange(length // rows, dtype=jnp.int32)
    )
    return (query_grads.reshape(length, width), sums[0], sums[1])


def body(
    hidden,
    seg_ids,
    key_mask,
    routes,
    gain_attn,
    w_query,
    w_keyval,
    w_out,
    gain_mlp,
    w_router,
    w_gate_up,
    w_down,
    cotangent,
):
    local_rows = hidden.shape[1]
    tensor_size = lax.axis_size("tensor")
    rank = lax.axis_index("tensor")
    length = local_rows * tensor_size
    segment = seg_ids[0]
    live_keys = key_mask[0]
    route_ids = routes[0]
    gain_one, gain_two, router, keyval_all, out_all = gather_turned(
        (gain_attn, gain_mlp, w_router, w_keyval, w_out), ("dp", "tensor"), (0, 0, 0, 0, 1)
    )
    query_weight, gate_up, down_weight = gather_turned(
        (w_query, w_gate_up, w_down), "dp", (0, 1, 2)
    )
    local_heads = query_weight.shape[1] // HEAD
    group = HEADS // KV_HEADS
    kv_count = 1
    first_kv = rank * local_heads // group
    keyval_cols = lax.dynamic_slice_in_dim(keyval_all, first_kv * 2 * HEAD, kv_count * 2 * HEAD, 1)
    gain_one_f = gain_one.astype(jnp.float32)
    gain_two_f = gain_two.astype(jnp.float32)
    hidden_f = hidden[0].astype(jnp.float32)
    inv_one = lax.rsqrt(jnp.mean(hidden_f * hidden_f, -1, keepdims=True) + 1e-06)
    unit_one = hidden_f * inv_one
    normed_local = (unit_one * gain_one_f).astype(jnp.bfloat16)
    normed = lax.all_gather(normed_local, "tensor", axis=0, tiled=True)
    cosine, sine = rope_tables(length, HEAD)
    query_pre = matmul(normed, query_weight)
    queries = rotate(query_pre, cosine, sine).astype(jnp.bfloat16)
    keyval_pre = matmul(normed, keyval_cols).reshape(length, kv_count, 2, HEAD)
    keys = rotate(keyval_pre[:, :, 0, :].reshape(length, kv_count * HEAD), cosine, sine).astype(
        jnp.bfloat16
    )
    values = keyval_pre[:, :, 1, :].reshape(length, kv_count * HEAD).astype(jnp.bfloat16)
    out_head, top_head, total_head = head_forward(queries, keys, values, segment, live_keys, length)
    attended_rows = lax.all_to_all(out_head, "tensor", split_axis=0, concat_axis=1, tiled=True)
    attn_local = matmul(attended_rows, out_all)
    mid = hidden_f + attn_local
    inv_two = lax.rsqrt(jnp.mean(mid * mid, -1, keepdims=True) + 1e-06)
    unit_two = mid * inv_two
    normed_mid_local = (unit_two * gain_two_f).astype(jnp.bfloat16)
    normed_mid = lax.all_gather(normed_mid_local, "tensor", axis=0, tiled=True)
    logits = matmul(normed_mid, router)
    chosen = jnp.take_along_axis(logits, route_ids, axis=1)
    gates = jax.nn.softmax(chosen, axis=-1)
    local_experts = gate_up.shape[0]
    hidden_units = down_weight.shape[1]
    capacity = length // 2
    kept = []
    moe_part = jnp.zeros((length, normed.shape[1]), jnp.float32)
    for expert in range(local_experts):
        expert_id = rank * local_experts + expert
        hits = route_ids == expert_id
        used = jnp.any(hits, 1)
        weight = jnp.sum(jnp.where(hits, gates, 0.0), 1)
        slot = jnp.cumsum(used.astype(jnp.int32), dtype=jnp.int32) - 1
        filled = jnp.sum(used.astype(jnp.int32), dtype=jnp.int32)
        target = jnp.where(used, slot, capacity)
        source_rows = (
            jnp.zeros((capacity,), jnp.int32)
            .at[target]
            .set(jnp.arange(length, dtype=jnp.int32), mode="drop")
        )
        live = jnp.arange(capacity, dtype=jnp.int32) < filled
        buffer = jnp.where(live[:, None], normed_mid[source_rows], jnp.zeros((), jnp.bfloat16))
        projected = matmul(buffer, gate_up[expert])
        gate_part = projected[:, :hidden_units]
        up_part = projected[:, hidden_units:]
        activated = (jax.nn.silu(gate_part) * up_part).astype(jnp.bfloat16)
        expert_out = matmul(activated, down_weight[expert])
        back_slot = jnp.clip(slot, 0, capacity - 1)
        moe_part = moe_part + jnp.where(used[:, None], weight[:, None] * expert_out[back_slot], 0.0)
        kept.append(
            (
                hits,
                used,
                weight,
                source_rows,
                live,
                back_slot,
                buffer,
                gate_part,
                up_part,
                activated,
                expert_out,
            )
        )
    moe_local = lax.psum_scatter(
        moe_part.astype(jnp.bfloat16), "tensor", scatter_dimension=0, tiled=True
    ).astype(jnp.float32)
    output = (mid + moe_local).astype(jnp.bfloat16)
    cot_local = cotangent[0]
    cot_all = lax.all_gather(cot_local, "tensor", axis=0, tiled=True)
    normed_mid_part = jnp.zeros((length, normed.shape[1]), jnp.float32)
    gate_grads = jnp.zeros(gates.shape, jnp.float32)
    gate_up_grads = []
    down_grads = []
    for expert in range(local_experts):
        (
            hits,
            used,
            weight,
            source_rows,
            live,
            back_slot,
            buffer,
            gate_part,
            up_part,
            activated,
            expert_out,
        ) = kept[expert]
        row_cot = cot_all[source_rows].astype(jnp.float32)
        row_weight = weight[source_rows]
        out_grad = jnp.where(live[:, None], row_weight[:, None] * row_cot, 0.0).astype(jnp.bfloat16)
        down_grads.append(contract_rows(activated, out_grad))
        act_grad = times_transposed(out_grad, down_weight[expert])
        sigmoid_gate = jax.nn.sigmoid(gate_part)
        gate_grad = act_grad * up_part * (sigmoid_gate * (1.0 + gate_part * (1.0 - sigmoid_gate)))
        up_grad = act_grad * (gate_part * sigmoid_gate)
        proj_grad = jnp.concatenate([gate_grad, up_grad], axis=1).astype(jnp.bfloat16)
        gate_up_grads.append(contract_rows(buffer, proj_grad))
        buffer_grad = times_transposed(proj_grad, gate_up[expert])
        normed_mid_part = normed_mid_part + jnp.where(used[:, None], buffer_grad[back_slot], 0.0)
        slot_dot = jnp.where(live, jnp.sum(row_cot * expert_out, -1), 0.0)
        token_dot = jnp.where(used, slot_dot[back_slot], 0.0)
        gate_grads = gate_grads + jnp.where(hits, token_dot[:, None], 0.0)
    mean_term = jnp.sum(gates * gate_grads, 1, keepdims=True)
    chosen_grad = gates * (gate_grads - mean_term)
    expert_cols = jnp.arange(router.shape[1], dtype=jnp.int32)
    logit_grad = jnp.sum(
        jnp.where(
            route_ids[:, :, None] == expert_cols[None, None, :], chosen_grad[:, :, None], 0.0
        ),
        1,
    )
    logit_upper, logit_lower = split_float(logit_grad)
    router_grad = contract_rows(normed_mid, logit_upper) + contract_rows(normed_mid, logit_lower)
    normed_mid_part = (
        normed_mid_part
        + times_transposed(logit_upper, router)
        + times_transposed(logit_lower, router)
    )
    normed_mid_grad = lax.psum_scatter(
        normed_mid_part.astype(jnp.bfloat16), "tensor", scatter_dimension=0, tiled=True
    ).astype(jnp.float32)
    scaled_two = normed_mid_grad * gain_two_f
    gain_two_grad = jnp.sum(normed_mid_grad * unit_two, 0)
    mid_grad = cot_local.astype(jnp.float32) + inv_two * (
        scaled_two - unit_two * jnp.mean(scaled_two * unit_two, -1, keepdims=True)
    )
    mid_grad_low = mid_grad.astype(jnp.bfloat16)
    row_grads = times_transposed(mid_grad_low, out_all).astype(jnp.bfloat16)
    out_grad_full = contract_rows(attended_rows, mid_grad_low)
    attended_grad = lax.all_to_all(row_grads, "tensor", split_axis=1, concat_axis=0, tiled=True)
    key_sums = [jnp.zeros((length, HEAD), jnp.float32)]
    value_sums = [jnp.zeros((length, HEAD), jnp.float32)]
    query_grad, key_grad, value_grad = head_backward(
        queries, keys, values, attended_grad, top_head, total_head, segment, live_keys, length
    )
    key_sums[0] = key_grad
    value_sums[0] = value_grad
    query_pre_grad = unrotate(query_grad, cosine, sine).astype(jnp.bfloat16)
    key_pre_grad = unrotate(key_sums[0], cosine, sine).reshape(length, kv_count, HEAD)
    value_pre_grad = value_sums[0].reshape(length, kv_count, HEAD)
    keyval_grad = jnp.stack([key_pre_grad, value_pre_grad], axis=2).reshape(
        length, kv_count * 2 * HEAD
    )
    keyval_upper, keyval_lower = split_float(keyval_grad)
    query_weight_grad = contract_rows(normed, query_pre_grad)
    keyval_part = contract_rows(normed, keyval_upper) + contract_rows(normed, keyval_lower)
    keyval_weight_grad = lax.dynamic_update_slice_in_dim(
        jnp.zeros(keyval_all.shape, jnp.float32), keyval_part, first_kv * 2 * HEAD, 1
    )
    normed_part = (
        times_transposed(query_pre_grad, query_weight)
        + times_transposed(keyval_upper, keyval_cols)
        + times_transposed(keyval_lower, keyval_cols)
    )
    normed_grad = lax.psum_scatter(
        normed_part.astype(jnp.bfloat16), "tensor", scatter_dimension=0, tiled=True
    ).astype(jnp.float32)
    scaled_one = normed_grad * gain_one_f
    gain_one_grad = jnp.sum(normed_grad * unit_one, 0)
    hidden_grad = mid_grad + inv_one * (
        scaled_one - unit_one * jnp.mean(scaled_one * unit_one, -1, keepdims=True)
    )
    query_sum, gate_up_sum, down_sum = tuple(
        (
            part.astype(jnp.float32)
            for part in sum_packed(
                (
                    query_weight_grad.astype(jnp.bfloat16),
                    jnp.stack(gate_up_grads).astype(jnp.bfloat16),
                    jnp.stack(down_grads).astype(jnp.bfloat16),
                ),
                "dp",
                (0, 1, 2),
            )
        )
    )
    gain_one_sum, gain_two_sum, router_sum, keyval_sum, out_sum = sum_packed(
        (gain_one_grad, gain_two_grad, router_grad, keyval_weight_grad, out_grad_full),
        ("dp", "tensor"),
        (0, 0, 0, 0, 1),
    )
    return (
        output[None],
        hidden_grad.astype(jnp.bfloat16)[None],
        gain_one_sum,
        query_sum,
        keyval_sum,
        out_sum,
        gain_two_sum,
        router_sum,
        gate_up_sum,
        down_sum,
    )


def solution(mesh):
    return jax.shard_map(
        body,
        mesh=mesh,
        in_specs=(
            P("dp", "tensor", None),
            P("dp", None),
            P("dp", None),
            P("dp", None, None),
            P(("dp", "tensor")),
            P("dp", "tensor"),
            P(("dp", "tensor"), None),
            P(None, ("dp", "tensor")),
            P(("dp", "tensor")),
            P(("dp", "tensor"), None),
            P("tensor", "dp", None),
            P("tensor", None, "dp"),
            P("dp", "tensor", None),
        ),
        out_specs=(
            P("dp", "tensor", None),
            P("dp", "tensor", None),
            P(("dp", "tensor")),
            P("dp", "tensor"),
            P(("dp", "tensor"), None),
            P(None, ("dp", "tensor")),
            P(("dp", "tensor")),
            P(("dp", "tensor"), None),
            P("tensor", "dp", None),
            P("tensor", None, "dp"),
        ),
        check_vma=False,
    )
```

profile of v0, /device:TPU:1, one launch (start us, length us, event | category | flops | bytes accessed | tf_op | source)
XLA Modules:
  0.0 1957.9 jit_solution(7507236140244343860)
XLA Ops:
  11.4 201.2 %all-gather.7.cloned.1.call-done = bf16[1024,2082]{1,0:T(8,128)(2,1)} async-done(((bf16[8,2082]{1,0:T(8,128)(2,1)}), bf16[1024,2082]{1,0:T(8,128)(2,1)}) %all-gather.7.cloned.1.call-update) | async-done | bytes 4263952 | tf_op jit(solution)/shard_map/all_gather | solution.py:17
  222.9 48.3 %all-gather.9.cloned.1.call-done = bf16[2048,1024]{1,0:T(8,128)(2,1)} async-done(((bf16[128,1024]{1,0:T(8,128)(2,1)}), bf16[2048,1024]{1,0:T(8,128)(2,1)}) %all-gather.9.cloned.1.call-update) | async-done | bytes 4194320 | tf_op jit(solution)/shard_map/all_gather | solution.py:234
  275.0 126.9 %all-gather.11.cloned.1.call-done = bf16[1024,3136]{0,1:T(8,128)(2,1)} async-done(((bf16[128,3136]{0,1:T(8,128)(2,1)}), bf16[1024,3136]{0,1:T(8,128)(2,1)}) %all-gather.11.cloned.1.call-update) | async-done | bytes 6422544 | tf_op jit(solution)/shard_map/all_gather | solution.py:17
  408.4 31.3 %while.32 = (s32[]{:T(128)}, bf16[4,512,64]{1,2,0:T(8,128)(2,1)S(1)}, f32[4,512]{1,0:T(4,128)}, f32[4,512]{1,0:T(4,128)}, s32[4]{0:T(128)S(1)}, /*index=5*/s32[2...) while((s32[]{:T(128)}, ...), condition=%wide.region_4.5_spmd, body=%wide.region_1.4_spmd.sunk | while | flops 194676992 | bytes 9639591 | solution.py:144
  440.1 16.9 all_to_all.38
  465.7 8.0 scatter_custom_fusion
  473.8 8.0 scatter_custom_fusion.1
  486.2 7.7 gather_fusion.8
  493.9 9.3 gather_fusion.5
  509.7 4.8 slice.206
  514.5 6.2 copy.166
  527.4 130.6 %gather_fusion.12 = f32[16384]{0:T(1024)S(1)} fusion(f32[2048,32]{0,1:T(8,128)S(1)} %fusion.108, s32[16384]{0:T(1024)S(1)} %reshape.706), kind=kCustom, calls=%fused_computation.12 | custom fusion | bytes 262144 | tf_op jit(solution)/shard_map/jit(take_along_axis)/gather | solution.py:252
  659.6 8.8 gather_fusion.2
  672.3 8.8 gather_fusion
  685.5 4.8 fusion.40
  704.6 8.6 gather_fusion.10
  713.3 5.2 fusion.34
  719.2 8.6 gather_fusion.11
  728.4 4.9 multiply_reduce_fusion.1
  733.3 6.6 gather_fusion.4
  739.9 5.7 multiply_convert_fusion.4
  745.6 6.2 gather_fusion.7
  751.9 5.9 multiply_convert_fusion.2
  761.1 6.7 fusion.37
  767.7 13.9 gather_fusion.6
  781.6 6.6 fusion.39
  788.2 13.9 gather_fusion.9
  806.0 7.2 add_convert_fusion.1
  813.3 5.4 copy.167
  818.7 14.0 gather_fusion.1
  832.7 5.4 copy.169
  838.1 13.9 gather_fusion.3
  852.0 8.9 add_convert_fusion.2
  874.5 15.0 reduce-scatter.11.cloned.1.call-done
  890.7 82.8 %reduce-scatter.9.cloned.1.call-done = bf16[128,1024]{1,0:T(8,128)(2,1)} async-done(((bf16[2048,1024]{1,0:T(8,128)(2,1)}), bf16[128,1024]{1,0:T(8,128)(2,1)}) %reduce-scatter.9.cloned.1.call-update) | async-done | bytes 262160 | tf_op jit(solution)/shard_map/reduce_scatter | solution.py:296
  979.7 6.0 all-to-all-start.1
  995.1 69.0 %while.33 = (s32[]{:T(128)}, f32[2048,64]{0,1:T(8,128)S(1)}, f32[2048,64]{0,1:T(8,128)S(1)}, f32[4,512,64]{1,0,2:T(4,128)}, s32[4]{0:T(128)S(1)}, /*index=5*/s32...) while((s32[]{:T(128)}, f32[2048,64]{0,1:T(8,128)S(1)}, ...), condition=%wide.region_29.30_spmd, body=%wide.region_27.29_spmd.sunk | while | flops 473811712 | bytes 26840800 | solution.py:189
  1080.6 17.8 pad_maximum_fusion
  1098.4 8.7 reshape.599
  1118.1 5.9 copy.188
  1132.1 5.4 copy.184
  1137.5 5.0 reshape_reshape.14
  1142.5 17.2 reduce-scatter.13.cloned.1.call-done
  1161.1 13.4 concatenate.47
  1174.5 7.8 pad.4
  1182.3 9.7 reshape.595
  1194.1 100.8 %reduce-scatter.15.cloned.1.call-done = bf16[3136,128]{1,0:T(8,128)(2,1)} async-done(((bf16[25088,128]{1,0:T(8,128)(2,1)}), bf16[3136,128]{1,0:T(8,128)(2,1)}) %reduce-scatter.15.cloned.1.call-update) | async-done | bytes 802832 | tf_op jit(solution)/shard_map/reduce_scatter | solution.py:37
  1299.5 644.6 %reduce-scatter.17.cloned.1.call-done = f32[136,128]{1,0:T(8,128)} async-done(((f32[17408,128]{1,0:T(8,128)}), f32[136,128]{1,0:T(8,128)}) %reduce-scatter.17.cloned.1.call-update) | async-done | bytes 69648
  (458 shorter events, 258.3 us)
Async XLA Ops:
  7.2 210.7 %copy-start.48 = (bf16[2,512,128]{2,1,0:T(8,128)(2,1)S(1)}, bf16[2,512,128]{2,1,0:T(8,128)(2,1)}, u32[]{:S(2)}) copy-start(bf16[2,512,128]{2,1,0:T(8,128)(2,1)} %param.28) | copy-start | bytes 786436
  7.2 205.4 %all-gather.7.cloned.1.call-start = ((), (), s32[]{:S(2)}) async-start(), calls=%async_computation.7 | async-start | bytes 4491264 | tf_op jit(solution)/shard_map/all_gather | solution.py:17
  10.2 261.0 %all-gather.9.cloned.1.call-start = ((), (), s32[]{:S(2)}) async-start(), calls=%async_computation.8 | async-start | bytes 4456448 | tf_op jit(solution)/shard_map/all_gather | solution.py:234
  11.4 205.1 %copy-start.73 = (f32[128]{0:T(128)}, f32[128]{0:T(128)S(1)}, u32[]{:S(2)}) copy-start(f32[128]{0:T(128)S(1)} %add_rsqrt_fusion.1) | copy-start | bytes 1540
  214.1 246.0 %copy-start.63 = (f32[1024]{0:T(1024)}, f32[1024]{0:T(1024)S(1)}, u32[]{:S(2)}) copy-start(f32[1024]{0:T(1024)S(1)} %get-tuple-element.461) | copy-start | bytes 12292
  216.5 185.4 %all-gather.11.cloned.1.call-start = ((), (), s32[]{:S(2)}) async-start(), calls=%async_computation.9 | async-start | bytes 7225344 | tf_op jit(solution)/shard_map/all_gather | solution.py:17
  219.5 266.6 %all-gather.15.cloned.1.call-start = ((), (), s32[]{:S(2)}) async-start(), calls=%async_computation.15 | async-start | bytes 4456448 | tf_op jit(solution)/shard_map/all_gather | solution.py:301
  220.1 303.7 %all-gather.13.cloned.1.call-start = ((), (), s32[]{:S(2)}) async-start(), calls=%async_computation.10 | async-start | bytes 4456448 | tf_op jit(solution)/shard_map/all_gather | solution.py:250
  220.2 185.3 %copy-start.77 = (f32[32]{0:T(128)}, f32[32]{0:T(128)S(1)}, u32[]{:S(2)}) copy-start(f32[32]{0:T(128)S(1)} %multiply_exponential_fusion) | copy-start | bytes 388
  222.9 52.0 %copy-start.26 = (bf16[1024,1024]{1,0:T(8,128)(2,1)}, bf16[1024,1024]{1,0:T(8,128)(2,1)S(1)}, u32[]{:S(2)}) copy-start(bf16[1024,1024]{1,0:T(8,128)(2,1)S(1)} %slice.196) | copy-start | bytes 6291460
  408.4 48.6 %copy-start.24 = (bf16[1,128,1024]{2,1,0:T(8,128)(2,1)S(1)}, bf16[1,128,1024]{2,1,0:T(8,128)(2,1)}, u32[]{:S(2)}) copy-start(bf16[1,128,1024]{2,1,0:T(8,128)(2,1)} %param.17) | copy-start | bytes 786436
  439.7 21.9 %copy-start.9 = (bf16[2048,64]{1,0:T(8,128)(2,1)}, bf16[2048,64]{1,0:T(8,128)(2,1)S(1)}, u32[]{:S(2)}) copy-start(bf16[2048,64]{1,0:T(8,128)(2,1)S(1)} %get-tuple-element.842) | copy-start | bytes 786436
  439.7 21.9 %copy-start.11 = (bf16[2048,64]{1,0:T(8,128)(2,1)}, bf16[2048,64]{1,0:T(8,128)(2,1)S(1)}, u32[]{:S(2)}) copy-start(bf16[2048,64]{1,0:T(8,128)(2,1)S(1)} %get-tuple-element.843) | copy-start | bytes 786436
  440.0 21.9 %copy-start.46 = (s32[1,2048,8]{1,2,0:T(8,128)S(1)}, s32[1,2048,8]{1,2,0:T(8,128)}, u32[]{:S(2)}) copy-start(s32[1,2048,8]{1,2,0:T(8,128)} %param.20) | copy-start | bytes 196612
  461.7 427.8 %reduce-scatter.11.cloned.1.call-start = ((), (), s32[]{:S(2)}) async-start(), calls=%async_computation.12 | async-start | bytes 4456448 | tf_op jit(solution)/shard_map/reduce_scatter | solution.py:351
  462.3 31.6 %copy-start.4 = (s32[1,2048,8]{2,1,0:T(8,128)}, s32[1,2048,8]{2,1,0:T(8,128)S(1)}, u32[]{:S(2)}) copy-start(s32[1,2048,8]{2,1,0:T(8,128)S(1)} %copy.163) | copy-start | bytes 196612
  464.5 21.7 %copy-start.51 = (pred[2048]{0:T(1024)(128)(4,1)}, pred[2048]{0:T(1024)(128)(4,1)S(1)}, u32[]{:S(2)}) copy-start(pred[2048]{0:T(1024)(128)(4,1)S(1)} %get-tuple-element.521) | copy-start | bytes 6148
  464.5 21.7 %copy-start.54 = (pred[2048]{0:T(1024)(128)(4,1)}, pred[2048]{0:T(1024)(128)(4,1)S(1)}, u32[]{:S(2)}) copy-start(pred[2048]{0:T(1024)(128)(4,1)S(1)} %get-tuple-element.533) | copy-start | bytes 6148
  484.9 9.0 copy-start.68
  485.0 9.0 copy-start.65
  527.4 131.2 %copy-start.5 = (s32[1,2048,8]{2,1,0:T(8,128)S(1)}, s32[1,2048,8]{2,1,0:T(8,128)}, u32[]{:S(2)}) copy-start(s32[1,2048,8]{2,1,0:T(8,128)} %copy-done.4) | copy-start | bytes 196612
  685.5 7.0 copy-start.31
  696.5 7.4 copy-start.21
  697.2 6.8 copy-start.17
  704.6 8.6 copy-start.52
  713.2 14.6 copy-start.57
  719.2 8.6 copy-start.55
  719.2 9.2 copy-start.27
  733.3 6.6 copy-start.8
  733.3 6.6 copy-start.83
  745.6 6.2 copy-start.6
  745.6 6.2 copy-start.80
  751.8 5.9 copy-start.22
  751.8 5.9 copy-start.28
  788.2 13.9 copy-start.47
  813.2 160.3 %reduce-scatter.9.cloned.1.call-start = ((), (), s32[]{:S(2)}) async-start(), calls=%async_computation.11 | async-start | bytes 4456448 | tf_op jit(solution)/shard_map/reduce_scatter | solution.py:296
  870.7 18.8 copy-start.19
  870.7 18.8 copy-start.64
  870.7 18.8 copy-start.76
  870.7 102.8 %copy-start.37 = (bf16[1,128,1024]{2,1,0:T(8,128)(2,1)S(1)}, bf16[1,128,1024]{2,1,0:T(8,128)(2,1)}, u32[]{:S(2)}) copy-start(bf16[1,128,1024]{2,1,0:T(8,128)(2,1)} %param.29) | copy-start | bytes 786436
  979.7 14.9 all-to-all-start.1
  985.7 174.0 %reduce-scatter.13.cloned.1.call-start = ((), (), s32[]{:S(2)}) async-start(), calls=%async_computation.13 | async-start | bytes 4456448 | tf_op jit(solution)/shard_map/reduce_scatter | solution.py:387
  995.1 70.5 %copy-start.78 = (f32[32]{0:T(128)S(1)}, f32[32]{0:T(128)}, u32[]{:S(2)}) copy-start(f32[32]{0:T(128)} %copy-done.77) | copy-start | bytes 388
  1079.0 215.8 %reduce-scatter.15.cloned.1.call-start = ((), (), s32[]{:S(2)}) async-start(), calls=%async_computation.14 | async-start | bytes 7225344 | tf_op jit(solution)/shard_map/reduce_scatter | solution.py:37
  1107.0 837.1 %reduce-scatter.17.cloned.1.call-start = ((), (), s32[]{:S(2)}) async-start(), calls=%async_computation.16 | async-start | bytes 8982528
  1137.5 22.2 %copy-start.25 = (bf16[1,128,1024]{2,1,0:T(8,128)(2,1)S(1)}, bf16[1,128,1024]{2,1,0:T(8,128)(2,1)}, u32[]{:S(2)}) copy-start(bf16[1,128,1024]{2,1,0:T(8,128)(2,1)} %param.17) | copy-start | bytes 786436
  1137.5 22.2 %copy-start.62 = (f32[1024]{0:T(1024)S(1)}, f32[1024]{0:T(1024)}, u32[]{:S(2)}) copy-start(f32[1024]{0:T(1024)} %copy-done.61) | copy-start | bytes 12292
  1137.5 22.2 %copy-start.74 = (f32[128]{0:T(128)S(1)}, f32[128]{0:T(128)}, u32[]{:S(2)}) copy-start(f32[128]{0:T(128)} %copy-done.73) | copy-start | bytes 1540
  (53 other events, 148.1 us)
Sparse Core Ops, SparseCore 0:
  10.4 202.1 all-gather.6
  216.6 54.5 all-gather.8
  273.3 128.5 all-gather.10
  404.2 57.8 all-gather.14
  464.4 53.8 all-gather.12
  813.4 76.0 reduce-scatter.10
  894.0 79.4 reduce-scatter.8
  1079.1 80.5 reduce-scatter.12
  1162.3 132.5 reduce-scatter.14
  1297.1 646.9 reduce-scatter.16
where the time goes:
time: 1980 us; the launch traced here: 1960 us
  waiting for transfers between devices  1240 us (63%)
  local copies, waits for them, and re-layouts  472 us (24%)
  matrix products  133 us (7%)
  other arithmetic  69.6 us (4%)
    unnamed x11, waiting for transfers between devices  645 us
    all_gather x2, waiting for transfers between devices, gather_turned(): lax.all_gather(both, axis, axis=0, tiled=True)  328 us
    gather x4, local copies, waits for them, and re-layouts, body(): chosen = jnp.take_along_axis(logits, route_ids, axis=1)  132 us
    reduce_scatter x1, waiting for transfers between devices, sum_packed(): lax.psum_scatter(lines, axis, tiled=True).reshape(-1)  101 us
    reduce_scatter x1, waiting for transfers between devices, body(): lax.psum_scatter(moe_part.astype(jnp.bfloat16), 'tensor', scatter_dimensi...  82.8 us
    dot_general x22, matrix products, times_transposed(): lax.dot_general(left, right, (((1,), (1,)), ((), ())), preferred_element_...  68.4 us
    all_gather x1, waiting for transfers between devices, body(): normed = lax.all_gather(normed_local, 'tensor', axis=0, tiled=True)  48.3 us
  transfers between devices with their start and end apart: 11, of which 8 were waited for; matrix products, arithmetic and copies ran while one was open for 14% of the time, Pallas kernels for 0%

commit v1 on v0

v1 whole, which is shorter than its diff:
```python
import math

import jax
import jax.numpy as jnp
import numpy as np
from jax import lax
from jax.experimental import pallas as pl
from jax.experimental.pallas import tpu as pltpu
from jax.sharding import PartitionSpec as P

HEAD = 64
LENGTH = 2048
WIDTH = 1024
UNITS = 512
ROWS = 128
PAIR = 256
REACH = 896
SPAN = REACH + PAIR
PADDED = REACH + LENGTH
CHIPS = 8
TENSOR = 16
DP = 8
TAIL = 304
SLOTS = 4
LOWEST = -1e30
BF = jnp.bfloat16
F32 = jnp.float32
MESH = pl.DeviceIdType.MESH
VMEM_BYTES = 60 * 1024 * 1024

NN = (((1,), (0,)), ((), ()))
NT = (((1,), (1,)), ((), ()))


def dot(left, right, dims=NN):
    return lax.dot_general(left, right, dims, preferred_element_type=F32)


def aligned(value, size):
    return pl.ds(pl.multiple_of(value * size, size), size)


def remote(src, dst, send, recv, axis, index):
    return pltpu.make_async_remote_copy(
        src_ref=src,
        dst_ref=dst,
        send_sem=send,
        recv_sem=recv,
        device_id={axis: index},
        device_id_type=MESH,
    )


class Place:
    def __init__(self):
        self.t = lax.axis_index("tensor")
        self.d = lax.axis_index("dp")
        self.core = lax.rem(self.t, 2)
        self.chip = self.t // 2
        self.twin = self.t + 1 - 2 * self.core
        self.x = lax.rem(self.d, 2)
        self.y = self.d // 2
        self.across = self.d + 1 - 2 * self.x

    def chip_at(self, k):
        return lax.rem(self.chip + k, CHIPS)

    def same_core(self, k):
        return 2 * self.chip_at(k) + self.core

    def tensor_at(self, k):
        return lax.rem(self.t + k, TENSOR)

    def dp_at(self, k):
        return lax.rem(self.d + k, DP)

    def y_at(self, k):
        return lax.rem(self.y + k, 4)

    def enter(self):
        barrier = pltpu.get_barrier_semaphore()
        for k in range(1, TENSOR):
            pl.semaphore_signal(
                barrier, inc=1, device_id={"tensor": self.tensor_at(k)}, device_id_type=MESH
            )
        for k in range(1, DP):
            pl.semaphore_signal(
                barrier, inc=1, device_id={"dp": self.dp_at(k)}, device_id_type=MESH
            )
        pl.semaphore_wait(barrier, TENSOR + DP - 2)


class Spread:
    def __init__(self, place, block, send, recv, source=None):
        self.place, self.block, self.send, self.recv = place, block, send, recv
        self.source = source

    def copy(self, number, index, dest, source=None):
        src = self.block(index) if source is None else source
        return remote(
            src, self.block(index), self.send.at[number], self.recv.at[index], "tensor", dest
        )

    def own(self, k):
        dest = self.place.twin if k == 0 else self.place.same_core(k)
        return self.copy(k, self.place.t, dest, self.source)

    def start(self):
        for k in range(1, CHIPS):
            self.own(k).start()
        self.own(0).start()

    def passed(self, k):
        return self.copy(CHIPS + k, self.place.same_core(k), self.place.twin)

    def arrived(self, index):
        self.copy(0, index, self.place.twin).wait_recv()

    def first(self, k):
        self.arrived(self.place.same_core(k))
        self.passed(k).start()

    def second(self, k):
        self.arrived(2 * self.place.chip_at(k) + 1 - self.place.core)

    def end(self):
        for k in range(CHIPS):
            self.own(k).wait_send()
        for k in range(1, CHIPS):
            self.passed(k).wait_send()


def lanes(shape):
    return lax.broadcasted_iota(jnp.int32, shape, len(shape) - 1)


def sublanes(shape):
    return lax.broadcasted_iota(jnp.int32, shape, 0)


def swapped(values):
    return jnp.where(
        lanes(values.shape) < HEAD // 2,
        pltpu.roll(values, 2 * HEAD - HEAD // 2, 1),
        pltpu.roll(values, HEAD // 2, 1),
    )


def document_starts(seg):
    starts = jnp.zeros(seg.shape, F32)
    for document in range(8):
        before = jnp.sum(jnp.where(seg < document, 1.0, 0.0), axis=1, keepdims=True)
        starts = starts + jnp.where(seg == document, before, 0.0)
    return starts


def key_codes(meta, code):
    code[0:REACH, :] = jnp.full((REACH, ROWS), -1.0, F32)

    @pl.loop(0, CHIPS)
    def _(i):
        live = meta[aligned(i, PAIR), 8:9] == 1
        places = (sublanes((PAIR, ROWS)) + i * PAIR).astype(F32)
        code[pl.ds(pl.multiple_of(REACH + i * PAIR, ROWS), PAIR), :] = jnp.where(
            live, places, -1.0
        )


def allowed(code, start_row, chunk):
    wide = jnp.concatenate([code, code], axis=1)
    ok = wide >= start_row
    if chunk >= REACH // ROWS:
        key = sublanes((ROWS, PAIR)) + (chunk * ROWS - REACH)
        query = lanes((ROWS, PAIR))
        ok = (ok & (key < query)) | (key == query)
    return ok


def attention_kernel(
    hid,
    cot,
    tiles,
    wq,
    rows,
    gu,
    down,
    cosine,
    sine,
    meta,
    seg,
    normed,
    queries,
    keyvals,
    keyvals_t,
    stats,
    heads_t,
    mid,
    normed_mid,
    wq_all,
    out_t,
    kv_full,
    small,
    gu_all,
    down_all,
    cot_all,
    hidden_all,
    tile_all,
    row_all,
    code,
    scores,
    probs,
    starts,
    wkv,
    att_src,
    att_t,
    h_send,
    h_recv,
    r_send,
    r_recv,
    c_send,
    c_recv,
    t1_send,
    t1_recv,
    t2_send,
    t2_recv,
    rd_send,
    rd_recv,
    wq_send,
    wq_recv,
    gu_send,
    gu_recv,
    dn_send,
    dn_recv,
    a_send,
    a_recv,
    local,
):
    at = Place()
    t, d = at.t, at.d
    hidden_all[aligned(t, ROWS), :] = hid[...]
    tile_all[d, t] = tiles[t]
    row_all[d, t] = rows[...]
    wq_all[HEAD : 2 * HEAD, :] = jnp.zeros((HEAD, WIDTH), BF)
    wq_all[0:HEAD, aligned(d, ROWS)] = wq[...]
    at.enter()

    spread_h = Spread(at, lambda b: hidden_all.at[aligned(b, ROWS)], h_send, h_recv)
    spread_r = Spread(at, lambda b: row_all.at[:, b], r_send, r_recv)
    spread_c = Spread(at, lambda b: cot_all.at[aligned(b, ROWS)], c_send, c_recv, cot)

    def tile_one(k, src):
        dest = at.tensor_at(k)
        return remote(
            tiles.at[dest], tile_all.at[d, src], t1_send.at[k], t1_recv.at[src], "tensor", dest
        )

    def tile_two(k, src):
        return remote(
            tile_all.at[src], tile_all.at[src], t2_send.at[k], t2_recv.at[src], "dp", at.dp_at(k)
        )

    def rows_dp(k, src):
        return remote(
            rows, row_all.at[src, t], rd_send.at[k], rd_recv.at[src], "dp", at.dp_at(k)
        )

    def wq_dp(k, src):
        return remote(
            wq,
            wq_all.at[pl.ds(0, HEAD), aligned(src, ROWS)],
            wq_send.at[k],
            wq_recv.at[src],
            "dp",
            at.dp_at(k),
        )

    def gu_block(s):
        return gu_all.at[:, aligned(s, ROWS), :]

    def down_block(s):
        return down_all.at[:, :, aligned(s, ROWS)]

    def expert(k, src, dest, first):
        return (
            remote(
                gu if first else gu_block(src),
                gu_block(src),
                gu_send.at[k],
                gu_recv.at[src],
                "dp",
                dest,
            ),
            remote(
                down if first else down_block(src),
                down_block(src),
                dn_send.at[k],
                dn_recv.at[src],
                "dp",
                dest,
            ),
        )

    def y_peer(k):
        return 2 * at.y_at(k) + at.x

    for k in range(1, TENSOR):
        tile_one(k, t).start()
    for k in range(1, DP):
        wq_dp(k, d).start()
        rows_dp(k, d).start()
    spread_h.start()
    for copy in expert(0, d, at.across, True):
        copy.start()
    for k in range(1, 4):
        for copy in expert(k, d, y_peer(k), True):
            copy.start()
    own_copies = (
        pltpu.make_async_copy(gu, gu_block(d), local.at[0]),
        pltpu.make_async_copy(down, down_block(d), local.at[1]),
        pltpu.make_async_copy(cot, cot_all.at[aligned(t, ROWS)], local.at[2]),
    )
    for copy in own_copies:
        copy.start()

    key_codes(meta, code)
    starts[...] = document_starts(seg[...])
    keyvals[0:REACH, :] = jnp.zeros((REACH, 2 * HEAD), BF)
    keyvals_t[:, 0:REACH] = jnp.zeros((2 * HEAD, REACH), BF)

    for k in range(1, TENSOR):
        tile_one(k, at.tensor_at(k)).wait_recv()
    for k in range(1, DP):
        tile_two(k, d).start()
    for k in range(1, DP):
        rows_dp(k, at.dp_at(k)).wait_recv()
        wq_dp(k, at.dp_at(k)).wait_recv()
    spread_r.start()
    for k in range(1, DP):
        tile_two(k, at.dp_at(k)).wait_recv()
    for j in range(DP):
        both = tile_all[j].astype(F32)
        wkv[j * ROWS : (j + 1) * ROWS, :] = both[:, 0:8].reshape(ROWS, ROWS).astype(BF)
        small[j * ROWS : (j + 1) * ROWS, :] = both[:, 8:16].reshape(ROWS, ROWS).astype(BF)
    columns = small[...].astype(F32).T
    gain_one = columns[32:33, :]
    gain_two = columns[33:34, :]

    @pl.loop(0, CHIPS)
    def _(i):
        @pl.when(i == 0)
        def _():
            spread_h.arrived(at.twin)

        @pl.when(i > 0)
        def _():
            spread_h.first(i)
            spread_h.second(i)

        block = at.chip_at(i)
        here = aligned(block, PAIR)
        hidden = hidden_all[here, :].astype(F32)
        inverse = lax.rsqrt(jnp.mean(hidden * hidden, axis=1, keepdims=True) + 1e-6)
        unit = (hidden * inverse * gain_one).astype(BF)
        normed[here, :] = unit
        cos, sin = cosine[here, :], sine[here, :]
        query = dot(unit, wq_all[...], NT)
        query = (query * cos + swapped(query) * sin).astype(BF)
        queries[here, :] = (query.astype(F32) * (1.0 / math.sqrt(HEAD))).astype(BF)
        keyval = dot(unit, wkv[...])
        keyval = keyval * cos + swapped(keyval) * sin
        later = pl.ds(pl.multiple_of(REACH + block * PAIR, ROWS), PAIR)
        keyvals[later, :] = keyval.astype(BF)
        keyvals_t[:, later] = keyval.T.astype(BF)

    for copy in expert(0, at.across, at.across, True):
        copy.wait_recv()
    for k in range(1, 4):
        for copy in expert(3 + k, at.across, y_peer(k), False):
            copy.start()
    for k in range(1, CHIPS):
        spread_r.first(k)
    for copy in own_copies:
        copy.wait()
    spread_c.start()

    def att_copy(dest, src):
        return remote(
            att_src.at[dest],
            att_t.at[aligned(src, HEAD), :],
            a_send.at[dest],
            a_recv.at[src],
            "tensor",
            dest,
        )

    @pl.loop(0, CHIPS)
    def _(i):
        block = at.chip_at(i + 1)
        here = aligned(block, PAIR)
        query = queries[here, :]
        start_row = starts[:, here]
        top = jnp.full((1, PAIR), LOWEST, F32)
        for chunk in range(SPAN // ROWS):
            keys = pl.ds(pl.multiple_of(block * PAIR + chunk * ROWS, ROWS), ROWS)
            score = dot(keyvals[keys, :], query, NT)
            score = jnp.where(allowed(code[keys, :], start_row, chunk), score, LOWEST)
            scores[chunk * ROWS : (chunk + 1) * ROWS, :] = score
            top = jnp.maximum(top, jnp.max(score, axis=0, keepdims=True))
        total = jnp.zeros((1, PAIR), F32)
        for chunk in range(SPAN // ROWS):
            place = slice(chunk * ROWS, (chunk + 1) * ROWS)
            weight = jnp.exp(scores[place, :] - top)
            total = total + jnp.sum(weight, axis=0, keepdims=True)
            probs[place, :] = weight.astype(BF)
        window = pl.ds(pl.multiple_of(block * PAIR, ROWS), SPAN)
        head = dot(keyvals_t[HEAD : 2 * HEAD, window], probs[...]) / total
        heads_t[:, here] = head
        stats[:, here] = top + jnp.log(total)
        att_src[2 * block] = head[:, 0:ROWS].astype(BF)
        att_src[2 * block + 1] = head[:, ROWS:PAIR].astype(BF)

        @pl.when(i < CHIPS - 1)
        def _():
            att_copy(2 * block, t).start()
            att_copy(2 * block + 1, t).start()

        @pl.when(i == CHIPS - 1)
        def _():
            att_copy(at.twin, t).start()

    att_t[aligned(t, HEAD), :] = att_src[t]
    spread_r.arrived(at.twin)
    for k in range(1, CHIPS):
        spread_r.second(k)

    @pl.loop(0, DP)
    def _(j):
        both = row_all[j].astype(F32)
        kv_full[aligned(j, ROWS), :] = both[:, 0:8].reshape(ROWS, WIDTH).astype(BF)
        out_t[aligned(j, ROWS), :] = both[:, 8:16].reshape(ROWS, WIDTH).astype(BF)

    for k in range(1, TENSOR):
        att_copy(at.tensor_at(k), at.tensor_at(k)).wait_recv()
    attended = att_t[...].astype(F32).T.astype(BF)
    middle = hid[...].astype(F32) + dot(attended, out_t[...], NT)
    mid[...] = middle
    inverse = lax.rsqrt(jnp.mean(middle * middle, axis=1, keepdims=True) + 1e-6)
    normed_mid[...] = (middle * inverse * gain_two).astype(BF)

    for k in range(1, CHIPS):
        spread_c.first(k)
    spread_c.arrived(at.twin)
    for k in range(1, CHIPS):
        spread_c.second(k)
    for k in range(1, 4):
        for other in (2 * at.y_at(k), 2 * at.y_at(k) + 1):
            for copy in expert(0, other, at.across, True):
                copy.wait_recv()
    for k in range(1, TENSOR):
        tile_one(k, t).wait_send()
        att_copy(at.tensor_at(k), t).wait_send()
    for k in range(1, DP):
        tile_two(k, d).wait_send()
        rows_dp(k, d).wait_send()
        wq_dp(k, d).wait_send()
    for k in range(7):
        for copy in expert(k, d, at.across, True):
            copy.wait_send()
    for spread in (spread_h, spread_r, spread_c):
        spread.end()


class Sum:
    def __init__(self, place, parts, twins, sums, landed, tw_send, tw_recv, send, recv):
        self.place, self.parts, self.twins = place, parts, twins
        self.sums, self.landed = sums, landed
        self.tw_send, self.tw_recv, self.send, self.recv = tw_send, tw_recv, send, recv

    def half(self, k):
        at = self.place
        return remote(
            self.parts.at[lax.rem(k, SLOTS), aligned(1 - at.core, ROWS), :],
            self.twins.at[k],
            self.tw_send.at[k],
            self.tw_recv.at[k],
            "tensor",
            at.twin,
        )

    def whole(self, k):
        return remote(
            self.sums.at[k],
            self.landed.at[k],
            self.send.at[k],
            self.recv.at[k],
            "tensor",
            self.place.same_core(k),
        )

    def put(self, k, value):
        @pl.when(k >= SLOTS)
        def _():
            self.half(k - SLOTS).wait_send()

        self.parts[lax.rem(k, SLOTS)] = value.astype(BF)
        self.half(k).start()

    def add(self, k):
        self.half(k).wait_recv()
        own = self.parts[lax.rem(k, SLOTS), aligned(self.place.core, ROWS), :].astype(F32)
        self.sums[k] = (own + self.twins[k].astype(F32)).astype(BF)

    def go(self, k):
        self.add(k)
        self.whole(k).start()

    def result(self):
        total = self.sums[0].astype(F32)
        for k in range(1, CHIPS):
            self.whole(k).wait_recv()
            total = total + self.landed[k].astype(F32)
        return total

    def end(self):
        for k in range(CHIPS - SLOTS, CHIPS):
            self.half(k).wait_send()
        for k in range(1, CHIPS):
            self.whole(k).wait_send()


def expert_kernel(
    normed_mid,
    cot_all,
    gu_all,
    down_all,
    small,
    meta,
    mid,
    cot,
    out_t,
    output,
    mid_grad,
    mid_low,
    att_grad_t,
    gu_grad,
    down_grad,
    router_t,
    gain_grad,
    nm_all,
    nm_t,
    cots,
    gus,
    downs,
    weighted_t,
    proj_grads,
    logit_t,
    n_parts,
    n_twins,
    n_sums,
    n_landed,
    m_parts,
    m_twins,
    m_sums,
    m_landed,
    g_send,
    g_recv,
    ntw_send,
    ntw_recv,
    ns_send,
    ns_recv,
    mtw_send,
    mtw_recv,
    ms_send,
    ms_recv,
    local,
):
    at = Place()
    t = at.t
    loads = (
        pltpu.make_async_copy(gu_all, gus, local.at[0]),
        pltpu.make_async_copy(down_all, downs, local.at[1]),
        pltpu.make_async_copy(cot_all, cots, local.at[2]),
    )
    for copy in loads:
        copy.start()
    nm_all[aligned(t, ROWS), :] = normed_mid[...]
    at.enter()
    spread = Spread(at, lambda b: nm_all.at[aligned(b, ROWS)], g_send, g_recv)
    spread.start()
    normed_sum = Sum(
        at, n_parts, n_twins, n_sums, n_landed, ntw_send, ntw_recv, ns_send, ns_recv
    )
    moe_sum = Sum(at, m_parts, m_twins, m_sums, m_landed, mtw_send, mtw_recv, ms_send, ms_recv)
    for copy in loads:
        copy.wait()

    @pl.loop(0, CHIPS)
    def _(i):
        @pl.when(i == 0)
        def _():
            spread.arrived(at.twin)

        @pl.when(i > 0)
        def _():
            spread.first(i)
            spread.second(i)

        here = aligned(at.chip_at(i), PAIR)
        nm = nm_all[here, :]
        nm_t[:, here] = nm.T
        cotangents = cots[here, :]
        place = lanes((PAIR, ROWS))
        routes = meta[here, :]
        named = place == routes[:, 0:1]
        for j in range(1, 8):
            named = named | (place == routes[:, j : j + 1])
        logits = jnp.where(named, dot(nm, small[...]), LOWEST)
        powers = jnp.exp(logits - jnp.max(logits, axis=1, keepdims=True))
        powers = jnp.where(named, powers, 0.0)
        gates = powers / jnp.sum(powers, axis=1, keepdims=True)
        gate_grads = jnp.zeros((PAIR, ROWS), F32)
        act_grads = dot(cotangents, downs[...], NT)
        weighted = []
        for e in range(2):
            mine = place == 2 * t + e
            gate = jnp.sum(jnp.where(mine, gates, 0.0), axis=1, keepdims=True)
            projected = dot(nm, gus[e])
            first, up = projected[:, :UNITS], projected[:, UNITS:]
            sigmoid = 1.0 / (1.0 + jnp.exp(-first))
            silu = first * sigmoid
            activated = silu * up
            act_grad = act_grads[:, e * UNITS : (e + 1) * UNITS]
            gate_grad = jnp.sum(activated * act_grad, axis=1, keepdims=True)
            gate_grads = gate_grads + jnp.where(mine, gate_grad, 0.0)
            weighted.append((activated * gate).astype(BF))
            act_grad = act_grad * gate
            proj_grads[here, e * WIDTH : e * WIDTH + UNITS] = (
                act_grad * up * (sigmoid * (1.0 + first * (1.0 - sigmoid)))
            ).astype(BF)
            proj_grads[here, e * WIDTH + UNITS : (e + 1) * WIDTH] = (act_grad * silu).astype(BF)
        mean = jnp.sum(gates * gate_grads, axis=1, keepdims=True)
        logit_grad = gates * (gate_grads - mean)
        logit_t[:, here] = logit_grad.T.astype(BF)
        normed_part = (
            dot(proj_grads[here, 0:WIDTH], gus[0], NT)
            + dot(proj_grads[here, WIDTH : 2 * WIDTH], gus[1], NT)
            + dot(logit_grad.astype(BF), small[...], NT)
        )
        normed_sum.put(i, normed_part)
        both = jnp.concatenate(weighted, axis=1)
        moe_sum.put(i, dot(both, downs[...]))
        weighted_t[:, here] = both.T

        @pl.when(i == 1)
        def _():
            normed_sum.add(0)
            moe_sum.add(0)

        @pl.when(i > 1)
        def _():
            normed_sum.go(i - 1)
            moe_sum.go(i - 1)

    normed_sum.go(CHIPS - 1)
    moe_sum.go(CHIPS - 1)

    @pl.loop(0, 4)
    def _(j):
        strip = aligned(j, PAIR)
        for e in range(2):
            gus[e, strip, :] = dot(
                nm_t[strip, :], proj_grads[:, e * WIDTH : (e + 1) * WIDTH]
            ).astype(BF)
        downs[strip, :] = dot(weighted_t[strip, :], cots[...]).astype(BF)

    stores = (
        pltpu.make_async_copy(gus, gu_grad, local.at[0]),
        pltpu.make_async_copy(downs, down_grad, local.at[1]),
    )
    for copy in stores:
        copy.start()
    router_t[...] = dot(logit_t[...], nm_all[...])

    columns = small[...].astype(F32).T
    gain_two = columns[33:34, :]
    normed_grad = normed_sum.result()
    middle = mid[...]
    inverse = lax.rsqrt(jnp.mean(middle * middle, axis=1, keepdims=True) + 1e-6)
    unit = middle * inverse
    gain_grad[...] = jnp.sum(normed_grad * unit, axis=0, keepdims=True)
    scaled = normed_grad * gain_two
    grad = cot[...].astype(F32) + inverse * (
        scaled - unit * jnp.mean(scaled * unit, axis=1, keepdims=True)
    )
    mid_grad[...] = grad
    low = grad.astype(BF)
    mid_low[...] = low
    att_grad_t[...] = dot(low, out_t[...]).T.astype(BF)
    output[...] = (middle + moe_sum.result()).astype(BF)
    for copy in stores:
        copy.wait()
    spread.end()
    normed_sum.end()
    moe_sum.end()


def back_kernel(
    att_grad_t,
    mid_low,
    mid_grad,
    gu_grad,
    down_grad,
    router_t,
    gain_grad,
    queries,
    keyvals,
    keyvals_t,
    stats,
    heads_t,
    meta,
    seg,
    cosine,
    sine,
    cosine_t,
    sine_t,
    wq_own,
    kv_full,
    normed,
    hid,
    small,
    hidden_grad,
    gu_out,
    down_out,
    query_out,
    kv_out,
    rest_out,
    grads_t,
    mid_all,
    wq_full,
    code,
    starts,
    kv_sum,
    tail_left,
    qg_src,
    kg_src,
    qg_all,
    kg_all,
    tail,
    tail_in,
    pieces,
    last,
    own_gu,
    own_down,
    gu_in,
    down_in,
    gu_half,
    down_half,
    gu_half_in,
    down_half_in,
    g_send,
    g_recv,
    m_send,
    m_recv,
    w_send,
    w_recv,
    q_send,
    q_recv,
    k_send,
    k_recv,
    gu_send,
    gu_recv,
    dn_send,
    dn_recv,
    t_send,
    t_recv,
    l_send,
    l_recv,
    local,
):
    at = Place()
    t, d = at.t, at.d
    grads_t[0:HEAD, :] = jnp.zeros((HEAD, LENGTH), BF)
    grads_t[HEAD : 2 * HEAD, aligned(t, ROWS)] = att_grad_t[aligned(t, HEAD), :]
    mid_all[aligned(t, ROWS), :] = mid_low[...]
    wq_full[aligned(t, HEAD), :] = wq_own[0:HEAD, :]
    at.enter()

    def back_copy(k, src):
        dest = at.tensor_at(k)
        return remote(
            att_grad_t.at[aligned(dest, HEAD), :],
            grads_t.at[pl.ds(HEAD, HEAD), aligned(src, ROWS)],
            g_send.at[k],
            g_recv.at[src],
            "tensor",
            dest,
        )

    def experts_y(k):
        y = at.y_at(k)
        dest = 2 * y + at.x
        return (
            remote(
                gu_grad.at[:, aligned(y, PAIR), :],
                gu_in.at[k],
                gu_send.at[k],
                gu_recv.at[k],
                "dp",
                dest,
            ),
            remote(
                down_grad.at[:, aligned(y, PAIR)],
                down_in.at[k],
                dn_send.at[k],
                dn_recv.at[k],
                "dp",
                dest,
            ),
        )

    def experts_x():
        return (
            remote(gu_half, gu_half_in, gu_send.at[0], gu_recv.at[0], "dp", at.across),
            remote(down_half, down_half_in, dn_send.at[0], dn_recv.at[0], "dp", at.across),
        )

    spread_m = Spread(at, lambda b: mid_all.at[aligned(b, ROWS)], m_send, m_recv)
    spread_w = Spread(at, lambda b: wq_full.at[aligned(b, HEAD)], w_send, w_recv)
    for k in range(1, TENSOR):
        back_copy(k, t).start()
    spread_w.start()
    for k in range(1, 4):
        for copy in experts_y(k):
            copy.start()
    own_copies = (
        pltpu.make_async_copy(gu_grad.at[:, aligned(at.y, PAIR), :], own_gu, local.at[0]),
        pltpu.make_async_copy(down_grad.at[:, aligned(at.y, PAIR)], own_down, local.at[1]),
    )
    for copy in own_copies:
        copy.start()
    spread_m.start()

    key_codes(meta, code)
    starts[...] = document_starts(seg[...])
    kv_sum[...] = jnp.zeros((PADDED, 2 * HEAD), F32)
    for k in range(1, TENSOR):
        back_copy(k, at.tensor_at(k)).wait_recv()

    def query_copy(dest, src):
        return remote(
            qg_src.at[dest],
            qg_all.at[aligned(src, HEAD), :],
            q_send.at[dest],
            q_recv.at[src],
            "tensor",
            dest,
        )

    def key_copy(dest, src):
        return remote(
            kg_src.at[dest], kg_all.at[src], k_send.at[dest], k_recv.at[src], "tensor", dest
        )

    @pl.loop(0, CHIPS)
    def _(i):
        here = aligned(i, PAIR)
        query = queries[here, :]
        start_row = starts[:, here]
        stat = stats[:, here]
        grad_t = grads_t[:, here]
        grad_rows = grad_t.astype(F32).T.astype(BF)
        head = heads_t[:, here]
        delta = jnp.sum(head * grad_t[HEAD : 2 * HEAD, :].astype(F32), axis=0, keepdims=True)
        query_grad = jnp.zeros((HEAD, PAIR), F32)
        for chunk in range(SPAN // ROWS):
            keys = pl.ds(pl.multiple_of(i * PAIR + chunk * ROWS, ROWS), ROWS)
            both = keyvals[keys, :]
            score = dot(both, query, NT)
            ok = allowed(code[keys, :], start_row, chunk)
            prob = jnp.exp(jnp.where(ok, score - stat, LOWEST))
            prob_grad = dot(both, grad_t)
            score_grad = (prob * (prob_grad - delta)).astype(BF)
            kv_sum[keys, :] += dot(score_grad, query) + dot(prob.astype(BF), grad_rows)
            query_grad = query_grad + dot(keyvals_t[0:HEAD, keys], score_grad)
        query_grad = query_grad * (1.0 / math.sqrt(HEAD))
        cos, sin = cosine_t[:, here], sine_t[:, here]
        upper, lower = query_grad[0 : HEAD // 2], query_grad[HEAD // 2 : HEAD]
        turned = jnp.concatenate(
            [upper * cos + lower * sin, lower * cos - upper * sin], axis=0
        ).astype(BF)
        tail_left[0:HEAD, here] = turned
        qg_src[2 * i] = turned[:, 0:ROWS]
        qg_src[2 * i + 1] = turned[:, ROWS:PAIR]

    @pl.loop(0, CHIPS)
    def _(i):
        here = aligned(i, PAIR)
        grad = kv_sum[pl.ds(pl.multiple_of(REACH + i * PAIR, ROWS), PAIR), :]
        grad = grad * cosine[here, :] - swapped(grad) * sine[here, :]
        tail_left[HEAD : 3 * HEAD, here] = grad.T.astype(BF)
        kg_src[2 * i] = grad[0:ROWS].astype(BF)
        kg_src[2 * i + 1] = grad[ROWS:PAIR].astype(BF)

    for k in range(1, TENSOR):
        key_copy(at.tensor_at(k), t).start()
        query_copy(at.tensor_at(k), t).start()
    qg_all[aligned(t, HEAD), :] = qg_src[t]
    kg_all[t] = kg_src[t]
    for k in range(1, CHIPS):
        spread_w.first(k)
    for k in range(1, CHIPS):
        spread_m.first(k)

    by_normed = dot(tail_left[...], normed[...])
    tail[0:HEAD, :] = by_normed[0:HEAD]
    tail[2 * HEAD : 4 * HEAD, :] = by_normed[HEAD : 3 * HEAD]

    spread_w.arrived(at.twin)
    for k in range(1, CHIPS):
        spread_w.second(k)
    for k in range(1, TENSOR):
        query_copy(at.tensor_at(k), at.tensor_at(k)).wait_recv()
        key_copy(at.tensor_at(k), at.tensor_at(k)).wait_recv()
    kv_rows = jnp.concatenate(
        [kg_all[2 * j].astype(F32) + kg_all[2 * j + 1].astype(F32) for j in range(CHIPS)], axis=1
    ).astype(BF)
    normed_grad = dot(qg_all[...].astype(F32).T.astype(BF), wq_full[...]) + dot(
        kv_rows, kv_full[...], NT
    )
    hidden = hid[...].astype(F32)
    inverse = lax.rsqrt(jnp.mean(hidden * hidden, axis=1, keepdims=True) + 1e-6)
    unit = hidden * inverse
    gain_one = small[...].astype(F32).T[32:33, :]
    gain_one_grad = jnp.sum(normed_grad * unit, axis=0, keepdims=True)
    scaled = normed_grad * gain_one
    hidden_grad[...] = (
        mid_grad[...]
        + inverse * (scaled - unit * jnp.mean(scaled * unit, axis=1, keepdims=True))
    ).astype(BF)

    spread_m.arrived(at.twin)
    for k in range(1, CHIPS):
        spread_m.second(k)
    tail[HEAD : 2 * HEAD, :] = dot(heads_t[...].astype(BF), mid_all[...])
    tail[4 * HEAD : 4 * HEAD + 32, :] = router_t[0:32, :]
    row = sublanes((16, WIDTH))
    tail[4 * HEAD + 32 : TAIL, :] = jnp.where(
        row == 0, gain_one_grad, jnp.where(row == 1, gain_grad[...], 0.0)
    )

    def tail_copy(k):
        dest = at.dp_at(k)
        return remote(
            tail.at[:, aligned(dest, ROWS)],
            tail_in.at[k],
            t_send.at[k],
            t_recv.at[k],
            "dp",
            dest,
        )

    for k in range(1, DP):
        tail_copy(k).start()

    for copy in own_copies:
        copy.wait()
    for k in range(1, 4):
        for copy in experts_y(k):
            copy.wait_recv()

    def gu_total(which):
        here = aligned(which, ROWS)
        total = own_gu[:, here, :].astype(F32)
        for k in range(1, 4):
            total = total + gu_in[k, :, here, :].astype(F32)
        return total

    def down_total(which):
        here = aligned(which, ROWS)
        total = own_down[:, here].astype(F32)
        for k in range(1, 4):
            total = total + down_in[k, :, here].astype(F32)
        return total

    gu_half[...] = gu_total(1 - at.x).astype(BF)
    down_half[...] = down_total(1 - at.x).astype(BF)
    for copy in experts_x():
        copy.start()

    total = tail[:, aligned(d, ROWS)]
    for k in range(1, DP):
        tail_copy(k).wait_recv()
        total = total + tail_in[k]
    query_out[...] = total[0:HEAD, :]
    turned = jnp.concatenate([total, jnp.zeros((384 - TAIL, ROWS), F32)], axis=0).T
    for j in range(TENSOR):
        pieces[j] = turned[j * 8 : (j + 1) * 8, :]

    def last_copy(k, src):
        dest = at.tensor_at(k)
        return remote(
            pieces.at[dest], last.at[src], l_send.at[k], l_recv.at[src], "tensor", dest
        )

    for k in range(1, TENSOR):
        last_copy(k, t).start()
    last[t] = pieces[t]

    gu_out[...] = gu_total(at.x)
    down_out[...] = down_total(at.x)
    for copy in experts_x():
        copy.wait_recv()
    gu_out[...] += gu_half_in[...].astype(F32)
    down_out[...] += down_half_in[...].astype(F32)

    for k in range(1, TENSOR):
        last_copy(k, at.tensor_at(k)).wait_recv()
    kv_out[...] = jnp.concatenate(
        [last[2 * j, :, 128:256] + last[2 * j + 1, :, 128:256] for j in range(CHIPS)], axis=1
    )
    shared = last[0, :, 256:384]
    for j in range(1, TENSOR):
        shared = shared + last[j, :, 256:384]
    rest_out[0] = shared
    for j in range(TENSOR):
        rest_out[j + 1] = last[j, :, 0:128]

    for k in range(1, TENSOR):
        back_copy(k, t).wait_send()
        query_copy(at.tensor_at(k), t).wait_send()
        key_copy(at.tensor_at(k), t).wait_send()
        last_copy(k, t).wait_send()
    for k in range(1, 4):
        for copy in experts_y(k):
            copy.wait_send()
    for copy in experts_x():
        copy.wait_send()
    for k in range(1, DP):
        tail_copy(k).wait_send()
    spread_m.end()
    spread_w.end()


def call(kernel, number, kinds, outs, scratch, args):
    spaces = {"v": pl.BlockSpec(memory_space=pltpu.VMEM), "h": pl.BlockSpec(memory_space=pl.ANY)}
    specs = [spaces[kind] for kind in kinds]
    return pl.pallas_call(
        kernel,
        out_shape=[jax.ShapeDtypeStruct(shape, dtype) for shape, dtype in outs],
        in_specs=specs[: len(args)],
        out_specs=specs[len(args) :],
        scratch_shapes=scratch,
        compiler_params=pltpu.CompilerParams(
            collective_id=number, has_side_effects=True, vmem_limit_bytes=VMEM_BYTES
        ),
    )(*args)


def sems(*counts):
    return [pltpu.SemaphoreType.DMA((count,)) for count in counts]


def rope_tables():
    half = HEAD // 2
    freqs = np.exp(
        np.arange(half, dtype=np.float32) * np.float32(-2.0 * math.log(10000.0) / HEAD)
    ).astype(np.float32)
    angles = np.arange(LENGTH, dtype=np.float32)[:, None] * freqs[None, :]
    cos, sin = np.cos(angles).astype(np.float32), np.sin(angles).astype(np.float32)
    ones, zeros = np.ones((LENGTH, HEAD), np.float32), np.zeros((LENGTH, HEAD), np.float32)
    return (
        np.concatenate([cos, cos, ones], axis=1),
        np.concatenate([-sin, sin, zeros], axis=1),
        np.ascontiguousarray(cos.T),
        np.ascontiguousarray(sin.T),
    )


def body(
    hidden,
    seg_ids,
    key_mask,
    routes,
    gain_attn,
    w_query,
    w_keyval,
    w_out,
    gain_mlp,
    w_router,
    w_gate_up,
    w_down,
    cotangent,
):
    V = pltpu.VMEM
    cosine, sine, cosine_t, sine_t = rope_tables()
    hid, cot = hidden[0], cotangent[0]
    meta = jnp.concatenate(
        [routes[0], key_mask[0][:, None], jnp.zeros((LENGTH, 7), jnp.int32)], axis=1
    )
    shares = jnp.concatenate(
        [w_router, gain_attn[:, None], gain_mlp[:, None], jnp.zeros((8, 94), BF)], axis=1
    )
    columns = jnp.repeat(w_keyval.reshape(8, CHIPS, ROWS).transpose(1, 0, 2), 2, axis=0)
    tiles = jnp.concatenate(
        [columns, jnp.broadcast_to(shares[None], (TENSOR, 8, ROWS))], axis=1
    )
    rows = jnp.concatenate([w_keyval, w_out.T], axis=0)
    (
        normed,
        queries,
        keyvals,
        keyvals_t,
        stats,
        heads_t,
        mid,
        normed_mid,
        wq_own,
        out_t,
        kv_full,
        small,
        gu_all,
        down_all,
        cot_all,
    ) = call(
        attention_kernel,
        1,
        "vhvvvhhvvvv" + "vvvvvvvvvvvvhhh",
        [
            ((LENGTH, WIDTH), BF),
            ((LENGTH, 2 * HEAD), BF),
            ((PADDED, 2 * HEAD), BF),
            ((2 * HEAD, PADDED), BF),
            ((1, LENGTH), F32),
            ((HEAD, LENGTH), F32),
            ((ROWS, WIDTH), F32),
            ((ROWS, WIDTH), BF),
            ((2 * HEAD, WIDTH), BF),
            ((WIDTH, WIDTH), BF),
            ((WIDTH, WIDTH), BF),
            ((WIDTH, ROWS), BF),
            ((2, WIDTH, WIDTH), BF),
            ((2, UNITS, WIDTH), BF),
            ((LENGTH, WIDTH), BF),
        ],
        [
            V((LENGTH, WIDTH), BF),
            V((DP, TENSOR, 16, ROWS), BF),
            V((DP, TENSOR, 16, WIDTH), BF),
            V((PADDED, ROWS), F32),
            V((SPAN, PAIR), F32),
            V((SPAN, PAIR), BF),
            V((1, LENGTH), F32),
            V((WIDTH, ROWS), BF),
            V((TENSOR, HEAD, ROWS), BF),
            V((WIDTH, ROWS), BF),
        ]
        + sems(16, 16, 16, 16, 16, 16, 16, 16, 8, 8, 8, 8, 8, 8, 8, 8, 8, 8, 16, 16, 3),
        (
            hid,
            cot,
            tiles,
            w_query.T,
            rows,
            w_gate_up,
            w_down,
            cosine,
            sine,
            meta,
            seg_ids,
        ),
    )
    parts = [
        V((SLOTS, PAIR, WIDTH), BF),
        V((CHIPS, ROWS, WIDTH), BF),
        V((CHIPS, ROWS, WIDTH), BF),
        V((CHIPS, ROWS, WIDTH), BF),
    ]
    output, mid_grad, mid_low, att_grad_t, gu_grad, down_grad, router_t, gain_grad = call(
        expert_kernel,
        2,
        "vhhhvvvvv" + "vvvvhhvv",
        [
            ((ROWS, WIDTH), BF),
            ((ROWS, WIDTH), F32),
            ((ROWS, WIDTH), BF),
            ((WIDTH, ROWS), BF),
            ((2, WIDTH, WIDTH), BF),
            ((WIDTH, WIDTH), BF),
            ((ROWS, WIDTH), F32),
            ((1, WIDTH), F32),
        ],
        [
            V((LENGTH, WIDTH), BF),
            V((WIDTH, LENGTH), BF),
            V((LENGTH, WIDTH), BF),
            V((2, WIDTH, WIDTH), BF),
            V((WIDTH, WIDTH), BF),
            V((WIDTH, LENGTH), BF),
            V((LENGTH, 2 * WIDTH), BF),
            V((ROWS, LENGTH), BF),
        ]
        + parts
        + parts
        + sems(16, 16, 8, 8, 8, 8, 8, 8, 8, 8, 3),
        (
            normed_mid,
            cot_all,
            gu_all,
            down_all.reshape(WIDTH, WIDTH),
            small,
            meta,
            mid,
            cot,
            out_t,
        ),
    )
    hidden_grad, gu_out, down_out, query_out, kv_out, rest = call(
        back_kernel,
        3,
        "vvvhhvvvvvvvvvvvvvvvvvv" + "vvvvvv",
        [
            ((ROWS, WIDTH), BF),
            ((2, ROWS, WIDTH), F32),
            ((WIDTH, ROWS), F32),
            ((HEAD, ROWS), F32),
            ((8, WIDTH), F32),
            ((TENSOR + 1, 8, ROWS), F32),
        ],
        [
            V((2 * HEAD, LENGTH), BF),
            V((LENGTH, WIDTH), BF),
            V((WIDTH, WIDTH), BF),
            V((PADDED, ROWS), F32),
            V((1, LENGTH), F32),
            V((PADDED, 2 * HEAD), F32),
            V((3 * HEAD, LENGTH), BF),
            V((TENSOR, HEAD, ROWS), BF),
            V((TENSOR, ROWS, ROWS), BF),
            V((WIDTH, ROWS), BF),
            V((TENSOR, ROWS, ROWS), BF),
            V((TAIL, WIDTH), F32),
            V((DP, TAIL, ROWS), F32),
            V((TENSOR, 8, 384), F32),
            V((TENSOR, 8, 384), F32),
            V((2, PAIR, WIDTH), BF),
            V((WIDTH, PAIR), BF),
            V((4, 2, PAIR, WIDTH), BF),
            V((4, WIDTH, PAIR), BF),
            V((2, ROWS, WIDTH), BF),
            V((WIDTH, ROWS), BF),
            V((2, ROWS, WIDTH), BF),
            V((WIDTH, ROWS), BF),
        ]
        + sems(16, 16, 16, 16, 16, 16, 16, 16, 16, 16, 8, 8, 8, 8, 8, 8, 16, 16, 2),
        (
            att_grad_t,
            mid_low,
            mid_grad,
            gu_grad,
            down_grad,
            router_t,
            gain_grad,
            queries,
            keyvals,
            keyvals_t,
            stats,
            heads_t,
            meta,
            seg_ids,
            cosine,
            sine,
            cosine_t,
            sine_t,
            wq_own,
            kv_full,
            normed,
            hid,
            small,
        ),
    )
    shared = rest[0]
    out_grad = rest[1:, :, HEAD : 2 * HEAD].transpose(0, 2, 1).reshape(WIDTH, 8)
    return (
        output[None],
        hidden_grad[None],
        shared[:, 32],
        query_out.T,
        kv_out,
        out_grad,
        shared[:, 33],
        shared[:, 0:32],
        gu_out,
        down_out.reshape(2, UNITS, ROWS),
    )


def solution(mesh):
    return jax.shard_map(
        body,
        mesh=mesh,
        in_specs=(
            P("dp", "tensor", None),
            P("dp", None),
            P("dp", None),
            P("dp", None, None),
            P(("dp", "tensor")),
            P("dp", "tensor"),
            P(("dp", "tensor"), None),
            P(None, ("dp", "tensor")),
            P(("dp", "tensor")),
            P(("dp", "tensor"), None),
            P("tensor", "dp", None),
            P("tensor", None, "dp"),
            P("dp", "tensor", None),
        ),
        out_specs=(
            P("dp", "tensor", None),
            P("dp", "tensor", None),
            P(("dp", "tensor")),
            P("dp", "tensor"),
            P(("dp", "tensor"), None),
            P(None, ("dp", "tensor")),
            P(("dp", "tensor")),
            P(("dp", "tensor"), None),
            P("tensor", "dp", None),
            P("tensor", None, "dp"),
        ),
        check_vma=False,
    )
```

time: 1980 us -> 370 us (0.19); the launches traced: 1960 us -> 369 us
  waiting for transfers between devices: 1240 us -> 0 us
  local copies, waits for them, and re-layouts: 472 us -> 16 us
  Pallas kernels: 0 us -> 349 us
  matrix products: 133 us -> 0 us
  other arithmetic: 69.6 us -> 3.68 us
    unnamed x11 -> x0, waiting for transfers between devices: 645 us -> none
    all_gather x5 -> x0, waiting for transfers between devices: 376 us -> none  [the longest x2 328 us: gather_turned(): lax.all_gather(both, axis, axis=0, tiled=True)]
    pallas_call x0 -> x3, Pallas kernels: none -> 349 us  [call(): pl.pallas_call(kernel, out_shape=[jax.ShapeDtypeStruct(shape, dtype) for...]
    gather x20 -> x0, local copies, waits for them, and re-layouts: 267 us -> none  [the longest x4 132 us: body(): chosen = jnp.take_along_axis(logits, route_ids, axis=1)]
    reduce_scatter x4 -> x0, waiting for transfers between devices: 216 us -> none  [the longest x1 101 us: sum_packed(): lax.psum_scatter(lines, axis, tiled=True).reshape(-1)]
    dot_general x56 -> x0, matrix products: 133 us -> none  [the longest x22 68.4 us: times_transposed(): lax.dot_general(left, right, (((1,), (1,)), ((), ())), preferred_element_...]
    dynamic_update_slice x25 -> x0, local copies, waits for them, and re-layouts: 53.9 us -> none  [the longest x8 15.1 us: head_backward(): lax.scan(one_block, (empty, empty), jnp.arange(length // rows, dtype=jnp....]
    reshape x10 -> x1, local copies, waits for them, and re-layouts: 33.4 us -> 0.7 us  [body(): out_grad = rest[1:, :, HEAD:2 * HEAD].transpose(0, 2, 1).reshape(WIDTH, 8)]
  transfers between devices with their start and end apart: 11 -> 0, of which waited for: 8 -> 0; matrix products, arithmetic and copies ran while one was open for 14% -> 0% of each run, Pallas kernels for 0% -> 0%
where the time goes in v1:
time: 370 us; the launch traced here: 369 us
  Pallas kernels  349 us (94%)
  local copies, waits for them, and re-layouts  16 us (4%)
    pallas_call x3, Pallas kernels, call(): pl.pallas_call(kernel, out_shape=[jax.ShapeDtypeStruct(shape, dtype) for...  349 us
    unnamed x10, local copies, waits for them, and re-layouts  9.3 us

profile of v1, /device:TPU:1, one launch (start us, length us, event | category | flops | bytes accessed | tf_op | source)
XLA Modules:
  0.0 369.4 jit_solution(6644716130274742413)
XLA Ops:
  0.7 0.1 pad.10.clone
  0.7 0.1 pad.2.clone
  0.8 0.7 copy.35
  1.6 0.7 copy.36
  2.3 0.8 maximum_maximum_fusion
  3.1 1.4 pad_maximum_fusion.1.rows
  4.4 0.7 broadcast_in_dim.27
  5.1 0.6 pad_maximum_fusion.tiles
  5.8 0.9 add_add_fusion
  6.7 1.3 copy.37.meta
  8.0 126.8 %shard_map.240 = (bf16[2048,1024]{1,0:T(8,128)(2,1)}, bf16[2048,128]{1,0:T(8,128)(2,1)}, bf16[2944,128]{1,0:T(8,128)(2,1)}, bf16[128,2944]{1,0:T(8,128)(2,1)}, f...) custom-call(bf16[128,1024]{1,0:T(8,128)(2,1)} %bitcast.27, ...), custom_call_target="tpu_custom_call" | custom-call | tf_op jit(solution)/shard_map/pallas_call | solution.py:1047
  134.8 105.7 %shard_map.241 = (bf16[128,1024]{1,0:T(8,128)(2,1)}, f32[128,1024]{1,0:T(8,128)}, bf16[128,1024]{1,0:T(8,128)(2,1)}, bf16[1024,128]{1,0:T(8,128)(2,1)}, bf16[2,1...) custom-call(bf16[128,1024]{1,0:T(8,128)(2,1)} %get-tuple-element.39.normed_mid, ...), custom_call_target="tpu_custom_call" | custom-call | tf_op jit(solution)/shard_map/pallas_call | solution.py:1047
  240.5 0.0 copy-start
  240.5 116.5 %shard_map.242 = (bf16[128,1024]{1,0:T(8,128)(2,1)}, f32[2,128,1024]{2,1,0:T(8,128)}, f32[1024,128]{1,0:T(8,128)}, f32[64,128]{1,0:T(8,128)}, f32[8,1024]{1,0:T(8,128)}, /*index=5*/f32[17,8,128]{2,1,0:T(8,128)}) custom-call(bf16[1024,128]{1,0:T(8,128)(2,1)} %get-tuple-element.47.att_grad_t, bf16[128,1024]{1,0:T(8,128)(2,1)} %get-tuple-element.48.mid_low, ...), custom_call_target="tpu_custom_call" | custom-call | tf_op jit(solution)/shard_map/pallas_call | solution.py:1047
  357.0 0.7 slice_bitcast_fusion.1
  357.7 0.0 copy-start.1
  357.7 0.9 slice_bitcast_fusion
  358.6 0.7 reshape.39
  359.3 0.7 slice_reduce_fusion
  360.1 0.0 copy-done
  360.1 0.7 copy.47
  360.8 1.7 copy.48
  362.4 1.4 copy.49
  363.8 1.4 copy.50
  365.2 2.3 copy.51
  367.5 1.9 copy.52
  369.4 0.0 copy-done.1
  (4 shorter events, 0.0 us)
Async XLA Ops:
  240.5 119.5 %copy-start = (bf16[128,1024]{1,0:T(8,128)(2,1)S(1)}, bf16[128,1024]{1,0:T(8,128)(2,1)}, u32[]{:S(2)}) copy-start(bf16[128,1024]{1,0:T(8,128)(2,1)} %get-tuple-element.46) | copy-start | bytes 786436
  357.7 11.7 %copy-start.1 = (f32[8,128]{1,0:T(8,128)}, f32[8,128]{1,0:T(8,128)S(1)}, u32[]{:S(2)}) copy-start(f32[8,128]{1,0:T(8,128)S(1)} %slice_bitcast_fusion.1) | copy-start | bytes 12292

commit v2 on v0

v2 whole, which is shorter than its diff:
```python
import math

import jax
import jax.numpy as jnp
import numpy as np
from jax import lax
from jax.experimental import pallas as pl
from jax.experimental.pallas import tpu as pltpu
from jax.sharding import PartitionSpec as P

HEAD = 64
LENGTH = 2048
WIDTH = 1024
UNITS = 512
ROWS = 128
PAIR = 256
REACH = 896
SPAN = REACH + PAIR
PADDED = REACH + LENGTH
CHIPS = 8
TENSOR = 16
DP = 8
TAIL = 240
SLOTS = 2
STEP_Z = (0, 0, 1, 3, 1, 3, 2, 2)
STEP_X = (0, 1, 0, 0, 1, 1, 0, 1)
SUM_Z = (1, 1, 2, 2, 3, 3, 0, 0)
SUM_X = (1, 0, 1, 0, 1, 0, 1, 0)
LOWEST = -1e30
BF = jnp.bfloat16
F32 = jnp.float32
MESH = pl.DeviceIdType.MESH
VMEM_BYTES = 62 * 1024 * 1024

NN = (((1,), (0,)), ((), ()))
NT = (((1,), (1,)), ((), ()))


def dot(left, right, dims=NN):
    return lax.dot_general(left, right, dims, preferred_element_type=F32)


def aligned(value, size):
    return pl.ds(pl.multiple_of(value * size, size), size)


def remote(src, dst, send, recv, axis, index):
    return pltpu.make_async_remote_copy(
        src_ref=src,
        dst_ref=dst,
        send_sem=send,
        recv_sem=recv,
        device_id={axis: index},
        device_id_type=MESH,
    )


class Place:
    def __init__(self):
        self.t = lax.axis_index("tensor")
        self.d = lax.axis_index("dp")
        self.core = lax.rem(self.t, 2)
        self.chip = self.t // 2
        self.twin = self.t + 1 - 2 * self.core
        self.x = lax.rem(self.d, 2)
        self.y = self.d // 2
        self.across = self.d + 1 - 2 * self.x
        self.z = self.chip // 2
        self.x_far = lax.rem(self.chip, 2)

    def chip_at(self, k):
        return lax.rem(self.chip + k, CHIPS)

    def same_core(self, k):
        return 2 * self.chip_at(k) + self.core

    def near(self, dz, dx):
        return 2 * lax.rem(self.z + dz, 4) + lax.rem(self.x_far + dx, 2)

    def near_core(self, dz, dx):
        return 2 * self.near(dz, dx) + self.core

    def listed(self, i, all_z, all_x):
        if isinstance(i, int):
            return self.near(all_z[i], all_x[i])
        dz, dx = jnp.int32(0), jnp.int32(0)
        for k in range(CHIPS):
            dz = jnp.where(i == k, all_z[k], dz)
            dx = jnp.where(i == k, all_x[k], dx)
        return self.near(dz, dx)

    def step(self, i):
        return self.listed(i, STEP_Z, STEP_X)

    def sum_step(self, i):
        return self.listed(i, SUM_Z, SUM_X)

    def step_core(self, i):
        return 2 * self.step(i) + self.core

    def tensor_at(self, k):
        return lax.rem(self.t + k, TENSOR)

    def dp_at(self, k):
        return lax.rem(self.d + k, DP)

    def y_at(self, k):
        return lax.rem(self.y + k, 4)

    def enter(self):
        barrier = pltpu.get_barrier_semaphore()
        for k in range(1, TENSOR):
            pl.semaphore_signal(
                barrier, inc=1, device_id={"tensor": self.tensor_at(k)}, device_id_type=MESH
            )
        for k in range(1, DP):
            pl.semaphore_signal(
                barrier, inc=1, device_id={"dp": self.dp_at(k)}, device_id_type=MESH
            )
        pl.semaphore_wait(barrier, TENSOR + DP - 2)


class Spread:
    def __init__(self, place, block, send, recv, source=None):
        self.place, self.block, self.send, self.recv = place, block, send, recv
        self.source = source

    def copy(self, number, index, dest, source=None):
        src = self.block(index) if source is None else source
        return remote(
            src, self.block(index), self.send.at[number], self.recv.at[index], "tensor", dest
        )

    def own(self, k):
        dest = self.place.twin if k == 0 else self.place.same_core(k)
        return self.copy(k, self.place.t, dest, self.source)

    def start(self):
        for k in range(1, CHIPS):
            self.own(k).start()
        self.own(0).start()

    def passed(self, k):
        return self.copy(CHIPS + k, self.place.same_core(k), self.place.twin)

    def arrived(self, index):
        self.copy(0, index, self.place.twin).wait_recv()

    def first(self, k):
        self.arrived(self.place.same_core(k))
        self.passed(k).start()

    def second(self, k):
        self.arrived(2 * self.place.chip_at(k) + 1 - self.place.core)

    def end(self):
        for k in range(CHIPS):
            self.own(k).wait_send()
        for k in range(1, CHIPS):
            self.passed(k).wait_send()


class Ring:
    SENDS = 17

    def __init__(self, place, block, half, send, recv, source=None):
        self.place, self.block, self.half = place, block, half
        self.send, self.recv, self.source = send, recv, source

    def copy(self, number, index, dest, source=None):
        src = self.block(index) if source is None else source
        return remote(
            src, self.block(index), self.send.at[number], self.recv.at[index], "tensor", dest
        )

    def piece(self, number, index, part, dest):
        ref = self.half(index, part)
        return remote(
            ref, ref, self.send.at[number], self.recv.at[TENSOR * part + index], "tensor", dest
        )

    def sent(self, number):
        at = self.place
        if number == 0:
            return self.copy(0, at.t, at.twin, self.source)
        if number < 4:
            return self.copy(number, at.t, at.step_core(number), self.source)
        if number < 6:
            return self.copy(number, at.step_core(1), at.step_core(number - 2))
        if number < 8:
            return self.piece(number, at.step_core(2 * number - 9), 0, at.step_core(2))
        if number < 10:
            return self.piece(number, at.step_core(2 * number - 14), 1, at.step_core(3))
        return self.copy(number, at.step_core(number - 9), at.twin)

    def start(self):
        for number in (1, 2, 3, 0):
            self.sent(number).start()

    def pass_on(self, i):
        index = self.place.step_core(i)
        if i < 6:
            self.copy(0, index, self.place.twin).wait_recv()
        else:
            self.piece(0, index, 0, self.place.twin).wait_recv()
            self.piece(0, index, 1, self.place.twin).wait_recv()
        for number in {1: (4, 5), 2: (8,), 3: (6,), 4: (9,), 5: (7,)}.get(i, ()):
            self.sent(number).start()
        self.sent(9 + i).start()

    def pass_on_at(self, i):
        for k in range(1, CHIPS):

            @pl.when(i == k - 1)
            def _(k=k):
                self.pass_on(k)

    def second(self, i):
        self.copy(0, 2 * self.place.step(i) + 1 - self.place.core, self.place.twin).wait_recv()

    def end(self):
        for number in range(self.SENDS):
            self.sent(number).wait_send()


def whole_ring(place, ref, send, recv, source=None):
    return Ring(
        place,
        lambda b: ref.at[aligned(b, ROWS)],
        lambda b, part: ref.at[pl.ds(pl.multiple_of(b * ROWS + part * HEAD, HEAD), HEAD)],
        send,
        recv,
        source,
    )


class Copies:
    def __init__(self, sems):
        self.sems, self.all, self.done = sems, [], 0

    def start(self, src, dst):
        copy = pltpu.make_async_copy(src, dst, self.sems.at[len(self.all)])
        copy.start()
        self.all.append(copy)

    def wait(self, count=None):
        end = len(self.all) if count is None else self.done + count
        for copy in self.all[self.done : end]:
            copy.wait()
        self.done = end


def lanes(shape):
    return lax.broadcasted_iota(jnp.int32, shape, len(shape) - 1)


def sublanes(shape):
    return lax.broadcasted_iota(jnp.int32, shape, 0)


def swapped(values):
    return jnp.where(
        lanes(values.shape) < HEAD // 2,
        pltpu.roll(values, 2 * HEAD - HEAD // 2, 1),
        pltpu.roll(values, HEAD // 2, 1),
    )


def document_starts(seg):
    starts = jnp.zeros(seg.shape, F32)
    for document in range(8):
        before = jnp.sum(jnp.where(seg < document, 1.0, 0.0), axis=1, keepdims=True)
        starts = starts + jnp.where(seg == document, before, 0.0)
    return starts


def key_codes(mask, code):
    code[0:REACH, :] = jnp.full((REACH, ROWS), -1.0, F32)

    @pl.loop(0, TENSOR)
    def _(i):
        row = mask[:, aligned(i, ROWS)].astype(F32)
        live = jnp.broadcast_to(row, (ROWS, ROWS)).T == 1.0
        places = (sublanes((ROWS, ROWS)) + i * ROWS).astype(F32)
        code[pl.ds(pl.multiple_of(REACH + i * ROWS, ROWS), ROWS), :] = jnp.where(
            live, places, -1.0
        )


def allowed(code, start_row, chunk):
    wide = jnp.concatenate([code, code], axis=1)
    ok = wide >= start_row
    if chunk >= REACH // ROWS:
        key = sublanes((ROWS, PAIR)) + (chunk * ROWS - REACH)
        query = lanes((ROWS, PAIR))
        ok = (ok & (key < query)) | (key == query)
    return ok


def turned_back(grad, r, here):
    cos, sin = r.cosine_t[:, here], r.sine_t[:, here]
    first, second = grad[0 : HEAD // 2], grad[HEAD // 2 : HEAD]
    return jnp.concatenate([first * cos + second * sin, second * cos - first * sin], axis=0)


class Halves:
    def __init__(self, place, parts, twins, sums, send, recv):
        self.place, self.parts, self.twins, self.sums = place, parts, twins, sums
        self.send, self.recv = send, recv

    def half(self, k):
        at = self.place
        return remote(
            self.parts.at[lax.rem(k, SLOTS), aligned(1 - at.core, ROWS), :],
            self.twins.at[k],
            self.send.at[k],
            self.recv.at[k],
            "tensor",
            at.twin,
        )

    def put(self, k, value):
        @pl.when(k >= SLOTS)
        def _():
            self.half(k - SLOTS).wait_send()

        self.parts[lax.rem(k, SLOTS)] = value.astype(BF)
        self.half(k).start()

    def add(self, k):
        self.half(k).wait_recv()
        own = self.parts[lax.rem(k, SLOTS), aligned(self.place.core, ROWS), :].astype(F32)
        self.sums[k] = (own + self.twins[k].astype(F32)).astype(BF)

    def end(self):
        for k in range(CHIPS - SLOTS, CHIPS):
            self.half(k).wait_send()


class Joined:
    def __init__(self, place, sums, crossed, joined, landed, sems):
        self.place, self.sums, self.crossed = place, sums, crossed
        self.joined, self.landed = joined, landed
        self.c_send, self.c_recv, self.send, self.recv = sems

    def cross(self, j):
        return remote(
            self.sums.at[2 * j],
            self.crossed.at[j],
            self.c_send.at[j],
            self.c_recv.at[j],
            "tensor",
            self.place.near_core(0, 1),
        )

    def whole(self, j):
        return remote(
            self.joined.at[j],
            self.landed.at[j],
            self.send.at[j],
            self.recv.at[j],
            "tensor",
            self.place.near_core(j + 1, 0),
        )

    def join(self, j):
        self.cross(j).wait_recv()
        total = self.sums[2 * j + 1].astype(F32) + self.crossed[j].astype(F32)
        self.joined[j] = total.astype(BF)
        self.whole(j).start()

    def result(self):
        self.cross(3).wait_recv()
        total = self.sums[7].astype(F32) + self.crossed[3].astype(F32)
        for j in range(3):
            self.whole(j).wait_recv()
            total = total + self.landed[j].astype(F32)
        return total

    def end(self):
        for j in range(4):
            self.cross(j).wait_send()
        for j in range(3):
            self.whole(j).wait_send()


def unpacked(ref, pair, first):
    both = ref[:, pl.ds(pl.multiple_of(first + pair * 16, 16), 16), :].astype(F32)
    return both[:, 0:8].reshape(ROWS, WIDTH), both[:, 8:16].reshape(ROWS, WIDTH)


def aligned_rows(ref, unit):
    def block(src, part=None):
        if part is None:
            return ref.at[pl.ds(pl.multiple_of(src * 2 * unit, unit), 2 * unit), :]
        return ref.at[pl.ds(pl.multiple_of((src * 2 + part) * unit, unit), unit), :]

    return block


def column_blocks(ref):
    def block(src, part=None):
        if part is None:
            return ref.at[:, aligned(src, ROWS)]
        return ref.at[pl.ds(part * PAIR, PAIR), aligned(src, ROWS)]

    return block


class Stream:
    def __init__(self, place, own, block, r, number):
        self.place, self.own, self.block = place, own, block
        self.send, self.recv = r.e_send, r.e_recv
        self.first_send, self.first_recv = 9 * number, 16 * number

    def at_y(self, k, other=False):
        at = self.place
        column = 1 - at.x if other else at.x
        return 2 * at.y_at(k) + column

    def copy(self, number, src, dest, part=None, own=False):
        ref = self.block(src, part)
        return remote(
            self.own if own else ref,
            ref,
            self.send.at[self.first_send + number],
            self.recv.at[self.first_recv + (8 if part == 1 else 0) + src],
            "dp",
            dest,
        )

    def sent(self, number):
        at, at_y = self.place, self.at_y
        if number == 0:
            return self.copy(0, at.d, at.across, own=True)
        if number < 3:
            return self.copy(number, at.d, at_y(2 * number - 1), own=True)
        if number < 5:
            return self.copy(number, at.across, at_y(2 * number - 5))
        other = number > 6
        if number % 2:
            return self.copy(number, at_y(3, other), at_y(1), 0)
        return self.copy(number, at_y(1, other), at_y(3), 1)

    def arrived(self, src, halves=False):
        for part in (0, 1) if halves else (None,):
            self.copy(0, src, self.place.across, part).wait_recv()

    def start(self):
        for number in (0, 1, 2):
            self.sent(number).start()

    def go_on(self):
        self.arrived(self.place.across)
        self.sent(3).start()
        self.sent(4).start()
        self.arrived(self.at_y(3))
        self.sent(5).start()
        self.arrived(self.at_y(1))
        self.sent(6).start()

    def go_further(self):
        self.arrived(self.at_y(3, True))
        self.sent(7).start()
        self.arrived(self.at_y(1, True))
        self.sent(8).start()

    def finish(self):
        self.arrived(self.at_y(2), True)
        self.arrived(self.at_y(2, True), True)

    def end(self):
        for number in range(9):
            self.sent(number).wait_send()


def expert_streams(at, r, e, gu_all, down_all):
    return (
        Stream(at, r.gu.at[e], aligned_rows(gu_all, HEAD), r, 0),
        Stream(at, r.down.at[e], column_blocks(down_all), r, 1),
    )


def attention_kernel(r):
    at = Place()
    t, d = at.t, at.d
    copies = Copies(r.local)
    copies.start(r.cosine, r.cosine_v)
    copies.start(r.sine, r.sine_v)
    r.hidden_all[aligned(t, ROWS), :] = r.hid[...]
    keyval, out_rows = r.w_keyval[...].astype(F32), r.w_out_t[...].astype(F32)
    r.rows[...] = jnp.concatenate([keyval, out_rows], axis=0).astype(BF)
    r.row_dp[d] = r.rows[...]
    r.shares[...] = jnp.zeros((8, ROWS), F32)
    r.shares[:, 0:32] = r.router[...].astype(F32)
    same = sublanes((8, 8)) == lanes((8, 8))
    for column, gain in ((32, r.gain_one), (33, r.gain_two)):
        wide = jnp.broadcast_to(gain[...].astype(F32), (8, 8))
        r.shares[:, column : column + 1] = jnp.sum(
            jnp.where(same, wide, 0.0), axis=1, keepdims=True
        )
    for j in range(CHIPS):
        tile = jnp.concatenate([keyval[:, j * ROWS : (j + 1) * ROWS], r.shares[...]], axis=0)
        r.tiles[2 * j] = tile.astype(BF)
        r.tiles[2 * j + 1] = tile.astype(BF)
    r.tile_all[d, t] = r.tiles[t]
    r.wq_all[HEAD : 2 * HEAD, :] = jnp.zeros((HEAD, WIDTH), BF)
    r.wq_all[0:HEAD, aligned(d, ROWS)] = r.w_query_t[...]
    at.enter()

    def tile_one(k, src):
        dest = at.tensor_at(k)
        return remote(
            r.tiles.at[dest],
            r.tile_all.at[d, src],
            r.t1_send.at[k],
            r.t1_recv.at[src],
            "tensor",
            dest,
        )

    def tile_two(k, src):
        ref = r.tile_all.at[src]
        return remote(ref, ref, r.t2_send.at[k], r.t2_recv.at[src], "dp", at.dp_at(k))

    def rows_dp(k, src):
        return remote(
            r.rows, r.row_dp.at[src], r.rd_send.at[k], r.rd_recv.at[src], "dp", at.dp_at(k)
        )

    def wq_dp(k, src):
        return remote(
            r.w_query_t,
            r.wq_all.at[pl.ds(0, HEAD), aligned(src, ROWS)],
            r.wq_send.at[k],
            r.wq_recv.at[src],
            "dp",
            at.dp_at(k),
        )

    streams = expert_streams(at, r, 0, r.gu_all, r.down_all)

    for k in range(1, TENSOR):
        tile_one(k, t).start()
    for k in range(1, DP):
        wq_dp(k, d).start()
    ring_h = whole_ring(at, r.hidden_all, r.h_send, r.h_recv)
    ring_h.start()
    copies.start(r.gu.at[0], r.gu_all.at[aligned(d, ROWS), :])
    copies.start(r.down.at[0], r.down_all.at[:, aligned(d, ROWS)])
    copies.start(r.cot, r.cot_all.at[aligned(t, ROWS)])

    key_codes(r.mask, r.code)
    r.starts[...] = document_starts(r.seg[...])
    r.keyvals_v[0:REACH, :] = jnp.zeros((REACH, 2 * HEAD), BF)
    r.keyvals_tv[:, 0:REACH] = jnp.zeros((2 * HEAD, REACH), BF)

    for k in range(1, TENSOR):
        tile_one(k, at.tensor_at(k)).wait_recv()
    for k in range(1, DP):
        tile_two(k, d).start()
    for k in range(1, DP):
        rows_dp(k, d).start()
    for stream in streams:
        stream.start()
    for i in range(1, 4):
        ring_h.pass_on(i)
    for k in range(1, DP):
        wq_dp(k, at.dp_at(k)).wait_recv()
        tile_two(k, at.dp_at(k)).wait_recv()
    for j in range(DP):
        both = r.tile_all[j].astype(F32)
        r.wqk[j * ROWS : (j + 1) * ROWS, ROWS:PAIR] = both[:, 0:8].reshape(ROWS, ROWS).astype(BF)
        r.small[j * ROWS : (j + 1) * ROWS, :] = both[:, 8:16].reshape(ROWS, ROWS).astype(BF)
    r.wqk[:, 0:ROWS] = r.wq_all[...].astype(F32).T.astype(BF)
    columns = r.small[...].astype(F32).T
    gain_one = columns[32:33, :]
    gain_two = columns[33:34, :]
    copies.wait(2)
    ring_o = Ring(
        at,
        lambda b: r.out_all.at[b],
        lambda b, part: r.out_all.at[b, pl.ds(part * 32, 32)],
        r.o_send,
        r.o_recv,
    )

    @pl.loop(0, CHIPS)
    def _(i):
        @pl.when(i == 1)
        def _():
            ring_h.pass_on(4)
            ring_h.pass_on(5)

        @pl.when(i == 2)
        def _():
            for k in range(1, DP):
                rows_dp(k, at.dp_at(k)).wait_recv()
            both = r.row_dp[...].astype(F32)
            r.wqkv_own[0:HEAD, :] = r.wq_all[0:HEAD, :]
            r.wqkv_own[HEAD : 2 * HEAD, :] = both[:, 0:8].reshape(HEAD, WIDTH).astype(BF)
            r.out_all[t] = both[:, 8:16].reshape(HEAD, WIDTH).astype(BF)
            ring_o.start()

        @pl.when(i == 5)
        def _():
            ring_h.pass_on(6)
            ring_h.pass_on(7)

        ring_h.second(i)
        block = at.step(i)
        here = aligned(block, PAIR)
        hidden = r.hidden_all[here, :].astype(F32)
        inverse = lax.rsqrt(jnp.mean(hidden * hidden, axis=1, keepdims=True) + 1e-6)
        unit = (hidden * inverse * gain_one).astype(BF)
        r.normed_v[here, :] = unit
        cos, sin = r.cosine_v[here, :], r.sine_v[here, :]
        projected = dot(unit, r.wqk[...])
        query, keyval = projected[:, 0:ROWS], projected[:, ROWS:PAIR]
        query = (query * cos + swapped(query) * sin).astype(BF)
        r.queries_v[here, :] = (query.astype(F32) * (1.0 / math.sqrt(HEAD))).astype(BF)
        keyval = keyval * cos + swapped(keyval) * sin
        later = pl.ds(pl.multiple_of(REACH + block * PAIR, ROWS), PAIR)
        r.keyvals_v[later, :] = keyval.astype(BF)
        r.keyvals_tv[:, later] = keyval.T.astype(BF)

    copies.start(r.normed_v, r.normed)
    copies.start(r.queries_v, r.queries)
    copies.start(r.keyvals_v, r.keyvals)
    copies.start(r.keyvals_tv, r.keyvals_t)
    ring_o.pass_on(1)
    ring_c = whole_ring(at, r.cot_all, r.c_send, r.c_recv, r.cot)
    ring_c.start()

    def att_copy(dest, src):
        return remote(
            r.att_src.at[dest],
            r.att_t.at[aligned(src, HEAD), :],
            r.a_send.at[dest],
            r.a_recv.at[src],
            "tensor",
            dest,
        )

    @pl.loop(0, CHIPS)
    def _(i):
        for step, chips in ((2, (2, 3)), (5, (4, 5))):

            @pl.when(i == step)
            def _(chips=chips):
                for k in chips:
                    ring_o.pass_on(k)

        block = at.chip_at(i + 1)
        here = aligned(block, PAIR)
        query = r.queries_v[here, :]
        start_row = r.starts[:, here]
        top = jnp.full((1, PAIR), LOWEST, F32)
        for chunk in range(SPAN // ROWS):
            keys = pl.ds(pl.multiple_of(block * PAIR + chunk * ROWS, ROWS), ROWS)
            score = dot(r.keyvals_v[keys, :], query, NT)
            score = jnp.where(allowed(r.code[keys, :], start_row, chunk), score, LOWEST)
            r.scores[chunk * ROWS : (chunk + 1) * ROWS, :] = score
            top = jnp.maximum(top, jnp.max(score, axis=0, keepdims=True))
        total = jnp.zeros((1, PAIR), F32)
        for chunk in range(SPAN // ROWS):
            place = slice(chunk * ROWS, (chunk + 1) * ROWS)
            weight = jnp.exp(r.scores[place, :] - top)
            total = total + jnp.sum(weight, axis=0, keepdims=True)
            r.probs[place, :] = weight.astype(BF)
        window = pl.ds(pl.multiple_of(block * PAIR, ROWS), SPAN)
        head = dot(r.keyvals_tv[HEAD : 2 * HEAD, window], r.probs[...]) / total
        r.heads_t[:, here] = head
        r.stats[:, here] = top + jnp.log(total)
        r.att_src[2 * block] = head[:, 0:ROWS].astype(BF)
        r.att_src[2 * block + 1] = head[:, ROWS:PAIR].astype(BF)

        @pl.when(i < CHIPS - 1)
        def _():
            att_copy(2 * block, t).start()
            att_copy(2 * block + 1, t).start()

        @pl.when(i == CHIPS - 1)
        def _():
            att_copy(at.twin, t).start()

    r.att_t[aligned(t, HEAD), :] = r.att_src[t]
    ring_o.pass_on(6)
    ring_o.pass_on(7)
    for stream in streams:
        stream.go_on()
    for i in range(1, 4):
        ring_c.pass_on(i)
    for i in range(CHIPS):
        ring_o.second(i)

    @pl.loop(0, 4)
    def _(j):
        first, second = unpacked(r.out_all, j, 0)
        r.out_tv[aligned(2 * j, ROWS), :] = first.astype(BF)
        r.out_tv[aligned(2 * j + 1, ROWS), :] = second.astype(BF)

    copies.start(r.out_tv, r.out_t)
    ring_c.pass_on(4)
    ring_c.pass_on(5)
    for k in range(1, TENSOR):
        att_copy(at.tensor_at(k), at.tensor_at(k)).wait_recv()
    attended = r.att_t[...].astype(F32).T.astype(BF)
    r.att_rows[...] = attended
    middle = r.hid[...].astype(F32) + dot(attended, r.out_tv[...], NT)
    r.mid[...] = middle
    inverse = lax.rsqrt(jnp.mean(middle * middle, axis=1, keepdims=True) + 1e-6)
    r.normed_mid[...] = (middle * inverse * gain_two).astype(BF)

    for stream in streams:
        stream.go_further()
    ring_c.pass_on(6)
    ring_c.pass_on(7)
    for i in range(CHIPS):
        ring_c.second(i)
    for stream in streams:
        stream.finish()
    for k in range(1, TENSOR):
        tile_one(k, t).wait_send()
        att_copy(at.tensor_at(k), t).wait_send()
    for k in range(1, DP):
        tile_two(k, d).wait_send()
        rows_dp(k, d).wait_send()
        wq_dp(k, d).wait_send()
    for stream in streams:
        stream.end()
    ring_h.end()
    ring_o.end()
    ring_c.end()
    copies.wait()


def expert_kernel(r):
    at = Place()
    t = at.t
    copies = Copies(r.local)
    copies.start(r.gu_all, r.gus.at[0])
    copies.start(r.down_all, r.downs.at[pl.ds(0, UNITS)])
    copies.start(r.cot_all, r.cots)
    copies.start(r.gu.at[1], r.gus.at[1, aligned(at.d, ROWS)])
    copies.start(r.down.at[1], r.downs.at[pl.ds(UNITS, UNITS), aligned(at.d, ROWS)])
    copies.start(r.out_t, r.out_tv)
    r.nm_all[aligned(t, ROWS), :] = r.normed_mid[...]
    at.enter()
    ring = whole_ring(at, r.nm_all, r.g_send, r.g_recv)
    ring.start()
    halves_n = Halves(at, r.n_parts, r.n_twins, r.n_sums, r.ntw_send, r.ntw_recv)
    halves_m = Halves(at, r.m_parts, r.m_twins, r.m_sums, r.mtw_send, r.mtw_recv)
    joined = Joined(
        at,
        r.n_sums,
        r.n_crossed,
        r.n_joined,
        r.n_landed,
        (r.nc_send, r.nc_recv, r.n_send, r.n_recv),
    )
    streams = expert_streams(at, r, 1, r.gus.at[1], r.downs.at[pl.ds(UNITS, UNITS)])
    for stream in streams:
        stream.start()

    def moe_along(j):
        return remote(
            r.m_sums.at[pl.ds(2 * j, 2)],
            r.m_landed.at[j],
            r.m_send.at[j],
            r.m_recv.at[j],
            "tensor",
            at.near_core(j + 1, 0),
        )

    copies.wait()

    def over_y(k):
        y = at.y_at(k)
        return (
            remote(
                r.gus.at[0, aligned(y, PAIR), :],
                r.y_gu.at[k],
                r.x_send.at[k],
                r.x_recv.at[k],
                "dp",
                2 * y + at.x,
            ),
            remote(
                r.down_first.at[:, aligned(y, PAIR)],
                r.y_down.at[k],
                r.y_send.at[k],
                r.y_recv.at[k],
                "dp",
                2 * y + at.x,
            ),
        )

    def one_pass(e):
        @pl.loop(0, CHIPS)
        def _(i):
            if e == 0:
                ring.pass_on_at(i)
                ring.second(i)

                @pl.when(i == 5)
                def _():
                    for stream in streams:
                        stream.go_on()

            here = aligned(at.step(i) if e == 0 else at.sum_step(i), PAIR)
            nm = r.nm_all[here, :]
            place = lanes((PAIR, ROWS))
            if e == 0:
                r.nm_t[:, here] = nm.T
                expert = sublanes((ROWS, PAIR))
                named = expert == r.routes_t[0:1, here]
                for j in range(1, 8):
                    named = named | (expert == r.routes_t[j : j + 1, here])
                named = jnp.where(named, 1.0, 0.0).T > 0.5
                logits = jnp.where(named, dot(nm, r.small[...]), LOWEST)
                powers = jnp.exp(logits - jnp.max(logits, axis=1, keepdims=True))
                powers = jnp.where(named, powers, 0.0)
                gates = powers / jnp.sum(powers, axis=1, keepdims=True)
            else:
                kept = r.gates[here, :]
                gates = jnp.where(place == 2 * HEAD - 1, 0.0, kept)
                earlier = kept[:, 2 * HEAD - 1 : 2 * HEAD]
            mine = place == 2 * t + e
            gate = jnp.sum(jnp.where(mine, gates, 0.0), axis=1, keepdims=True)
            act_grad = dot(r.cots[here, :], r.downs[e * UNITS : (e + 1) * UNITS, :], NT)
            projected = dot(nm, r.gus[e])
            first, up = projected[:, :UNITS], projected[:, UNITS:]
            sigmoid = 1.0 / (1.0 + jnp.exp(-first))
            silu = first * sigmoid
            activated = silu * up
            gate_grad = jnp.sum(activated * act_grad, axis=1, keepdims=True)
            gate_grads = jnp.where(mine, gate_grad, 0.0)
            weighted = (activated * gate).astype(BF)
            r.weighted_t[:, here] = weighted.T
            act_grad = act_grad * gate
            r.proj_grads[here, 0:UNITS] = (
                act_grad * up * (sigmoid * (1.0 + first * (1.0 - sigmoid)))
            ).astype(BF)
            r.proj_grads[here, UNITS:WIDTH] = (act_grad * silu).astype(BF)
            normed_part = dot(r.proj_grads[here, :], r.gus[e], NT)
            if e == 0:
                r.gates[here, :] = jnp.where(place == 2 * HEAD - 1, gate_grad, gates)
                r.weighted[here, :] = weighted
                r.n_first[here, :] = normed_part.astype(BF)
                return
            gate_grads = gate_grads + jnp.where(place == 2 * t, earlier, 0.0)
            mean = jnp.sum(gates * gate_grads, axis=1, keepdims=True)
            logit_grad = gates * (gate_grads - mean)
            r.logit_t[:, here] = logit_grad.T.astype(BF)
            normed_part = normed_part + dot(logit_grad.astype(BF), r.small[...], NT)
            halves_n.put(i, normed_part + r.n_first[here, :].astype(F32))
            both = jnp.concatenate([r.weighted[here, :], weighted], axis=1)
            halves_m.put(i, dot(both, r.downs[...]))

            @pl.when(i > 0)
            def _():
                halves_n.add(i - 1)
                halves_m.add(i - 1)

            for j in range(4):

                @pl.when(i == 2 * j + 1)
                def _(j=j):
                    joined.cross(j).start()

            for j in range(2):

                @pl.when(i == 2 * j + 4)
                def _(j=j):
                    joined.join(j)

            @pl.when(i == 3)
            def _():
                moe_along(0).start()

    def weight_gradients(e):
        @pl.loop(0, 4)
        def _(j):
            strip = aligned(j, PAIR)
            r.gus[e, strip, :] = dot(r.nm_t[strip, :], r.proj_grads[...]).astype(BF)

        @pl.loop(0, 2)
        def _(j):
            strip = aligned(j, PAIR)
            result = dot(r.weighted_t[strip, :], r.cots[...]).astype(BF)
            if e == 0:
                r.down_first[strip, :] = result
            else:
                r.downs[pl.ds(pl.multiple_of(UNITS + j * PAIR, PAIR), PAIR), :] = result

    one_pass(0)
    for stream in streams:
        stream.go_further()
    weight_gradients(0)
    for k in range(1, 4):
        for copy in over_y(k):
            copy.start()
    for stream in streams:
        stream.finish()
    one_pass(1)
    joined.join(2)
    halves_n.add(CHIPS - 1)
    halves_m.add(CHIPS - 1)
    moe_along(1).start()
    for stream in streams:
        stream.end()
    weight_gradients(1)
    copies.start(r.gus.at[1], r.gu_grad)
    copies.start(r.downs.at[pl.ds(UNITS, UNITS)], r.down_grad)
    r.router_t[...] = dot(r.logit_t[...], r.nm_all[...])[0:32, :]

    gain_two = r.small[...].astype(F32).T[33:34, :]
    normed_grad = joined.result()
    middle = r.mid[...]
    inverse = lax.rsqrt(jnp.mean(middle * middle, axis=1, keepdims=True) + 1e-6)
    unit = middle * inverse
    r.gain_grad[...] = jnp.sum(normed_grad * unit, axis=0, keepdims=True)
    scaled = normed_grad * gain_two
    grad = r.cot[...].astype(F32) + inverse * (
        scaled - unit * jnp.mean(scaled * unit, axis=1, keepdims=True)
    )
    r.mid_grad[...] = grad
    turned = grad.T.reshape(DP, TENSOR, 8, ROWS).transpose(1, 0, 2, 3)
    r.mid_t[...] = turned.reshape(WIDTH, ROWS).astype(BF)
    r.att_grad_t[...] = dot(grad.astype(BF), r.out_tv[...]).T.astype(BF)
    across, own = r.m_sums[6].astype(F32), r.mid[...] + r.m_sums[7].astype(F32)
    for j in range(2):
        moe_along(j).wait_recv()
        across = across + r.m_landed[j, 0].astype(F32)
        own = own + r.m_landed[j, 1].astype(F32)
    r.moe_across[...] = across
    r.moe_own[...] = own
    r.moe_last[...] = r.m_sums[4:6]
    gu = r.gus[0, aligned(at.y, PAIR), :].astype(F32)
    down = r.down_first[:, aligned(at.y, PAIR)].astype(F32)
    for k in range(1, 4):
        for copy in over_y(k):
            copy.wait_recv()
        gu = gu + r.y_gu[k].astype(F32)
        down = down + r.y_down[k].astype(F32)
    r.ys_gu[0] = gu[0:ROWS].astype(BF)
    r.ys_gu[1] = gu[ROWS:PAIR].astype(BF)
    r.ys_down[0] = down[:, 0:ROWS].astype(BF)
    r.ys_down[1] = down[:, ROWS:PAIR].astype(BF)
    for k in range(1, 4):
        for copy in over_y(k):
            copy.wait_send()
    ring.end()
    for j in range(2):
        moe_along(j).wait_send()
    halves_n.end()
    halves_m.end()
    joined.end()
    copies.wait()


def back_kernel(r):
    at = Place()
    t, d = at.t, at.d
    copies = Copies(r.local)
    copies.start(r.queries, r.queries_v)
    copies.start(r.keyvals, r.keyvals_v)
    copies.start(r.keyvals_t, r.keyvals_tv)
    copies.start(r.gu_grad.at[aligned(at.y, PAIR), :], r.gu_own)
    copies.start(r.down_grad.at[:, aligned(at.y, PAIR)], r.down_own)
    copies.start(r.normed, r.normed_v)
    r.grads_t[0:HEAD, :] = jnp.zeros((HEAD, LENGTH), BF)
    r.grads_t[HEAD : 2 * HEAD, aligned(t, ROWS)] = r.att_grad_t[aligned(t, HEAD), :]
    r.wqkv[t] = r.wqkv_own[...]
    at.enter()

    def back_copy(k, src):
        dest = at.tensor_at(k)
        return remote(
            r.att_grad_t.at[aligned(dest, HEAD), :],
            r.grads_t.at[pl.ds(HEAD, HEAD), aligned(src, ROWS)],
            r.g_send.at[k],
            r.g_recv.at[src],
            "tensor",
            dest,
        )

    def then_across():
        return (
            remote(
                r.ys_gu.at[1 - at.x], r.yx_gu0, r.x_send.at[0], r.x_recv.at[0], "dp", at.across
            ),
            remote(
                r.ys_down.at[1 - at.x], r.yx_down0, r.x_send.at[1], r.x_recv.at[1], "dp", at.across
            ),
        )

    def pair(gu_src, gu_dst, down_src, down_dst, number, dest):
        return (
            remote(gu_src, gu_dst, r.gu_send.at[number], r.gu_recv.at[number], "dp", dest),
            remote(down_src, down_dst, r.dn_send.at[number], r.dn_recv.at[number], "dp", dest),
        )

    def over_y(k):
        y = at.y_at(k)
        return pair(
            r.gu_grad.at[aligned(y, PAIR), :],
            r.y_gu.at[k],
            r.down_grad.at[:, aligned(y, PAIR)],
            r.y_down.at[k],
            k,
            2 * y + at.x,
        )

    def then_x():
        return pair(r.s_gu, r.yx_gu, r.s_down, r.yx_down, 0, at.across)

    for k in range(1, TENSOR):
        back_copy(k, t).start()
    ring_w = Ring(
        at,
        lambda b: r.wqkv.at[b],
        lambda b, part: r.wqkv.at[b, pl.ds(part * HEAD, HEAD)],
        r.w_send,
        r.w_recv,
    )
    ring_w.start()
    for k in range(1, 4):
        for copy in over_y(k):
            copy.start()
    for copy in then_across():
        copy.start()

    key_codes(r.mask, r.code)
    r.starts[...] = document_starts(r.seg[...])
    r.kv_sum[...] = jnp.zeros((PADDED, 2 * HEAD), F32)
    r.out_terms[...] = (
        dot(r.mid_t[...], r.att_rows[...]).reshape(CHIPS, ROWS, WIDTH).astype(BF)
    )

    def out_half():
        return remote(
            r.out_terms.at[:, aligned(1 - at.core, HEAD), :],
            r.out_twins,
            r.ot_send.at[0],
            r.ot_recv.at[0],
            "tensor",
            at.twin,
        )

    out_half().start()
    copies.wait(3)
    for k in range(1, TENSOR):
        back_copy(k, at.tensor_at(k)).wait_recv()

    def query_copy(dest, src):
        return remote(
            r.query_src.at[dest],
            r.query_all.at[src],
            r.b_send.at[dest],
            r.b_recv.at[src],
            "tensor",
            dest,
        )

    @pl.loop(0, CHIPS)
    def _(i):
        for step, chips in ((2, (1,)), (3, (2, 3)), (6, (4, 5))):

            @pl.when(i == step)
            def _(chips=chips):
                for k in chips:
                    ring_w.pass_on(k)

        block = at.chip_at(i + 1)
        here = aligned(block, PAIR)
        query = r.queries_v[here, :]
        start_row = r.starts[:, here]
        stat = r.stats[:, here]
        grad_t = r.grads_t[:, here]
        grad_rows = grad_t.astype(F32).T.astype(BF)
        head = r.heads_t[:, here]
        delta = jnp.sum(head * grad_t[HEAD : 2 * HEAD, :].astype(F32), axis=0, keepdims=True)
        query_grad = jnp.zeros((HEAD, PAIR), F32)
        for chunk in range(SPAN // ROWS):
            keys = pl.ds(pl.multiple_of(block * PAIR + chunk * ROWS, ROWS), ROWS)
            both = r.keyvals_v[keys, :]
            score = dot(both, query, NT)
            ok = allowed(r.code[keys, :], start_row, chunk)
            prob = jnp.exp(jnp.where(ok, score - stat, LOWEST))
            prob_grad = dot(both, grad_t)
            score_grad = (prob * (prob_grad - delta)).astype(BF)
            r.kv_sum[keys, :] += dot(score_grad, query) + dot(prob.astype(BF), grad_rows)
            query_grad = query_grad + dot(r.keyvals_tv[0:HEAD, keys], score_grad)
        turned = turned_back(query_grad * (1.0 / math.sqrt(HEAD)), r, here).astype(BF)
        r.tail_left[0:HEAD, here] = turned
        r.query_src[2 * block] = turned[:, 0:ROWS]
        r.query_src[2 * block + 1] = turned[:, ROWS:PAIR]

        @pl.when(i < CHIPS - 1)
        def _():
            query_copy(2 * block, t).start()
            query_copy(2 * block + 1, t).start()

        @pl.when(i == CHIPS - 1)
        def _():
            query_copy(at.twin, t).start()

    @pl.loop(0, CHIPS)
    def _(i):
        here = aligned(i, PAIR)
        grad = r.kv_sum[pl.ds(pl.multiple_of(REACH + i * PAIR, ROWS), PAIR), :].T
        grad = jnp.concatenate(
            [turned_back(grad[0:HEAD], r, here), grad[HEAD : 2 * HEAD]], axis=0
        ).astype(BF)
        r.tail_left[HEAD : 3 * HEAD, here] = grad
        r.back_src[2 * i] = grad[:, 0:ROWS]
        r.back_src[2 * i + 1] = grad[:, ROWS:PAIR]

    def grad_copy(k, src):
        dest = at.tensor_at(k)
        return remote(
            r.back_src.at[dest],
            r.back_all.at[src],
            r.q_send.at[k],
            r.q_recv.at[src],
            "tensor",
            dest,
        )

    for k in range(1, TENSOR):
        grad_copy(k, t).start()
    r.back_all[t] = r.back_src[t]
    r.query_all[t] = r.query_src[t]
    out_half().wait_recv()
    r.out_sums[...] = (
        r.out_terms[:, aligned(at.core, HEAD), :].astype(F32) + r.out_twins[...].astype(F32)
    ).astype(BF)

    def out_along(k):
        return remote(
            r.out_sums.at[pl.ds(2 * lax.rem(at.z + k, 4), 2)],
            r.out_landed.at[k],
            r.o_send.at[k],
            r.o_recv.at[k],
            "tensor",
            at.near_core(k, 0),
        )

    def out_across():
        return remote(
            r.out_joined,
            r.out_crossed,
            r.o_send.at[0],
            r.o_recv.at[0],
            "tensor",
            at.near_core(0, 1),
        )

    def out_total(x):
        total = r.out_sums[2 * at.z + x].astype(F32)
        for k in range(1, 4):
            total = total + r.out_landed[k, x].astype(F32)
        return total

    for k in range(1, 4):
        out_along(k).start()

    def moe_along():
        return remote(
            r.moe_last, r.m_landed, r.m_send.at[0], r.m_recv.at[0], "tensor", at.near_core(3, 0)
        )

    def moe_across():
        return remote(
            r.m_joined, r.m_crossed, r.m_send.at[1], r.m_recv.at[1], "tensor", at.near_core(0, 1)
        )

    moe_along().start()

    copies.wait()
    r.tail[0 : 3 * HEAD, :] = dot(r.tail_left[...], r.normed_v[...]).astype(BF)

    ring_w.pass_on(6)
    ring_w.pass_on(7)
    for i in range(CHIPS):
        ring_w.second(i)

    @pl.loop(0, 4)
    def _(j):
        first, second = unpacked(r.wqkv, j, HEAD)
        r.kv_full[aligned(2 * j, ROWS), :] = first.astype(BF)
        r.kv_full[aligned(2 * j + 1, ROWS), :] = second.astype(BF)

    for k in range(1, TENSOR):
        grad_copy(k, at.tensor_at(k)).wait_recv()
        query_copy(at.tensor_at(k), at.tensor_at(k)).wait_recv()
    query_rows = r.query_all[...].astype(F32).reshape(WIDTH, ROWS).T.astype(BF)
    pairs = r.back_all[...].astype(F32).reshape(CHIPS, 2, ROWS, ROWS)
    kv_rows = (pairs[:, 0] + pairs[:, 1]).reshape(WIDTH, ROWS).T.astype(BF)
    wq_full = r.wqkv[:, 0:HEAD, :].reshape(WIDTH, WIDTH)
    normed_grad = dot(query_rows, wq_full) + dot(kv_rows, r.kv_full[...], NT)
    hidden = r.hid[...].astype(F32)
    inverse = lax.rsqrt(jnp.mean(hidden * hidden, axis=1, keepdims=True) + 1e-6)
    unit = hidden * inverse
    gain_one = r.small[...].astype(F32).T[32:33, :]
    gain_one_grad = jnp.sum(normed_grad * unit, axis=0, keepdims=True)
    scaled = normed_grad * gain_one
    r.hidden_grad[...] = (
        r.mid_grad[...]
        + inverse * (scaled - unit * jnp.mean(scaled * unit, axis=1, keepdims=True))
    ).astype(BF)
    r.tail[3 * HEAD : 3 * HEAD + 32, :] = r.router_t[...].astype(BF)
    row = sublanes((16, WIDTH))
    r.tail[3 * HEAD + 32 : TAIL, :] = jnp.where(
        row == 0, gain_one_grad, jnp.where(row == 1, r.gain_grad[...], 0.0)
    ).astype(BF)

    def tail_copy(k):
        dest = at.dp_at(k)
        return remote(
            r.tail.at[:, aligned(dest, ROWS)],
            r.tail_in.at[k],
            r.t_send.at[k],
            r.t_recv.at[k],
            "dp",
            dest,
        )

    for k in range(1, DP):
        tail_copy(k).start()

    for k in range(1, 4):
        for copy in over_y(k):
            copy.wait_recv()

    def y_total(x):
        here = aligned(x, ROWS)
        gu = r.gu_own[here, :].astype(F32)
        down = r.down_own[:, here].astype(F32)
        for k in range(1, 4):
            gu = gu + r.y_gu[k, here, :].astype(F32)
            down = down + r.y_down[k, :, here].astype(F32)
        return gu, down

    gu, down = y_total(1 - at.x)
    r.s_gu[...] = gu.astype(BF)
    r.s_down[...] = down.astype(BF)
    for copy in then_x():
        copy.start()

    for k in range(1, 4):
        out_along(k).wait_recv()
    r.out_joined[...] = out_total(1 - at.x_far).astype(BF)
    out_across().start()
    moe_along().wait_recv()
    r.m_joined[...] = (r.moe_across[...] + r.m_landed[0].astype(F32)).astype(BF)
    moe_across().start()
    out_across().wait_recv()
    r.out_rows[...] = out_total(at.x_far) + r.out_crossed[...].astype(F32)

    def out_copy(k):
        dest = at.dp_at(k)
        return remote(
            r.out_rows.at[aligned(dest, 8), :],
            r.out_in.at[k],
            r.od_send.at[k],
            r.od_recv.at[k],
            "dp",
            dest,
        )

    for k in range(1, DP):
        out_copy(k).start()

    total = r.tail[:, aligned(d, ROWS)].astype(F32)
    for k in range(1, DP):
        tail_copy(k).wait_recv()
        total = total + r.tail_in[k].astype(F32)
    r.query_out[...] = total[0:HEAD, :]
    turned = jnp.concatenate(
        [total[HEAD:TAIL], jnp.zeros((256 + HEAD - TAIL, ROWS), F32)], axis=0
    ).T
    for j in range(TENSOR):
        r.pieces[j] = turned[j * 8 : (j + 1) * 8, :]

    def last_copy(k, src):
        dest = at.tensor_at(k)
        return remote(
            r.pieces.at[dest], r.last.at[src], r.l_send.at[k], r.l_recv.at[src], "tensor", dest
        )

    for k in range(1, TENSOR):
        last_copy(k, t).start()
    r.last[t] = r.pieces[t]

    moe_across().wait_recv()
    r.output[...] = (
        r.moe_own[...] + r.m_landed[1].astype(F32) + r.m_crossed[...].astype(F32)
    ).astype(BF)

    gu, down = y_total(at.x)
    for copy in then_x():
        copy.wait_recv()
    r.gu_out[1] = gu + r.yx_gu[...].astype(F32)
    r.down_out[1] = down + r.yx_down[...].astype(F32)
    for copy in then_across():
        copy.wait_recv()
    r.gu_out[0] = r.ys_gu[at.x].astype(F32) + r.yx_gu0[...].astype(F32)
    r.down_out[0] = r.ys_down[at.x].astype(F32) + r.yx_down0[...].astype(F32)

    total = r.out_rows[aligned(d, 8), :]
    for k in range(1, DP):
        out_copy(k).wait_recv()
        total = total + r.out_in[k]
    r.out_grad[...] = total
    for k in range(1, TENSOR):
        last_copy(k, at.tensor_at(k)).wait_recv()
    r.kv_out[...] = jnp.concatenate(
        [r.last[2 * j, :, 0:ROWS] + r.last[2 * j + 1, :, 0:ROWS] for j in range(CHIPS)], axis=1
    )
    shared = r.last[0, :, ROWS:PAIR]
    for j in range(1, TENSOR):
        shared = shared + r.last[j, :, ROWS:PAIR]
    r.router_out[...] = shared[:, 0:32]
    wide = jnp.concatenate([shared, jnp.zeros((ROWS - 8, ROWS), F32)], axis=0).T
    r.gain_one_out[...] = wide[32:33, 0:8]
    r.gain_two_out[...] = wide[33:34, 0:8]

    for k in range(1, TENSOR):
        back_copy(k, t).wait_send()
        grad_copy(k, t).wait_send()
        query_copy(at.tensor_at(k), t).wait_send()
        last_copy(k, t).wait_send()
    for k in range(1, 4):
        for copy in over_y(k):
            copy.wait_send()
    for copy in then_across():
        copy.wait_send()
    for copy in then_x():
        copy.wait_send()
    for k in range(1, DP):
        tail_copy(k).wait_send()
        out_copy(k).wait_send()
    out_half().wait_send()
    for k in range(1, 4):
        out_along(k).wait_send()
    out_across().wait_send()
    moe_along().wait_send()
    moe_across().wait_send()
    ring_w.end()


def store_kernel(r):
    copies = Copies(r.local)
    for name in STORED:
        copies.start(getattr(r, name), getattr(r, name + "_kept"))
    for name in STORED:
        copies.wait(1)
        copies.start(getattr(r, name + "_kept"), getattr(r, name + "_done"))
    copies.wait()


STORED = (
    "output",
    "hidden_grad",
    "gain_one_out",
    "query_out",
    "kv_out",
    "out_grad",
    "gain_two_out",
    "router_out",
    "gu_out",
    "down_out",
)


class Refs:
    def __init__(self, names, refs):
        for name, ref in zip(names, refs):
            setattr(self, name, ref)


def call(kernel, number, inputs, outputs, scratch, reaches=True):
    def space(name):
        return pl.BlockSpec(memory_space=pltpu.VMEM if name.endswith("_v") else pl.ANY)

    names = [name.removesuffix("_v") for name in (*inputs, *outputs)] + list(scratch)
    params = {"vmem_limit_bytes": VMEM_BYTES}
    if reaches:
        params |= {"collective_id": number, "has_side_effects": True}
    values = pl.pallas_call(
        lambda *refs: kernel(Refs(names, refs)),
        out_shape=[jax.ShapeDtypeStruct(shape, dtype) for shape, dtype in outputs.values()],
        in_specs=[space(name) for name in inputs],
        out_specs=[space(name) for name in outputs],
        scratch_shapes=list(scratch.values()),
        compiler_params=pltpu.CompilerParams(**params),
        name=kernel.__name__,
    )(*inputs.values())
    return Refs([name.removesuffix("_v") for name in outputs], values)


def sems(**counts):
    return {name: pltpu.SemaphoreType.DMA((count,)) for name, count in counts.items()}


def rope_tables():
    half = HEAD // 2
    freqs = np.exp(
        np.arange(half, dtype=np.float32) * np.float32(-2.0 * math.log(10000.0) / HEAD)
    ).astype(np.float32)
    angles = np.arange(LENGTH, dtype=np.float32)[:, None] * freqs[None, :]
    cos, sin = np.cos(angles).astype(np.float32), np.sin(angles).astype(np.float32)
    ones, zeros = np.ones((LENGTH, HEAD), np.float32), np.zeros((LENGTH, HEAD), np.float32)
    return (
        np.concatenate([cos, cos, ones], axis=1),
        np.concatenate([-sin, sin, zeros], axis=1),
        np.ascontiguousarray(cos.T),
        np.ascontiguousarray(sin.T),
    )


def body(
    hidden,
    seg_ids,
    key_mask,
    routes,
    gain_attn,
    w_query,
    w_keyval,
    w_out,
    gain_mlp,
    w_router,
    w_gate_up,
    w_down,
    cotangent,
):
    V = pltpu.VMEM
    cosine, sine, cosine_t, sine_t = rope_tables()
    hid, cot = hidden[0], cotangent[0]
    a = call(
        attention_kernel,
        1,
        dict(
            hid_v=hid,
            cot=cot,
            w_keyval_v=w_keyval,
            w_out_t_v=w_out.T,
            w_query_t_v=w_query.T,
            router_v=w_router,
            gain_one_v=gain_attn.reshape(1, 8),
            gain_two_v=gain_mlp.reshape(1, 8),
            gu=w_gate_up,
            down=w_down,
            cosine=cosine,
            sine=sine,
            mask_v=key_mask,
            seg_v=seg_ids,
        ),
        dict(
            normed=((LENGTH, WIDTH), BF),
            queries=((LENGTH, 2 * HEAD), BF),
            keyvals=((PADDED, 2 * HEAD), BF),
            keyvals_t=((2 * HEAD, PADDED), BF),
            stats_v=((1, LENGTH), F32),
            heads_t_v=((HEAD, LENGTH), F32),
            mid_v=((ROWS, WIDTH), F32),
            normed_mid_v=((ROWS, WIDTH), BF),
            att_rows_v=((ROWS, WIDTH), BF),
            wqkv_own_v=((ROWS, WIDTH), BF),
            out_t=((WIDTH, WIDTH), BF),
            small_v=((WIDTH, ROWS), BF),
            gu_all=((WIDTH, WIDTH), BF),
            down_all=((UNITS, WIDTH), BF),
            cot_all=((LENGTH, WIDTH), BF),
        ),
        dict(
            cosine_v=V((LENGTH, ROWS), F32),
            sine_v=V((LENGTH, ROWS), F32),
            hidden_all=V((LENGTH, WIDTH), BF),
            normed_v=V((LENGTH, WIDTH), BF),
            queries_v=V((LENGTH, 2 * HEAD), BF),
            keyvals_v=V((PADDED, 2 * HEAD), BF),
            keyvals_tv=V((2 * HEAD, PADDED), BF),
            out_tv=V((WIDTH, WIDTH), BF),
            rows=V((16, WIDTH), BF),
            row_dp=V((DP, 16, WIDTH), BF),
            shares=V((8, ROWS), F32),
            tiles=V((TENSOR, 16, ROWS), BF),
            tile_all=V((DP, TENSOR, 16, ROWS), BF),
            out_all=V((TENSOR, HEAD, WIDTH), BF),
            wq_all=V((2 * HEAD, WIDTH), BF),
            code=V((PADDED, ROWS), F32),
            scores=V((SPAN, PAIR), F32),
            probs=V((SPAN, PAIR), BF),
            starts=V((1, LENGTH), F32),
            wqk=V((WIDTH, PAIR), BF),
            att_src=V((TENSOR, HEAD, ROWS), BF),
            att_t=V((WIDTH, ROWS), BF),
        )
        | sems(
            h_send=17,
            h_recv=32,
            c_send=17,
            c_recv=32,
            o_send=17,
            o_recv=32,
            t1_send=16,
            t1_recv=16,
            t2_send=8,
            t2_recv=8,
            rd_send=8,
            rd_recv=8,
            wq_send=8,
            wq_recv=8,
            e_send=20,
            e_recv=32,
            a_send=16,
            a_recv=16,
            local=16,
        ),
    )
    b = call(
        expert_kernel,
        2,
        dict(
            normed_mid_v=a.normed_mid,
            cot_all=a.cot_all,
            gu_all=a.gu_all,
            down_all=a.down_all,
            gu=w_gate_up,
            down=w_down,
            small_v=a.small,
            routes_t_v=routes[0].T,
            mid_v=a.mid,
            cot_v=cot,
            out_t=a.out_t,
        ),
        dict(
            moe_across_v=((ROWS, WIDTH), F32),
            moe_own_v=((ROWS, WIDTH), F32),
            moe_last_v=((2, ROWS, WIDTH), BF),
            mid_grad_v=((ROWS, WIDTH), F32),
            mid_t_v=((WIDTH, ROWS), BF),
            att_grad_t_v=((WIDTH, ROWS), BF),
            gu_grad=((WIDTH, WIDTH), BF),
            down_grad=((UNITS, WIDTH), BF),
            ys_gu_v=((2, ROWS, WIDTH), BF),
            ys_down_v=((2, UNITS, ROWS), BF),
            router_t_v=((32, WIDTH), F32),
            gain_grad_v=((1, WIDTH), F32),
        ),
        dict(
            out_tv=V((WIDTH, WIDTH), BF),
            nm_all=V((LENGTH, WIDTH), BF),
            nm_t=V((WIDTH, LENGTH), BF),
            cots=V((LENGTH, WIDTH), BF),
            gus=V((2, WIDTH, WIDTH), BF),
            downs=V((WIDTH, WIDTH), BF),
            down_first=V((UNITS, WIDTH), BF),
            weighted=V((LENGTH, UNITS), BF),
            weighted_t=V((UNITS, LENGTH), BF),
            proj_grads=V((LENGTH, WIDTH), BF),
            gates=V((LENGTH, ROWS), F32),
            n_first=V((LENGTH, WIDTH), BF),
            y_gu=V((4, PAIR, WIDTH), BF),
            y_down=V((4, UNITS, PAIR), BF),
            logit_t=V((ROWS, LENGTH), BF),
            n_parts=V((SLOTS, PAIR, WIDTH), BF),
            n_twins=V((CHIPS, ROWS, WIDTH), BF),
            n_sums=V((CHIPS, ROWS, WIDTH), BF),
            n_crossed=V((4, ROWS, WIDTH), BF),
            n_joined=V((3, ROWS, WIDTH), BF),
            n_landed=V((3, ROWS, WIDTH), BF),
            m_parts=V((SLOTS, PAIR, WIDTH), BF),
            m_twins=V((CHIPS, ROWS, WIDTH), BF),
            m_sums=V((CHIPS, ROWS, WIDTH), BF),
            m_landed=V((2, 2, ROWS, WIDTH), BF),
        )
        | sems(
            g_send=17,
            g_recv=32,
            ntw_send=8,
            ntw_recv=8,
            nc_send=4,
            nc_recv=4,
            n_send=3,
            n_recv=3,
            e_send=20,
            e_recv=32,
            mtw_send=8,
            mtw_recv=8,
            x_send=4,
            x_recv=4,
            y_send=4,
            y_recv=4,
            m_send=8,
            m_recv=8,
            local=8,
        ),
    )
    c = call(
        back_kernel,
        3,
        dict(
            att_grad_t_v=b.att_grad_t,
            mid_t_v=b.mid_t,
            mid_grad_v=b.mid_grad,
            moe_across_v=b.moe_across,
            moe_own_v=b.moe_own,
            moe_last_v=b.moe_last,
            gu_grad=b.gu_grad,
            down_grad=b.down_grad,
            ys_gu_v=b.ys_gu,
            ys_down_v=b.ys_down,
            router_t_v=b.router_t,
            gain_grad_v=b.gain_grad,
            queries=a.queries,
            keyvals=a.keyvals,
            keyvals_t=a.keyvals_t,
            stats_v=a.stats,
            heads_t_v=a.heads_t,
            mask_v=key_mask,
            seg_v=seg_ids,
            cosine_t_v=cosine_t,
            sine_t_v=sine_t,
            wqkv_own_v=a.wqkv_own,
            att_rows_v=a.att_rows,
            normed=a.normed,
            hid_v=hid,
            small_v=a.small,
        ),
        dict(
            output_v=((ROWS, WIDTH), BF),
            hidden_grad_v=((ROWS, WIDTH), BF),
            gain_one_out_v=((1, 8), F32),
            query_out_v=((HEAD, ROWS), F32),
            kv_out_v=((8, WIDTH), F32),
            out_grad_v=((8, WIDTH), F32),
            gain_two_out_v=((1, 8), F32),
            router_out_v=((8, 32), F32),
            gu_out_v=((2, ROWS, WIDTH), F32),
            down_out_v=((2, UNITS, ROWS), F32),
        ),
        dict(
            queries_v=V((LENGTH, 2 * HEAD), BF),
            keyvals_v=V((PADDED, 2 * HEAD), BF),
            keyvals_tv=V((2 * HEAD, PADDED), BF),
            normed_v=V((LENGTH, WIDTH), BF),
            gu_own=V((PAIR, WIDTH), BF),
            down_own=V((UNITS, PAIR), BF),
            grads_t=V((2 * HEAD, LENGTH), BF),
            wqkv=V((TENSOR, ROWS, WIDTH), BF),
            kv_full=V((WIDTH, WIDTH), BF),
            code=V((PADDED, ROWS), F32),
            starts=V((1, LENGTH), F32),
            kv_sum=V((PADDED, 2 * HEAD), F32),
            tail_left=V((3 * HEAD, LENGTH), BF),
            query_src=V((TENSOR, HEAD, ROWS), BF),
            query_all=V((TENSOR, HEAD, ROWS), BF),
            back_src=V((TENSOR, ROWS, ROWS), BF),
            back_all=V((TENSOR, ROWS, ROWS), BF),
            out_terms=V((CHIPS, ROWS, WIDTH), BF),
            out_twins=V((CHIPS, HEAD, WIDTH), BF),
            out_sums=V((CHIPS, HEAD, WIDTH), BF),
            out_landed=V((4, 2, HEAD, WIDTH), BF),
            out_joined=V((HEAD, WIDTH), BF),
            out_crossed=V((HEAD, WIDTH), BF),
            out_rows=V((HEAD, WIDTH), F32),
            out_in=V((DP, 8, WIDTH), F32),
            m_landed=V((2, ROWS, WIDTH), BF),
            m_joined=V((ROWS, WIDTH), BF),
            m_crossed=V((ROWS, WIDTH), BF),
            tail=V((TAIL, WIDTH), BF),
            tail_in=V((DP, TAIL, ROWS), BF),
            pieces=V((TENSOR, 8, PAIR), F32),
            last=V((TENSOR, 8, PAIR), F32),
            yx_gu0=V((ROWS, WIDTH), BF),
            yx_down0=V((UNITS, ROWS), BF),
            y_gu=V((4, PAIR, WIDTH), BF),
            y_down=V((4, UNITS, PAIR), BF),
            s_gu=V((ROWS, WIDTH), BF),
            s_down=V((UNITS, ROWS), BF),
            yx_gu=V((ROWS, WIDTH), BF),
            yx_down=V((UNITS, ROWS), BF),
        )
        | sems(
            g_send=16,
            g_recv=16,
            w_send=17,
            w_recv=32,
            q_send=16,
            q_recv=16,
            b_send=16,
            b_recv=16,
            x_send=4,
            x_recv=4,
            gu_send=4,
            gu_recv=4,
            dn_send=4,
            dn_recv=4,
            ot_send=1,
            ot_recv=1,
            o_send=8,
            o_recv=8,
            m_send=8,
            m_recv=8,
            t_send=8,
            t_recv=8,
            od_send=8,
            od_recv=8,
            l_send=16,
            l_recv=16,
            local=8,
        ),
    )
    values = {name: getattr(c, name) for name in STORED}
    done = call(
        store_kernel,
        0,
        values,
        {name + "_done": (value.shape, value.dtype) for name, value in values.items()},
        {name + "_kept": V(value.shape, value.dtype) for name, value in values.items()}
        | sems(local=2 * len(STORED)),
        reaches=False,
    )
    return (
        done.output_done[None],
        done.hidden_grad_done[None],
        done.gain_one_out_done.reshape(8),
        done.query_out_done.T,
        done.kv_out_done,
        done.out_grad_done.T,
        done.gain_two_out_done.reshape(8),
        done.router_out_done,
        done.gu_out_done,
        done.down_out_done,
    )


def solution(mesh):
    return jax.shard_map(
        body,
        mesh=mesh,
        in_specs=(
            P("dp", "tensor", None),
            P("dp", None),
            P("dp", None),
            P("dp", None, None),
            P(("dp", "tensor")),
            P("dp", "tensor"),
            P(("dp", "tensor"), None),
            P(None, ("dp", "tensor")),
            P(("dp", "tensor")),
            P(("dp", "tensor"), None),
            P("tensor", "dp", None),
            P("tensor", None, "dp"),
            P("dp", "tensor", None),
        ),
        out_specs=(
            P("dp", "tensor", None),
            P("dp", "tensor", None),
            P(("dp", "tensor")),
            P("dp", "tensor"),
            P(("dp", "tensor"), None),
            P(None, ("dp", "tensor")),
            P(("dp", "tensor")),
            P(("dp", "tensor"), None),
            P("tensor", "dp", None),
            P("tensor", None, "dp"),
        ),
        check_vma=False,
    )
```

time: 1980 us -> 261 us (0.13); the launches traced: 1960 us -> 261 us
  waiting for transfers between devices: 1240 us -> 0 us
  local copies, waits for them, and re-layouts: 472 us -> 0 us
  Pallas kernels: 0 us -> 260 us
  matrix products: 133 us -> 0 us
  other arithmetic: 69.6 us -> 0 us
    unnamed x11 -> x0, waiting for transfers between devices: 645 us -> none
    all_gather x5 -> x0, waiting for transfers between devices: 376 us -> none  [the longest x2 328 us: gather_turned(): lax.all_gather(both, axis, axis=0, tiled=True)]
    gather x20 -> x0, local copies, waits for them, and re-layouts: 267 us -> none  [the longest x4 132 us: body(): chosen = jnp.take_along_axis(logits, route_ids, axis=1)]
    pallas_call x0 -> x4, Pallas kernels: none -> 260 us  [call(): pl.pallas_call(lambda *refs: kernel(Refs(names, refs)), out_shape=[jax.Sh...]
    reduce_scatter x4 -> x0, waiting for transfers between devices: 216 us -> none  [the longest x1 101 us: sum_packed(): lax.psum_scatter(lines, axis, tiled=True).reshape(-1)]
    dot_general x56 -> x0, matrix products: 133 us -> none  [the longest x22 68.4 us: times_transposed(): lax.dot_general(left, right, (((1,), (1,)), ((), ())), preferred_element_...]
    dynamic_update_slice x25 -> x0, local copies, waits for them, and re-layouts: 53.9 us -> none  [the longest x8 15.1 us: head_backward(): lax.scan(one_block, (empty, empty), jnp.arange(length // rows, dtype=jnp....]
    reshape x10 -> x0, local copies, waits for them, and re-layouts: 33.4 us -> none  [the longest x2 18.3 us: sum_packed(): jnp.pad(lines, ((0, 0), (0, rows * 128 - lines.shape[1]))).reshape(-1, 128)]
  transfers between devices with their start and end apart: 11 -> 0, of which waited for: 8 -> 0; matrix products, arithmetic and copies ran while one was open for 14% -> 0% of each run, Pallas kernels for 0% -> 0%
where the time goes in v2:
time: 261 us
  Pallas kernels  260 us (100%)
    pallas_call x4, Pallas kernels, call(): pl.pallas_call(lambda *refs: kernel(Refs(names, refs)), out_shape=[jax.Sh...  260 us

profile of v2, /device:TPU:1, one launch (start us, length us, event | category | flops | bytes accessed | tf_op | source)
XLA Modules:
  0.0 260.7 jit_solution(204922739316222145)
XLA Ops:
  0.6 75.9 %attention_kernel.1 = (bf16[2048,1024]{1,0:T(8,128)(2,1)}, bf16[2048,128]{1,0:T(8,128)(2,1)}, bf16[2944,128]{1,0:T(8,128)(2,1)}, bf16[128,2944]{1,0:T(8,128)(2,1...) custom-call(bf16[128,1024]{1,0:T(8,128)(2,1)} %bitcast.15, ...), custom_call_target="tpu_custom_call" | custom-call | tf_op jit(solution)/shard_map/attention_kernel/pallas_call | solution.py:1393
  76.5 99.4 %expert_kernel.1 = (f32[128,1024]{1,0:T(8,128)}, f32[128,1024]{1,0:T(8,128)}, bf16[2,128,1024]{2,1,0:T(8,128)(2,1)}, f32[128,1024]{1,0:T(8,128)}, bf16[1024,128]...) custom-call(bf16[128,1024]{1,0:T(8,128)(2,1)} %get-tuple-element.57., ...), custom_call_target="tpu_custom_call" | custom-call | tf_op jit(solution)/shard_map/expert_kernel/pallas_call | solution.py:1393
  175.9 81.9 %back_kernel.1 = (bf16[128,1024]{1,0:T(8,128)(2,1)}, bf16[128,1024]{1,0:T(8,128)(2,1)}, f32[1,8]{1,0:T(1,128)}, f32[64,128]{1,0:T(8,128)}, f32[8,1024]{1,0:T(8,1...) custom-call(bf16[1024,128]{1,0:T(8,128)(2,1)} %get-tuple-element.64., ...), custom_call_target="tpu_custom_call" | custom-call | tf_op jit(solution)/shard_map/back_kernel/pallas_call | solution.py:1393
  257.8 2.8 %store_kernel.1 = (bf16[128,1024]{1,0:T(8,128)(2,1)}, bf16[128,1024]{1,0:T(8,128)(2,1)}, f32[1,8]{1,0:T(1,128)}, f32[64,128]{1,0:T(8,128)}, f32[8,1024]{1,0:T(8,...) custom-call(bf16[128,1024]{1,0:T(8,128)(2,1)} %get-tuple-element.84., ...), custom_call_target="tpu_custom_call" | custom-call | tf_op jit(solution)/shard_map/store_kernel/pallas_call | solution.py:1393

commit v3 on v2

v3 whole, which is shorter than its diff:
```python
import math

import jax
import jax.numpy as jnp
import numpy as np
from jax import lax
from jax.experimental import pallas as pl
from jax.experimental.pallas import tpu as pltpu
from jax.sharding import PartitionSpec as P

HEAD = 64
LENGTH = 2048
WIDTH = 1024
UNITS = 512
ROWS = 128
PAIR = 256
CHUNK = 384
REACH = 896
SPAN = REACH + PAIR
PADDED = REACH + LENGTH
CHIPS = 8
TENSOR = 16
DP = 8
TAIL = 240
SLOTS = 2
STEP_Z = (0, 0, 1, 3, 1, 3, 2, 2)
STEP_X = (0, 1, 0, 0, 1, 1, 0, 1)
SUM_Z = (2, 2, 1, 1, 3, 3, 0, 0)
SUM_X = (1, 0, 1, 0, 1, 0, 1, 0)
LOWEST = -1e30
TP = "tensor"
SP = "dp"
BF = jnp.bfloat16
F32 = jnp.float32
MESH = pl.DeviceIdType.MESH
VMEM_BYTES = 63 * 1024 * 1024

NN = (((1,), (0,)), ((), ()))
NT = (((1,), (1,)), ((), ()))
TN = (((0,), (0,)), ((), ()))


def dot(left, right, dims=NN):
    return lax.dot_general(left, right, dims, preferred_element_type=F32)


def aligned(value, size):
    return pl.ds(pl.multiple_of(value * size, size), size)


def remote(src, dst, send, recv, axis, index):
    return pltpu.make_async_remote_copy(
        src_ref=src,
        dst_ref=dst,
        send_sem=send,
        recv_sem=recv,
        device_id={axis: index},
        device_id_type=MESH,
    )


def all_sent(ref, sem, place):
    remote(ref, ref, sem, sem, TP, place.twin).wait_send()


def all_landed(ref, sem, place):
    remote(ref, ref, sem, sem, TP, place.twin).wait_recv()


class Place:
    def __init__(self):
        self.t = lax.axis_index(TP)
        self.d = lax.axis_index(SP)
        self.core = lax.rem(self.t, 2)
        self.chip = self.t // 2
        self.twin = self.t + 1 - 2 * self.core
        self.x = lax.rem(self.d, 2)
        self.y = self.d // 2
        self.across = self.d + 1 - 2 * self.x
        self.z = self.chip // 2
        self.x_far = lax.rem(self.chip, 2)

    def chip_at(self, k):
        return lax.rem(self.chip + k, CHIPS)

    def same_core(self, k):
        return 2 * self.chip_at(k) + self.core

    def near(self, dz, dx):
        return 2 * lax.rem(self.z + dz, 4) + lax.rem(self.x_far + dx, 2)

    def near_core(self, dz, dx):
        return 2 * self.near(dz, dx) + self.core

    def listed(self, i, all_z, all_x):
        if isinstance(i, int):
            return self.near(all_z[i], all_x[i])
        dz, dx = jnp.int32(0), jnp.int32(0)
        for k in range(CHIPS):
            dz = jnp.where(i == k, all_z[k], dz)
            dx = jnp.where(i == k, all_x[k], dx)
        return self.near(dz, dx)

    def step(self, i):
        return self.listed(i, STEP_Z, STEP_X)

    def sum_step(self, i):
        return self.listed(i, SUM_Z, SUM_X)

    def step_core(self, i):
        return 2 * self.step(i) + self.core

    def tensor_at(self, k):
        return lax.rem(self.t + k, TENSOR)

    def dp_at(self, k):
        return lax.rem(self.d + k, DP)

    def y_at(self, k):
        return lax.rem(self.y + k, 4)

    def enter(self):
        barrier = pltpu.get_barrier_semaphore()
        for k in range(1, TENSOR):
            pl.semaphore_signal(
                barrier, inc=1, device_id={TP: self.tensor_at(k)}, device_id_type=MESH
            )
        for k in range(1, DP):
            pl.semaphore_signal(
                barrier, inc=1, device_id={SP: self.dp_at(k)}, device_id_type=MESH
            )
        pl.semaphore_wait(barrier, TENSOR + DP - 2)


class Spread:
    def __init__(self, place, block, send, recv, source=None):
        self.place, self.block, self.send, self.recv = place, block, send, recv
        self.source = source

    def copy(self, number, index, dest, source=None):
        src = self.block(index) if source is None else source
        return remote(
            src, self.block(index), self.send.at[number], self.recv.at[index], TP, dest
        )

    def own(self, k):
        dest = self.place.twin if k == 0 else self.place.same_core(k)
        return self.copy(k, self.place.t, dest, self.source)

    def start(self):
        for k in range(1, CHIPS):
            self.own(k).start()
        self.own(0).start()

    def passed(self, k):
        return self.copy(CHIPS + k, self.place.same_core(k), self.place.twin)

    def arrived(self, index):
        self.copy(0, index, self.place.twin).wait_recv()

    def first(self, k):
        self.arrived(self.place.same_core(k))
        self.passed(k).start()

    def second(self, k):
        self.arrived(2 * self.place.chip_at(k) + 1 - self.place.core)

    def end(self):
        for k in range(CHIPS):
            self.own(k).wait_send()
        for k in range(1, CHIPS):
            self.passed(k).wait_send()


class Ring:
    SENDS = 17

    def __init__(self, place, block, half, send, recv, source=None, most=None):
        self.place, self.block, self.half = place, block, half
        self.send, self.recv, self.source, self.most = send, recv, source, most

    def send_sem(self, number):
        return self.send.at[number if self.most is None else 0]

    def copy(self, number, index, dest, source=None):
        src = self.block(index) if source is None else source
        return remote(
            src, self.block(index), self.send_sem(number), self.recv.at[index], TP, dest
        )

    def piece(self, number, index, part, dest):
        ref = self.half(index, part)
        place = TENSOR + lax.rem(index // 2, 2) if part else index
        return remote(ref, ref, self.send_sem(number), self.recv.at[place], TP, dest)

    def sent(self, number):
        at = self.place
        if number == 0:
            return self.copy(0, at.t, at.twin, self.source)
        if number < 4:
            return self.copy(number, at.t, at.step_core(number), self.source)
        if number < 6:
            return self.copy(number, at.step_core(1), at.step_core(number - 2))
        if number < 8:
            return self.piece(number, at.step_core(2 * number - 9), 0, at.step_core(2))
        if number < 10:
            return self.piece(number, at.step_core(2 * number - 14), 1, at.step_core(3))
        return self.copy(number, at.step_core(number - 9), at.twin)

    def start(self):
        for number in (1, 2, 3, 0):
            self.sent(number).start()

    def pass_on(self, i):
        index = self.place.step_core(i)
        if i < 6:
            self.copy(0, index, self.place.twin).wait_recv()
        else:
            self.piece(0, index, 0, self.place.twin).wait_recv()
            self.piece(0, index, 1, self.place.twin).wait_recv()
        for number in {1: (4, 5), 2: (8,), 3: (6,), 4: (9,), 5: (7,)}.get(i, ()):
            self.sent(number).start()
        self.sent(9 + i).start()

    def pass_on_at(self, i):
        for k in range(1, CHIPS):

            @pl.when(i == k - 1)
            def _(k=k):
                self.pass_on(k)

    def second(self, i):
        self.copy(0, 2 * self.place.step(i) + 1 - self.place.core, self.place.twin).wait_recv()

    def end(self):
        if self.most is not None:
            all_sent(self.most, self.send.at[0], self.place)
            return
        for number in range(self.SENDS):
            self.sent(number).wait_send()


def whole_ring(place, ref, send, recv, source=None):
    return Ring(
        place,
        lambda b: ref.at[aligned(b, ROWS)],
        lambda b, part: ref.at[pl.ds(pl.multiple_of(b * ROWS + part * HEAD, HEAD), HEAD)],
        send,
        recv,
        source,
        ref.at[pl.ds(0, 15 * ROWS)],
    )


class Copies:
    def __init__(self, sems):
        self.sems, self.all, self.done = sems, [], 0

    def start(self, src, dst):
        copy = pltpu.make_async_copy(src, dst, self.sems.at[len(self.all)])
        copy.start()
        self.all.append(copy)

    def wait(self, count=None):
        end = len(self.all) if count is None else self.done + count
        for copy in self.all[self.done : end]:
            copy.wait()
        self.done = end


def lanes(shape):
    return lax.broadcasted_iota(jnp.int32, shape, len(shape) - 1)


def sublanes(shape):
    return lax.broadcasted_iota(jnp.int32, shape, 0)


def swapped(values):
    return jnp.where(
        lanes(values.shape) < HEAD // 2,
        pltpu.roll(values, 2 * HEAD - HEAD // 2, 1),
        pltpu.roll(values, HEAD // 2, 1),
    )


def document_starts(seg):
    starts = jnp.zeros(seg.shape, F32)
    for document in range(8):
        before = jnp.sum(jnp.where(seg < document, 1.0, 0.0), axis=1, keepdims=True)
        starts = starts + jnp.where(seg == document, before, 0.0)
    return starts


def key_codes(mask, code):
    code[0:REACH, :] = jnp.full((REACH, ROWS), -1.0, F32)

    @pl.loop(0, TENSOR)
    def _(i):
        row = mask[:, aligned(i, ROWS)].astype(F32)
        live = jnp.broadcast_to(row, (ROWS, ROWS)).T == 1.0
        places = (sublanes((ROWS, ROWS)) + i * ROWS).astype(F32)
        code[pl.ds(pl.multiple_of(REACH + i * ROWS, ROWS), ROWS), :] = jnp.where(
            live, places, -1.0
        )


def allowed(code, start_row, chunk):
    ok = jnp.concatenate([code, code], axis=1) >= start_row
    if (chunk + 1) * CHUNK > REACH:
        key = sublanes((CHUNK, PAIR)) + (chunk * CHUNK - REACH)
        query = lanes((CHUNK, PAIR))
        ok = (ok & (key < query)) | (key == query)
    return ok


def turned_back(grad, r, here):
    cos, sin = r.cosine_t[:, here], r.sine_t[:, here]
    first, second = grad[0 : HEAD // 2], grad[HEAD // 2 : HEAD]
    return jnp.concatenate([first * cos + second * sin, second * cos - first * sin], axis=0)


class Halves:
    def __init__(self, place, parts, twins, sums, send, recv):
        self.place, self.parts, self.twins, self.sums = place, parts, twins, sums
        self.send, self.recv = send, recv

    def half(self, k):
        at = self.place
        return remote(
            self.parts.at[lax.rem(k, SLOTS), aligned(1 - at.core, ROWS), :],
            self.twins.at[k],
            self.send.at[lax.rem(k, SLOTS)],
            self.recv.at[k],
            TP,
            at.twin,
        )

    def put(self, k, value):
        @pl.when(k >= SLOTS)
        def _():
            self.half(k - SLOTS).wait_send()

        self.parts[lax.rem(k, SLOTS)] = value.astype(BF)
        self.half(k).start()

    def add(self, k):
        self.half(k).wait_recv()
        own = self.parts[lax.rem(k, SLOTS), aligned(self.place.core, ROWS), :].astype(F32)
        self.sums(k)[...] = (own + self.twins[k].astype(F32)).astype(BF)

    def end(self):
        for k in range(CHIPS - SLOTS, CHIPS):
            self.half(k).wait_send()


class Joined:
    def __init__(self, place, sums, crossed, landed, sems):
        self.place, self.sums, self.crossed, self.landed = place, sums, crossed, landed
        self.c_send, self.c_recv, self.send, self.recv = sems

    def cross(self, j):
        return remote(
            self.sums.at[2 * j],
            self.crossed.at[j],
            self.c_send.at[j],
            self.c_recv.at[j],
            TP,
            self.place.near_core(0, 1),
        )

    def whole(self, j):
        return remote(
            self.sums.at[2 * j + 1],
            self.landed.at[j],
            self.send.at[j],
            self.recv.at[j],
            TP,
            self.place.near_core(SUM_Z[2 * j], 0),
        )

    def join(self, j):
        self.cross(j).wait_recv()
        total = self.sums[2 * j + 1].astype(F32) + self.crossed[j].astype(F32)
        self.sums[2 * j + 1] = total.astype(BF)
        self.whole(j).start()

    def result(self):
        self.cross(3).wait_recv()
        total = self.sums[7].astype(F32) + self.crossed[3].astype(F32)
        for j in range(3):
            self.whole(j).wait_recv()
            total = total + self.landed[j].astype(F32)
        return total

    def end(self):
        for j in range(4):
            self.cross(j).wait_send()
        for j in range(3):
            self.whole(j).wait_send()


def unpacked(both):
    return both[:, 0:8].reshape(ROWS, WIDTH), both[:, 8:16].reshape(ROWS, WIDTH)


def aligned_rows(ref, unit):
    def block(src, part=None):
        if part is None:
            return ref.at[pl.ds(pl.multiple_of(src * 2 * unit, unit), 2 * unit), :]
        return ref.at[pl.ds(pl.multiple_of((src * 2 + part) * unit, unit), unit), :]

    return block


def column_blocks(ref):
    def block(src, part=None):
        if part is None:
            return ref.at[:, aligned(src, ROWS)]
        return ref.at[pl.ds(part * PAIR, PAIR), aligned(src, ROWS)]

    return block


class Stream:
    def __init__(self, place, own, block, most, r, number):
        self.place, self.own, self.block, self.most = place, own, block, most
        self.send, self.recv = r.e_send, r.e_recv
        self.number, self.first_recv = number, 10 * number

    def at_y(self, k, other=False):
        at = self.place
        column = 1 - at.x if other else at.x
        return 2 * at.y_at(k) + column

    def copy(self, number, src, dest, part=None, source=None):
        ref = self.block(src, part)
        return remote(
            ref if source is None else source,
            ref,
            self.send.at[self.number],
            self.recv.at[self.first_recv + (8 + lax.rem(src, 2) if part else src)],
            SP,
            dest,
        )

    def sent(self, number):
        at, at_y = self.place, self.at_y
        if number == 0:
            return self.copy(0, at.d, at.across, source=self.own)
        if number < 3:
            return self.copy(number, at.d, at_y(2 * number - 1), source=self.own)
        if number < 5:
            return self.copy(number, at.across, at_y(2 * number - 5))
        other = number > 6
        if number % 2:
            return self.copy(number, at_y(3, other), at_y(1), 0)
        return self.copy(number, at_y(1, other), at_y(3), 1)

    def arrived(self, src, halves=False):
        for part in (0, 1) if halves else (None,):
            self.copy(0, src, self.place.across, part).wait_recv()

    def start_x(self):
        self.sent(0).start()

    def start_y(self):
        self.sent(1).start()
        self.sent(2).start()

    def from_across(self):
        self.arrived(self.place.across)
        self.sent(3).start()
        self.sent(4).start()

    def from_y(self):
        self.arrived(self.at_y(3))
        self.sent(5).start()
        self.arrived(self.at_y(1))
        self.sent(6).start()

    def from_y_across(self):
        self.arrived(self.at_y(3, True))
        self.sent(7).start()
        self.arrived(self.at_y(1, True))
        self.sent(8).start()

    def finish(self):
        self.arrived(self.at_y(2), True)
        self.arrived(self.at_y(2, True), True)

    def end(self):
        all_sent(self.most, self.send.at[self.number], self.place)


def expert_streams(at, r, e):
    downs = r.downs.at[pl.ds(e * UNITS, UNITS)]
    return (
        Stream(
            at,
            r.gu.at[e],
            aligned_rows(r.gus.at[e], HEAD),
            r.gus.at[e, pl.ds(0, 7 * ROWS)],
            r,
            2 * e,
        ),
        Stream(
            at,
            r.down.at[e],
            column_blocks(downs),
            downs.at[:, pl.ds(0, 7 * ROWS)],
            r,
            2 * e + 1,
        ),
    )


def layer_kernel(r):
    at = Place()
    t, d = at.t, at.d
    copies = Copies(r.local)
    r.load()
    r.hidden_all[aligned(t, ROWS), :] = r.hid[...]
    keyval, out_rows = r.w_keyval[...].astype(F32), r.w_out_t[...].astype(F32)
    r.rows[...] = jnp.concatenate([keyval, out_rows], axis=0).astype(BF)
    r.row_dp[d] = r.rows[...]
    r.shares[...] = jnp.zeros((8, ROWS), F32)
    r.shares[:, 0:32] = r.router[...].astype(F32)
    same = sublanes((8, 8)) == lanes((8, 8))
    for column, gain in ((32, r.gain_one), (33, r.gain_two)):
        wide = jnp.broadcast_to(gain[...].astype(F32), (8, 8))
        r.shares[:, column : column + 1] = jnp.sum(
            jnp.where(same, wide, 0.0), axis=1, keepdims=True
        )
    for j in range(CHIPS):
        tile = jnp.concatenate([keyval[:, j * ROWS : (j + 1) * ROWS], r.shares[...]], axis=0)
        r.tiles[2 * j] = tile.astype(BF)
        r.tiles[2 * j + 1] = tile.astype(BF)
    r.tile_all[d, t] = r.tiles[t]
    r.wq_all[HEAD : 2 * HEAD, :] = jnp.zeros((HEAD, WIDTH), BF)
    r.wq_all[0:HEAD, aligned(d, ROWS)] = r.w_query_t[...]
    at.enter()

    def tile_one(k, src):
        dest = at.tensor_at(k)
        return remote(
            r.tiles.at[dest],
            r.tile_all.at[d, src],
            r.t1_send.at[0],
            r.t1_recv.at[0],
            TP,
            dest,
        )

    def tile_two(k, src):
        ref = r.tile_all.at[src]
        return remote(ref, ref, r.t2_send.at[0], r.t2_recv.at[0], SP, at.dp_at(k))

    def rows_dp(k, src):
        return remote(
            r.rows, r.row_dp.at[src], r.rd_send.at[0], r.rd_recv.at[0], SP, at.dp_at(k)
        )

    def wq_dp(k, src):
        return remote(
            r.w_query_t,
            r.wq_all.at[pl.ds(0, HEAD), aligned(src, ROWS)],
            r.wq_send.at[0],
            r.wq_recv.at[0],
            SP,
            at.dp_at(k),
        )

    first_expert, second_expert = expert_streams(at, r, 0), expert_streams(at, r, 1)

    for k in range(1, TENSOR):
        tile_one(k, t).start()
    for k in range(1, DP):
        wq_dp(k, d).start()
    ring_h = whole_ring(at, r.hidden_all, r.h_send, r.h_recv)
    ring_h.start()
    for e in range(2):
        copies.start(r.gu.at[e], r.gus.at[e, aligned(d, ROWS)])
        copies.start(r.down.at[e], r.downs.at[pl.ds(e * UNITS, UNITS), aligned(d, ROWS)])
    copies.start(r.cot, r.cots.at[aligned(t, ROWS)])

    key_codes(r.mask, r.code)
    r.starts[...] = document_starts(r.seg[...])
    r.keyvals[0:REACH, :] = jnp.zeros((REACH, 2 * HEAD), BF)
    r.keyvals_t[:, 0:REACH] = jnp.zeros((2 * HEAD, REACH), BF)

    all_landed(r.tile_all.at[0, pl.ds(0, 15)], r.t1_recv.at[0], at)
    for k in range(1, DP):
        tile_two(k, d).start()
    for k in range(1, DP):
        rows_dp(k, d).start()
    for stream in first_expert:
        stream.start_x()
        stream.start_y()
    for i in range(1, 4):
        ring_h.pass_on(i)
    seven_wq = r.wq_all.at[pl.ds(0, HEAD), pl.ds(0, 7 * ROWS)]
    all_landed(seven_wq, r.wq_recv.at[0], at)
    all_landed(r.tile_all.at[pl.ds(0, 7)], r.t2_recv.at[0], at)
    for j in range(DP):
        both = r.tile_all[j].astype(F32)
        r.wqk[j * ROWS : (j + 1) * ROWS, ROWS:PAIR] = both[:, 0:8].reshape(ROWS, ROWS).astype(BF)
        r.small[j * ROWS : (j + 1) * ROWS, :] = both[:, 8:16].reshape(ROWS, ROWS).astype(BF)
    r.wqk[:, 0:ROWS] = r.wq_all[...].astype(F32).T.astype(BF)
    columns = r.small[...].astype(F32).T
    gain_one = columns[32:33, :]
    gain_two = columns[33:34, :]
    r.need("cosine", "sine")
    ring_o = Ring(
        at,
        lambda b: r.out_all.at[b // 2, aligned(lax.rem(b, 2), HEAD)],
        lambda b, part: r.out_all.at[b // 2, aligned(2 * lax.rem(b, 2) + part, 32)],
        r.o_send,
        r.o_recv,
    )

    ring_c = whole_ring(at, r.cots, r.c_send, r.c_recv, r.cot)
    @pl.loop(0, CHIPS)
    def _(i):
        @pl.when(i == 1)
        def _():
            ring_h.pass_on(4)
            ring_h.pass_on(5)

        @pl.when(i == 2)
        def _():
            all_landed(r.row_dp.at[pl.ds(0, 7)], r.rd_recv.at[0], at)
            both = r.row_dp[...].astype(F32)
            r.wqkv_own[0:HEAD, :] = r.wq_all[0:HEAD, :]
            r.wqkv_own[HEAD : 2 * HEAD, :] = both[:, 0:8].reshape(HEAD, WIDTH).astype(BF)
            r.out_all[at.chip, aligned(at.core, HEAD), :] = (
                both[:, 8:16].reshape(HEAD, WIDTH).astype(BF)
            )
            ring_o.start()

        @pl.when(i == 4)
        def _():
            ring_c.start()

        @pl.when(i == 5)
        def _():
            ring_h.pass_on(6)
            ring_h.pass_on(7)

        ring_h.second(i)
        block = at.step(i)
        here = aligned(block, PAIR)
        hidden = r.hidden_all[here, :].astype(F32)
        inverse = lax.rsqrt(jnp.mean(hidden * hidden, axis=1, keepdims=True) + 1e-6)
        unit = (hidden * inverse * gain_one).astype(BF)
        r.normed[here, :] = unit
        cos, sin = r.cosine[here, :], r.sine[here, :]
        projected = dot(unit, r.wqk[...])
        query, keyval = projected[:, 0:ROWS], projected[:, ROWS:PAIR]
        query = (query * cos + swapped(query) * sin).astype(BF)
        r.queries[here, :] = (query.astype(F32) * (1.0 / math.sqrt(HEAD))).astype(BF)
        keyval = keyval * cos + swapped(keyval) * sin
        later = pl.ds(pl.multiple_of(REACH + block * PAIR, ROWS), PAIR)
        r.keyvals[later, :] = keyval.astype(BF)
        r.keyvals_t[:, later] = keyval.T.astype(BF)

    r.save("normed", "queries", "keyvals", "keyvals_t", "small")
    ring_o.pass_on(1)
    for stream in first_expert:
        stream.from_across()
    for stream in first_expert:
        stream.from_y()
    for stream in second_expert:
        stream.start_x()

    def att_copy(dest, src):
        return remote(
            r.att_src.at[dest],
            r.att_t.at[aligned(src, HEAD), :],
            r.a_send.at[0],
            r.a_recv.at[0],
            TP,
            dest,
        )

    @pl.loop(0, CHIPS)
    def _(i):
        for step, ring, chips in (
            (0, ring_o, (2, 3)),
            (4, ring_o, (4, 5)),
        ):

            @pl.when(i == step)
            def _(ring=ring, chips=chips):
                for k in chips:
                    ring.pass_on(k)

        block = at.chip_at(i + 1)
        here = aligned(block, PAIR)
        query = r.queries[here, :]
        start_row = r.starts[:, here]
        top = jnp.full((1, PAIR), LOWEST, F32)
        for chunk in range(SPAN // CHUNK):
            keys = pl.ds(pl.multiple_of(block * PAIR + chunk * CHUNK, ROWS), CHUNK)
            score = dot(r.keyvals[keys, :], query, NT)
            score = jnp.where(allowed(r.code[keys, :], start_row, chunk), score, LOWEST)
            r.scores[chunk * CHUNK : (chunk + 1) * CHUNK, :] = score
            top = jnp.maximum(top, jnp.max(score, axis=0, keepdims=True))
        total = jnp.zeros((1, PAIR), F32)
        for chunk in range(SPAN // CHUNK):
            place = slice(chunk * CHUNK, (chunk + 1) * CHUNK)
            weight = jnp.exp(r.scores[place, :] - top)
            total = total + jnp.sum(weight, axis=0, keepdims=True)
            r.probs[place, :] = weight.astype(BF)
        window = pl.ds(pl.multiple_of(block * PAIR, ROWS), SPAN)
        head = dot(r.keyvals_t[HEAD : 2 * HEAD, window], r.probs[...]) / total
        r.heads_t[:, here] = head
        r.stats[:, here] = top + jnp.log(total)
        r.att_src[2 * block] = head[:, 0:ROWS].astype(BF)
        r.att_src[2 * block + 1] = head[:, ROWS:PAIR].astype(BF)

        @pl.when(i < CHIPS - 1)
        def _():
            att_copy(2 * block, t).start()
            att_copy(2 * block + 1, t).start()

        @pl.when(i == CHIPS - 1)
        def _():
            att_copy(at.twin, t).start()

    r.save("stats", "heads_t")
    ring_c.pass_on(1)
    r.att_t[aligned(t, HEAD), :] = r.att_src[t]
    ring_o.pass_on(6)
    ring_o.pass_on(7)
    for i in range(CHIPS):
        ring_o.second(i)

    @pl.loop(0, 4)
    def _(j):
        sides = [
            r.out_all[:, pl.ds(pl.multiple_of(core * HEAD + j * 16, 16), 16), :].astype(F32)
            for core in range(2)
        ]
        first, second = unpacked(jnp.stack(sides, axis=1).reshape(TENSOR, 16, WIDTH))
        r.out_t[aligned(2 * j, ROWS), :] = first.astype(BF)
        r.out_t[aligned(2 * j + 1, ROWS), :] = second.astype(BF)

    r.save("out_t")
    for stream in first_expert:
        stream.from_y_across()
    all_landed(r.att_t.at[pl.ds(0, 15 * HEAD)], r.a_recv.at[0], at)
    attended = r.att_t[...].astype(F32).T.astype(BF)
    r.att_rows[...] = attended
    middle = r.hid[...].astype(F32) + dot(attended, r.out_t[...], NT)
    r.mid[...] = middle
    inverse = lax.rsqrt(jnp.mean(middle * middle, axis=1, keepdims=True) + 1e-6)
    r.nm_all[aligned(t, ROWS), :] = (middle * inverse * gain_two).astype(BF)
    ring = whole_ring(at, r.nm_all, r.g_send, r.g_recv)
    ring.start()
    r.save("att_rows")
    for stream in second_expert:
        stream.start_y()
    ring_c.pass_on(2)
    ring_c.pass_on(3)
    for stream in second_expert:
        stream.from_across()
    for stream in first_expert:
        stream.finish()
    copies.wait()
    ring_h.end()
    ring_o.end()
    r.finish("normed")
    r.finish("out_t")
    r.proj_grads, r.n_first, r.gates, r.n_sums = r.hidden_all, r.normed, r.cosine, r.out_all
    r.m_sums = r.out_t


    def moe_sums(k, count=1):
        return r.m_sums.at[pl.ds(pl.multiple_of(k * ROWS, ROWS), count * ROWS)]

    halves_n = Halves(at, r.n_parts, r.n_twins, lambda k: r.n_sums.at[k], r.ntw_send, r.ntw_recv)
    halves_m = Halves(at, r.m_parts, r.m_twins, moe_sums, r.mtw_send, r.mtw_recv)
    joined = Joined(
        at,
        r.n_sums,
        r.n_crossed,
        r.n_landed,
        (r.nc_send, r.nc_recv, r.n_send, r.n_recv),
    )
    ring_w = Ring(
        at,
        lambda b: r.wqkv.at[b],
        lambda b, part: r.wqkv.at[b, pl.ds(part * HEAD, HEAD)],
        r.h_send,
        r.h_recv,
        r.wqkv_own,
        r.wqkv.at[pl.ds(0, 15)],
    )
    copies.start(r.wqkv_own, r.wqkv.at[t])

    def moe_along():
        return remote(
            moe_sums(0, 2),
            r.m_landed,
            r.m_send.at[0],
            r.m_recv.at[0],
            TP,
            at.near_core(SUM_Z[0], 0),
        )

    def gu_over_y(k):
        y = at.y_at(k)
        return remote(
            r.gus.at[0, aligned(y, PAIR), :],
            r.y_gu.at[k - 1],
            r.x_send.at[k],
            r.x_recv.at[k],
            SP,
            2 * y + at.x,
        )

    def down_over_y(e, k):
        y = at.y_at(k)
        return remote(
            r.down_grads.at[e, :, aligned(y, PAIR)],
            r.y_down.at[e, k - 1],
            r.y_send.at[4 * e + k],
            r.y_recv.at[4 * e + k],
            SP,
            2 * y + at.x,
        )

    def gate_copy(dest, src):
        return remote(
            r.gate_src.at[dest],
            r.gate_all.at[src],
            r.gg_send.at[0],
            r.gg_recv.at[0],
            TP,
            dest,
        )

    def one_pass(e):
        @pl.loop(0, CHIPS)
        def _(i):
            if e == 0:
                for k in range(2, CHIPS):

                    @pl.when(i == k - 1)
                    def _(k=k):
                        ring.pass_on(k)

                ring.second(i)

                @pl.when(i == 1)
                def _():
                    ring_c.pass_on(4)
                    ring_c.pass_on(5)

                @pl.when(i == 4)
                def _():
                    for stream in second_expert:
                        stream.from_y()

                @pl.when(i == 5)
                def _():
                    ring_c.pass_on(6)
                    ring_c.pass_on(7)

                ring_c.second(i)

                @pl.when(i == 6)
                def _():
                    ring_w.start()

            here = aligned(at.step(i) if e == 0 else at.sum_step(i), PAIR)
            nm = r.nm_all[here, :]
            place = lanes((PAIR, ROWS))
            if e == 0:
                expert = sublanes((ROWS, PAIR))
                named = expert == r.routes_t[0:1, here]
                for j in range(1, 8):
                    named = named | (expert == r.routes_t[j : j + 1, here])
                named = jnp.where(named, 1.0, 0.0).T > 0.5
                logits = jnp.where(named, dot(nm, r.small[...]), LOWEST)
                powers = jnp.exp(logits - jnp.max(logits, axis=1, keepdims=True))
                powers = jnp.where(named, powers, 0.0)
                gates = powers / jnp.sum(powers, axis=1, keepdims=True)
            else:
                kept = r.gates[here, :]
                gates = jnp.where(place == 2 * HEAD - 1, 0.0, kept)
                earlier = kept[:, 2 * HEAD - 1 : 2 * HEAD]
            mine = place == 2 * t + e
            gate = jnp.sum(jnp.where(mine, gates, 0.0), axis=1, keepdims=True)
            act_grad = dot(r.cots[here, :], r.downs[e * UNITS : (e + 1) * UNITS, :], NT)
            projected = dot(nm, r.gus[e])
            first, up = projected[:, :UNITS], projected[:, UNITS:]
            sigmoid = 1.0 / (1.0 + jnp.exp(-first))
            silu = first * sigmoid
            activated = silu * up
            gate_grad = jnp.sum(activated * act_grad, axis=1, keepdims=True)
            weighted = (activated * gate).astype(BF)
            r.weighted_t[:, here] = weighted.T
            act_grad = act_grad * gate
            r.proj_grads[here, 0:UNITS] = (
                act_grad * up * (sigmoid * (1.0 + first * (1.0 - sigmoid)))
            ).astype(BF)
            r.proj_grads[here, UNITS:WIDTH] = (act_grad * silu).astype(BF)
            normed_part = dot(r.proj_grads[here, :], r.gus[e], NT)
            if e == 0:
                r.gates[here, :] = jnp.where(place == 2 * HEAD - 1, gate_grad, gates)
                r.weighted[here, :] = weighted
                r.n_first[here, :] = normed_part.astype(BF)

                @pl.when(i == 0)
                def _():
                    ring.pass_on(1)

                return
            row = 2 * lax.rem(t, 4)
            gate_grads = jnp.where(
                place == row, earlier, jnp.where(place == row + 1, gate_grad, 0.0)
            ).T
            chip = at.sum_step(i)
            r.gate_src[2 * chip] = gate_grads[0:8, 0:ROWS]
            r.gate_src[2 * chip + 1] = gate_grads[0:8, ROWS:PAIR]

            @pl.when(i < CHIPS - 1)
            def _():
                gate_copy(2 * chip, t).start()
                gate_copy(2 * chip + 1, t).start()

            @pl.when(i == CHIPS - 1)
            def _():
                gate_copy(at.twin, t).start()

            halves_n.put(i, normed_part + r.n_first[here, :].astype(F32))
            both = jnp.concatenate([r.weighted[here, :], weighted], axis=1)
            halves_m.put(i, dot(both, r.downs[...]))

            @pl.when(i > 0)
            def _():
                halves_n.add(i - 1)
                halves_m.add(i - 1)

            for j in range(4):

                @pl.when(i == 2 * j + 1)
                def _(j=j):
                    joined.cross(j).start()

            for j in range(2):

                @pl.when(i == 2 * j + 4)
                def _(j=j):
                    joined.join(j)

            @pl.when(i == 3)
            def _():
                moe_along().start()

            for step, chips in ((0, (2, 3)), (2, (4, 5))):

                @pl.when(i == step)
                def _(chips=chips):
                    for k in chips:
                        ring_w.pass_on(k)

    def down_gradients(e):
        @pl.loop(0, 2)
        def _(j):
            strip = aligned(j, PAIR)
            r.down_grads[e, strip, :] = dot(r.weighted_t[strip, :], r.cots[...]).astype(BF)

    def gate_up_gradients(e):
        @pl.loop(0, 4)
        def _(j):
            strip = aligned(j, PAIR)
            r.gus[e, strip, :] = dot(r.nm_all[:, strip], r.proj_grads[...], TN).astype(BF)

    one_pass(0)
    for stream in second_expert:
        stream.from_y_across()
    for stream in first_expert:
        stream.end()
    down_gradients(0)
    for k in range(1, 4):
        down_over_y(0, k).start()
    gate_up_gradients(0)
    ring_w.pass_on(1)
    for k in range(1, 4):
        gu_over_y(k).start()
    for stream in second_expert:
        stream.finish()
    one_pass(1)
    joined.join(2)
    halves_n.add(CHIPS - 1)
    halves_m.add(CHIPS - 1)
    out_rows = r.n_first.at[pl.ds(0, WIDTH)]
    copies.start(r.out_t_d, out_rows)
    for stream in second_expert:
        stream.end()
    down_gradients(1)
    for k in range(1, 4):
        down_over_y(1, k).start()
    gate_up_gradients(1)
    copies.start(r.gus.at[1], r.gu_grad)
    r.gate_all[t] = r.gate_src[t]
    all_landed(r.gate_all.at[pl.ds(0, 15)], r.gg_recv.at[0], at)
    groups = r.gate_all[...].reshape(4, 4, 8, ROWS)
    gate_grads = (groups[:, 0] + groups[:, 1] + groups[:, 2] + groups[:, 3]).reshape(32, ROWS)
    gate_grads = jnp.concatenate([gate_grads, jnp.zeros((ROWS - 32, ROWS), F32)], axis=0).T
    own_rows = aligned(t, ROWS)
    gates = jnp.where(lanes((ROWS, ROWS)) < 32, r.gates[own_rows, :], 0.0)
    mean = jnp.sum(gates * gate_grads, axis=1, keepdims=True)
    logit_grad = gates * (gate_grads - mean)
    r.router_t[...] = dot(logit_grad.T.astype(BF), r.nm_all[own_rows, :])[0:32, :]
    by_router = dot(logit_grad.astype(BF), r.small[...], NT)

    gain_two = r.small[...].astype(F32).T[33:34, :]
    normed_grad = joined.result() + by_router
    middle = r.mid[...]
    inverse = lax.rsqrt(jnp.mean(middle * middle, axis=1, keepdims=True) + 1e-6)
    unit = middle * inverse
    r.gain_grad[...] = jnp.sum(normed_grad * unit, axis=0, keepdims=True)
    scaled = normed_grad * gain_two
    grad = r.cots[aligned(t, ROWS), :].astype(F32) + inverse * (
        scaled - unit * jnp.mean(scaled * unit, axis=1, keepdims=True)
    )
    r.mid_grad[...] = grad
    turned = grad.T.reshape(DP, TENSOR, 8, ROWS).transpose(1, 0, 2, 3)
    r.mid_t[...] = turned.reshape(WIDTH, ROWS).astype(BF)
    copies.wait()
    r.att_grad_t[...] = dot(grad.astype(BF), out_rows[...]).T.astype(BF)
    r.save("att_grad_t", "mid_grad", "mid_t", "gain_grad", "router_t")
    across, own = moe_sums(6)[...].astype(F32), middle + moe_sums(7)[...].astype(F32)
    moe_along().wait_recv()
    r.moe_across[...] = across + r.m_landed[0:ROWS, :].astype(F32)
    r.mid[...] = own + r.m_landed[ROWS:PAIR, :].astype(F32)
    copies.start(moe_sums(2, 4), r.moe_last)
    r.save("moe_across", "mid")
    gu = r.gus[0, aligned(at.y, PAIR), :].astype(F32)
    for k in range(1, 4):
        gu_over_y(k).wait_recv()
        gu = gu + r.y_gu[k - 1].astype(F32)
    r.ys_gu[0] = gu[0:ROWS].astype(BF)
    r.ys_gu[1] = gu[ROWS:PAIR].astype(BF)
    for e in range(2):
        down = r.down_grads[e, :, aligned(at.y, PAIR)].astype(F32)
        for k in range(1, 4):
            down_over_y(e, k).wait_recv()
            down = down + r.y_down[e, k - 1].astype(F32)
        r.ys_down[0, e] = down[:, 0:ROWS].astype(BF)
        r.ys_down[1, e] = down[:, ROWS:PAIR].astype(BF)
    r.save("ys_gu", "ys_down")
    for k in range(1, 4):
        gu_over_y(k).wait_send()
        for e in range(2):
            down_over_y(e, k).wait_send()
    ring_w.pass_on(6)
    ring_w.pass_on(7)
    all_sent(r.tiles.at[pl.ds(0, 15)], r.t1_send.at[0], at)
    all_sent(r.tile_all.at[pl.ds(0, 7)], r.t2_send.at[0], at)
    all_sent(r.row_dp.at[pl.ds(0, 7)], r.rd_send.at[0], at)
    all_sent(seven_wq, r.wq_send.at[0], at)
    all_sent(r.att_src.at[pl.ds(0, 15)], r.a_send.at[0], at)
    all_sent(r.gate_src.at[pl.ds(0, 15)], r.gg_send.at[0], at)
    ring.end()
    ring_c.end()
    moe_along().wait_send()
    for i in range(CHIPS):
        ring_w.second(i)
    ring_w.end()
    halves_n.end()
    halves_m.end()
    joined.end()
    copies.wait()
    r.end()


def back_kernel(r):
    at = Place()
    t, d = at.t, at.d
    copies = Copies(r.local)
    r.load()
    copies.start(r.gu_grad.at[aligned(at.y, PAIR), :], r.gu_own)
    r.need("att_grad_t")
    r.grads_t[0:HEAD, :] = jnp.zeros((HEAD, LENGTH), BF)
    r.grads_t[HEAD : 2 * HEAD, aligned(t, ROWS)] = r.att_grad_t[aligned(t, HEAD), :]
    at.enter()

    def back_copy(k, src):
        dest = at.tensor_at(k)
        return remote(
            r.att_grad_t.at[aligned(dest, HEAD), :],
            r.grads_t.at[pl.ds(HEAD, HEAD), aligned(src, ROWS)],
            r.g_send.at[0],
            r.g_recv.at[0],
            TP,
            dest,
        )

    def then_across():
        return (
            remote(
                r.ys_gu.at[1 - at.x], r.yx_gu0, r.x_send.at[0], r.x_recv.at[0], SP, at.across
            ),
            remote(
                r.ys_down.at[1 - at.x], r.yx_down, r.x_send.at[1], r.x_recv.at[1], SP, at.across
            ),
        )

    def over_y(k):
        y = at.y_at(k)
        return remote(
            r.gu_grad.at[aligned(y, PAIR), :],
            r.y_gu.at[k],
            r.gu_send.at[k],
            r.gu_recv.at[k],
            SP,
            2 * y + at.x,
        )

    def then_x():
        return remote(r.s_gu, r.yx_gu, r.gu_send.at[0], r.gu_recv.at[0], SP, at.across)

    def moe_along(j):
        return remote(
            r.moe_last.at[aligned(j, PAIR)],
            r.m_landed.at[j],
            r.m_send.at[j],
            r.m_recv.at[j],
            TP,
            at.near_core(SUM_Z[2 * j + 2], 0),
        )

    for k in range(1, TENSOR):
        back_copy(k, t).start()
    for j in range(2):
        moe_along(j).start()
    for k in range(1, 4):
        over_y(k).start()
    r.need("ys_gu", "ys_down")
    for copy in then_across():
        copy.start()

    r.need("mid_t", "att_rows")
    r.out_terms[...] = (
        dot(r.mid_t[...], r.att_rows[...]).reshape(CHIPS, ROWS, WIDTH).astype(BF)
    )

    def out_half():
        return remote(
            r.out_terms.at[:, aligned(1 - at.core, HEAD), :],
            r.out_twins,
            r.ot_send.at[0],
            r.ot_recv.at[0],
            TP,
            at.twin,
        )

    out_half().start()
    key_codes(r.mask, r.code)
    r.starts[...] = document_starts(r.seg[...])
    r.kv_sum[...] = jnp.zeros((PADDED, 2 * HEAD), F32)

    def out_along(k):
        return remote(
            r.out_sums.at[pl.ds(2 * lax.rem(at.z + k, 4), 2)],
            r.out_landed.at[k],
            r.o_send.at[k],
            r.o_recv.at[k],
            TP,
            at.near_core(k, 0),
        )

    def out_across():
        return remote(
            r.out_joined, r.out_crossed, r.o_send.at[0], r.o_recv.at[0], TP, at.near_core(0, 1)
        )

    def out_total(x):
        total = r.out_sums[2 * at.z + x].astype(F32)
        for k in range(1, 4):
            total = total + r.out_landed[k, x].astype(F32)
        return total


    def moe_across():
        return remote(
            r.m_joined, r.m_crossed, r.m_send.at[2], r.m_recv.at[2], TP, at.near_core(0, 1)
        )

    out_half().wait_recv()
    r.out_sums[...] = (
        r.out_terms[:, aligned(at.core, HEAD), :].astype(F32) + r.out_twins[...].astype(F32)
    ).astype(BF)
    r.need("queries", "keyvals", "keyvals_t", "stats", "heads_t", "cosine_t", "sine_t")
    all_landed(r.grads_t.at[pl.ds(HEAD, HEAD), pl.ds(0, 15 * ROWS)], r.g_recv.at[0], at)

    def query_copy(dest, src):
        return remote(
            r.query_src.at[dest],
            r.query_all.at[src],
            r.b_send.at[0],
            r.b_recv.at[0],
            TP,
            dest,
        )

    @pl.loop(0, CHIPS)
    def _(i):
        block = at.chip_at(i + 1)
        here = aligned(block, PAIR)
        query = r.queries[here, :]
        start_row = r.starts[:, here]
        stat = r.stats[:, here]
        grad_t = r.grads_t[:, here]
        grad_rows = grad_t.astype(F32).T.astype(BF)
        head = r.heads_t[:, here]
        delta = jnp.sum(head * grad_t[HEAD : 2 * HEAD, :].astype(F32), axis=0, keepdims=True)
        query_grad = jnp.zeros((HEAD, PAIR), F32)
        for chunk in range(SPAN // CHUNK):
            keys = pl.ds(pl.multiple_of(block * PAIR + chunk * CHUNK, ROWS), CHUNK)
            both = r.keyvals[keys, :]
            score = dot(both, query, NT)
            ok = allowed(r.code[keys, :], start_row, chunk)
            prob = jnp.exp(jnp.where(ok, score - stat, LOWEST))
            prob_grad = dot(both, grad_t)
            score_grad = (prob * (prob_grad - delta)).astype(BF)
            r.kv_sum[keys, :] += dot(score_grad, query) + dot(prob.astype(BF), grad_rows)
            query_grad = query_grad + dot(r.keyvals_t[0:HEAD, keys], score_grad)
        turned = turned_back(query_grad * (1.0 / math.sqrt(HEAD)), r, here).astype(BF)
        r.tail_left[0:HEAD, here] = turned
        r.query_src[2 * block] = turned[:, 0:ROWS]
        r.query_src[2 * block + 1] = turned[:, ROWS:PAIR]

        @pl.when(i < CHIPS - 1)
        def _():
            query_copy(2 * block, t).start()
            query_copy(2 * block + 1, t).start()

        @pl.when(i == CHIPS - 1)
        def _():
            query_copy(at.twin, t).start()

    @pl.loop(0, CHIPS)
    def _(i):
        here = aligned(i, PAIR)
        grad = r.kv_sum[pl.ds(pl.multiple_of(REACH + i * PAIR, ROWS), PAIR), :].T
        grad = jnp.concatenate(
            [turned_back(grad[0:HEAD], r, here), grad[HEAD : 2 * HEAD]], axis=0
        ).astype(BF)
        r.tail_left[HEAD : 3 * HEAD, here] = grad
        r.back_src[2 * i] = grad[:, 0:ROWS]
        r.back_src[2 * i + 1] = grad[:, ROWS:PAIR]

    def grad_copy(k, src):
        dest = at.tensor_at(k)
        return remote(
            r.back_src.at[dest],
            r.back_all.at[src],
            r.q_send.at[0],
            r.q_recv.at[0],
            TP,
            dest,
        )

    for k in range(1, TENSOR):
        grad_copy(k, t).start()
    r.back_all[t] = r.back_src[t]
    r.query_all[t] = r.query_src[t]
    for k in range(1, 4):
        out_along(k).start()
    r.need("moe_across", "moe_own")
    across = r.moe_across[...]
    for j in range(2):
        moe_along(j).wait_recv()
        across = across + r.m_landed[j, 0:ROWS].astype(F32)
    r.m_joined[...] = across.astype(BF)
    moe_across().start()

    copies.wait()
    r.need("normed")
    r.tail[0 : 3 * HEAD, :] = dot(r.tail_left[...], r.normed[...]).astype(BF)

    r.need("wqkv")

    @pl.loop(0, 4)
    def _(j):
        rows = pl.ds(pl.multiple_of(HEAD + j * 16, 16), 16)
        first, second = unpacked(r.wqkv[:, rows, :].astype(F32))
        r.kv_full[aligned(2 * j, ROWS), :] = first.astype(BF)
        r.kv_full[aligned(2 * j + 1, ROWS), :] = second.astype(BF)

    all_landed(r.query_all.at[pl.ds(0, 15)], r.b_recv.at[0], at)
    all_landed(r.back_all.at[pl.ds(0, 15)], r.q_recv.at[0], at)
    r.need("hid", "small", "mid_grad", "router_t", "gain_grad")
    query_rows = r.query_all[...].astype(F32).reshape(WIDTH, ROWS).T.astype(BF)
    pairs = r.back_all[...].astype(F32).reshape(CHIPS, 2, ROWS, ROWS)
    kv_rows = (pairs[:, 0] + pairs[:, 1]).reshape(WIDTH, ROWS).T.astype(BF)
    wq_full = r.wqkv[:, 0:HEAD, :].reshape(WIDTH, WIDTH)
    normed_grad = dot(query_rows, wq_full) + dot(kv_rows, r.kv_full[...], NT)
    hidden = r.hid[...].astype(F32)
    inverse = lax.rsqrt(jnp.mean(hidden * hidden, axis=1, keepdims=True) + 1e-6)
    unit = hidden * inverse
    gain_one = r.small[...].astype(F32).T[32:33, :]
    gain_one_grad = jnp.sum(normed_grad * unit, axis=0, keepdims=True)
    scaled = normed_grad * gain_one
    r.hidden_grad[...] = (
        r.mid_grad[...]
        + inverse * (scaled - unit * jnp.mean(scaled * unit, axis=1, keepdims=True))
    ).astype(BF)
    r.tail[3 * HEAD : 3 * HEAD + 32, :] = r.router_t[...].astype(BF)
    row = sublanes((16, WIDTH))
    r.tail[3 * HEAD + 32 : TAIL, :] = jnp.where(
        row == 0, gain_one_grad, jnp.where(row == 1, r.gain_grad[...], 0.0)
    ).astype(BF)

    def tail_copy(k):
        dest = at.dp_at(k)
        return remote(
            r.tail.at[:, aligned(dest, ROWS)],
            r.tail_in.at[k],
            r.t_send.at[0],
            r.t_recv.at[0],
            SP,
            dest,
        )

    for k in range(1, DP):
        tail_copy(k).start()

    for k in range(1, 4):
        over_y(k).wait_recv()

    def y_total(x):
        here = aligned(x, ROWS)
        gu = r.gu_own[here, :].astype(F32)
        for k in range(1, 4):
            gu = gu + r.y_gu[k, here, :].astype(F32)
        return gu

    r.s_gu[...] = y_total(1 - at.x).astype(BF)
    then_x().start()

    for k in range(1, 4):
        out_along(k).wait_recv()
    r.out_joined[...] = out_total(1 - at.x_far).astype(BF)
    out_across().start()
    moe_across().wait_recv()
    own = r.moe_own[...] + r.m_crossed[...].astype(F32)
    for j in range(2):
        own = own + r.m_landed[j, ROWS:PAIR].astype(F32)
    r.output[...] = own.astype(BF)
    r.save("output")
    out_across().wait_recv()
    r.out_rows[...] = out_total(at.x_far) + r.out_crossed[...].astype(F32)

    def out_copy(k):
        dest = at.dp_at(k)
        return remote(
            r.out_rows.at[aligned(dest, 8), :],
            r.out_in.at[k],
            r.od_send.at[0],
            r.od_recv.at[0],
            SP,
            dest,
        )

    for k in range(1, DP):
        out_copy(k).start()

    total = r.tail[:, aligned(d, ROWS)].astype(F32)
    all_landed(r.tail_in.at[pl.ds(0, 7)], r.t_recv.at[0], at)
    for k in range(1, DP):
        total = total + r.tail_in[k].astype(F32)
    r.query_out[...] = total[0:HEAD, :]
    r.save("hidden_grad", "query_out")
    turned = jnp.concatenate(
        [total[HEAD:TAIL], jnp.zeros((256 + HEAD - TAIL, ROWS), F32)], axis=0
    ).T
    for j in range(TENSOR):
        r.pieces[j] = turned[j * 8 : (j + 1) * 8, :]

    def last_copy(k, src):
        dest = at.tensor_at(k)
        return remote(
            r.pieces.at[dest], r.last.at[src], r.l_send.at[0], r.l_recv.at[0], TP, dest
        )

    for k in range(1, TENSOR):
        last_copy(k, t).start()
    r.last[t] = r.pieces[t]

    for copy in then_across():
        copy.wait_recv()
    r.gu_out[0] = r.ys_gu[at.x].astype(F32) + r.yx_gu0[...].astype(F32)
    r.down_out[...] = r.ys_down[at.x].astype(F32) + r.yx_down[...].astype(F32)
    then_x().wait_recv()
    r.gu_out[1] = y_total(at.x) + r.yx_gu[...].astype(F32)
    r.save("gu_out", "down_out")
    total = r.out_rows[aligned(d, 8), :]
    all_landed(r.out_in.at[pl.ds(0, 7)], r.od_recv.at[0], at)
    for k in range(1, DP):
        total = total + r.out_in[k]
    r.out_grad[...] = total
    all_landed(r.last.at[pl.ds(0, 15)], r.l_recv.at[0], at)
    r.kv_out[...] = jnp.concatenate(
        [r.last[2 * j, :, 0:ROWS] + r.last[2 * j + 1, :, 0:ROWS] for j in range(CHIPS)], axis=1
    )
    shared = r.last[0, :, ROWS:PAIR]
    for j in range(1, TENSOR):
        shared = shared + r.last[j, :, ROWS:PAIR]
    r.router_out[...] = shared[:, 0:32]
    wide = jnp.concatenate([shared, jnp.zeros((ROWS - 8, ROWS), F32)], axis=0).T
    r.gain_one_out[...] = wide[32:33, 0:8]
    r.gain_two_out[...] = wide[33:34, 0:8]
    r.save("out_grad", "kv_out", "router_out", "gain_one_out", "gain_two_out")

    all_sent(r.att_grad_t.at[pl.ds(0, 15 * HEAD)], r.g_send.at[0], at)
    all_sent(r.query_src.at[pl.ds(0, 15)], r.b_send.at[0], at)
    all_sent(r.back_src.at[pl.ds(0, 15)], r.q_send.at[0], at)
    all_sent(r.pieces.at[pl.ds(0, 15)], r.l_send.at[0], at)
    all_sent(r.tail_in.at[pl.ds(0, 7)], r.t_send.at[0], at)
    all_sent(r.out_in.at[pl.ds(0, 7)], r.od_send.at[0], at)
    for k in range(1, 4):
        over_y(k).wait_send()
    for copy in then_across():
        copy.wait_send()
    then_x().wait_send()
    out_half().wait_send()
    for k in range(1, 4):
        out_along(k).wait_send()
    out_across().wait_send()
    for j in range(2):
        moe_along(j).wait_send()
    moe_across().wait_send()
    r.end()


def store_kernel(r):
    copies = Copies(r.local)
    for name in STORED:
        copies.start(getattr(r, name), getattr(r, name + "_kept"))
    for name in STORED:
        copies.wait(1)
        copies.start(getattr(r, name + "_kept"), getattr(r, name + "_done"))
    copies.wait()


STORED = (
    "output",
    "hidden_grad",
    "gain_one_out",
    "query_out",
    "kv_out",
    "out_grad",
    "gain_two_out",
    "router_out",
    "gu_out",
    "down_out",
)


class Refs:
    def __init__(self, names, refs, loads=(), saves=()):
        for name, ref in zip(names, refs):
            setattr(self, name, ref)
        self.loads, self.saves, self.saved = list(loads), list(saves), []

    def copy_in(self, name):
        sem = self.load_sems.at[self.loads.index(name)]
        return pltpu.make_async_copy(getattr(self, name + "_d"), getattr(self, name), sem)

    def copy_out(self, name):
        sem = self.save_sems.at[self.saves.index(name)]
        return pltpu.make_async_copy(getattr(self, name), getattr(self, name + "_d"), sem)

    def load(self):
        for name in self.loads:
            self.copy_in(name).start()

    def need(self, *names):
        for name in names:
            self.copy_in(name).wait()

    def save(self, *names):
        for name in names:
            self.copy_out(name).start()
            self.saved.append(name)

    def finish(self, name):
        self.copy_out(name).wait()
        self.saved.remove(name)

    def end(self):
        for name in self.saved:
            self.copy_out(name).wait()


def call(kernel, number, inputs, outputs, scratch, reaches=True):
    def space(name):
        return pl.BlockSpec(memory_space=pltpu.VMEM if name.endswith("_v") else pl.ANY)

    outputs = {name: jax.ShapeDtypeStruct(shape, dtype) for name, (shape, dtype) in outputs.items()}
    loads = [name[:-2] for name in inputs if name.endswith("_d")]
    saves = [name[:-2] for name in outputs if name.endswith("_d")]
    scratch = dict(scratch)
    for name in loads:
        scratch[name] = pltpu.VMEM(inputs[name + "_d"].shape, inputs[name + "_d"].dtype)
    for name in saves:
        scratch[name] = pltpu.VMEM(outputs[name + "_d"].shape, outputs[name + "_d"].dtype)
    scratch |= sems(load_sems=max(1, len(loads)), save_sems=max(1, len(saves)))
    names = [name.removesuffix("_v") for name in (*inputs, *outputs)] + list(scratch)
    params = {"vmem_limit_bytes": VMEM_BYTES}
    if reaches:
        params |= {"collective_id": number, "has_side_effects": True}
    values = pl.pallas_call(
        lambda *refs: kernel(Refs(names, refs, loads, saves)),
        out_shape=list(outputs.values()),
        in_specs=[space(name) for name in inputs],
        out_specs=[space(name) for name in outputs],
        scratch_shapes=list(scratch.values()),
        compiler_params=pltpu.CompilerParams(**params),
        name=kernel.__name__,
    )(*inputs.values())
    return Refs([name.removesuffix("_v").removesuffix("_d") for name in outputs], values)


def sems(**counts):
    return {name: pltpu.SemaphoreType.DMA((count,)) for name, count in counts.items()}


def rope_tables():
    half = HEAD // 2
    freqs = np.exp(
        np.arange(half, dtype=np.float32) * np.float32(-2.0 * math.log(10000.0) / HEAD)
    ).astype(np.float32)
    angles = np.arange(LENGTH, dtype=np.float32)[:, None] * freqs[None, :]
    cos, sin = np.cos(angles).astype(np.float32), np.sin(angles).astype(np.float32)
    ones, zeros = np.ones((LENGTH, HEAD), np.float32), np.zeros((LENGTH, HEAD), np.float32)
    return (
        np.concatenate([cos, cos, ones], axis=1),
        np.concatenate([-sin, sin, zeros], axis=1),
        np.ascontiguousarray(cos.T),
        np.ascontiguousarray(sin.T),
    )


def body(
    hidden,
    seg_ids,
    key_mask,
    routes,
    gain_attn,
    w_query,
    w_keyval,
    w_out,
    gain_mlp,
    w_router,
    w_gate_up,
    w_down,
    cotangent,
):
    V = pltpu.VMEM
    cosine, sine, cosine_t, sine_t = rope_tables()
    hid, cot = hidden[0], cotangent[0]
    a = call(
        layer_kernel,
        1,
        dict(
            hid_v=hid,
            cot=cot,
            w_keyval_v=w_keyval,
            w_out_t_v=w_out.T,
            w_query_t_v=w_query.T,
            router_v=w_router,
            gain_one_v=gain_attn.reshape(1, 8),
            gain_two_v=gain_mlp.reshape(1, 8),
            gu=w_gate_up,
            down=w_down,
            cosine_d=cosine,
            sine_d=sine,
            mask_v=key_mask,
            seg_v=seg_ids,
            routes_t_v=routes[0].T,
        ),
        dict(
            normed_d=((LENGTH, WIDTH), BF),
            queries_d=((LENGTH, 2 * HEAD), BF),
            keyvals_d=((PADDED, 2 * HEAD), BF),
            keyvals_t_d=((2 * HEAD, PADDED), BF),
            stats_d=((1, LENGTH), F32),
            heads_t_d=((HEAD, LENGTH), F32),
            att_rows_d=((ROWS, WIDTH), BF),
            small_d=((WIDTH, ROWS), BF),
            out_t_d=((WIDTH, WIDTH), BF),
            wqkv=((TENSOR, ROWS, WIDTH), BF),
            moe_across_d=((ROWS, WIDTH), F32),
            mid_d=((ROWS, WIDTH), F32),
            moe_last=((2 * PAIR, WIDTH), BF),
            mid_grad_d=((ROWS, WIDTH), F32),
            mid_t_d=((WIDTH, ROWS), BF),
            att_grad_t_d=((WIDTH, ROWS), BF),
            gu_grad=((WIDTH, WIDTH), BF),
            ys_gu_d=((2, ROWS, WIDTH), BF),
            ys_down_d=((2, 2, UNITS, ROWS), BF),
            router_t_d=((32, WIDTH), F32),
            gain_grad_d=((1, WIDTH), F32),
        ),
        dict(
            hidden_all=V((LENGTH, WIDTH), BF),
            nm_all=V((LENGTH, WIDTH), BF),
            cots=V((LENGTH, WIDTH), BF),
            gus=V((2, WIDTH, WIDTH), BF),
            downs=V((WIDTH, WIDTH), BF),
            down_grads=V((2, UNITS, WIDTH), BF),
            weighted=V((LENGTH, UNITS), BF),
            weighted_t=V((UNITS, LENGTH), BF),
            wqkv_own=V((ROWS, WIDTH), BF),
            rows=V((16, WIDTH), BF),
            row_dp=V((DP, 16, WIDTH), BF),
            shares=V((8, ROWS), F32),
            tiles=V((TENSOR, 16, ROWS), BF),
            tile_all=V((DP, TENSOR, 16, ROWS), BF),
            out_all=V((CHIPS, ROWS, WIDTH), BF),
            wq_all=V((2 * HEAD, WIDTH), BF),
            code=V((PADDED, ROWS), F32),
            scores=V((SPAN, PAIR), F32),
            probs=V((SPAN, PAIR), BF),
            starts=V((1, LENGTH), F32),
            wqk=V((WIDTH, PAIR), BF),
            att_src=V((TENSOR, HEAD, ROWS), BF),
            att_t=V((WIDTH, ROWS), BF),
            y_gu=V((3, PAIR, WIDTH), BF),
            y_down=V((2, 3, UNITS, PAIR), BF),
            n_parts=V((SLOTS, PAIR, WIDTH), BF),
            n_twins=V((CHIPS, ROWS, WIDTH), BF),
            n_crossed=V((4, ROWS, WIDTH), BF),
            n_landed=V((3, ROWS, WIDTH), BF),
            m_parts=V((SLOTS, PAIR, WIDTH), BF),
            m_twins=V((CHIPS, ROWS, WIDTH), BF),
            m_landed=V((PAIR, WIDTH), BF),
            gate_src=V((TENSOR, 8, ROWS), F32),
            gate_all=V((TENSOR, 8, ROWS), F32),
        )
        | sems(
            h_send=1,
            h_recv=18,
            c_send=1,
            c_recv=18,
            o_send=17,
            o_recv=18,
            g_send=1,
            g_recv=18,
            t1_send=1,
            t1_recv=1,
            t2_send=1,
            t2_recv=1,
            rd_send=1,
            rd_recv=1,
            wq_send=1,
            wq_recv=1,
            e_send=4,
            e_recv=40,
            a_send=1,
            a_recv=1,
            ntw_send=SLOTS,
            ntw_recv=8,
            nc_send=4,
            nc_recv=4,
            n_send=3,
            n_recv=3,
            mtw_send=SLOTS,
            mtw_recv=8,
            m_send=1,
            m_recv=1,
            gg_send=1,
            gg_recv=1,
            x_send=4,
            x_recv=4,
            y_send=8,
            y_recv=8,
            local=12,
        ),
    )
    c = call(
        back_kernel,
        3,
        dict(
            att_grad_t_d=a.att_grad_t,
            mid_t_d=a.mid_t,
            mid_grad_d=a.mid_grad,
            moe_across_d=a.moe_across,
            moe_own_d=a.mid,
            moe_last=a.moe_last,
            wqkv_d=a.wqkv,
            gu_grad=a.gu_grad,
            ys_gu_d=a.ys_gu,
            ys_down_d=a.ys_down,
            router_t_d=a.router_t,
            gain_grad_d=a.gain_grad,
            queries_d=a.queries,
            keyvals_d=a.keyvals,
            keyvals_t_d=a.keyvals_t,
            stats_d=a.stats,
            heads_t_d=a.heads_t,
            mask_v=key_mask,
            seg_v=seg_ids,
            cosine_t_d=cosine_t,
            sine_t_d=sine_t,
            att_rows_d=a.att_rows,
            normed_d=a.normed,
            hid_d=hid,
            small_d=a.small,
        ),
        dict(
            output_d=((ROWS, WIDTH), BF),
            hidden_grad_d=((ROWS, WIDTH), BF),
            gain_one_out_d=((1, 8), F32),
            query_out_d=((HEAD, ROWS), F32),
            kv_out_d=((8, WIDTH), F32),
            out_grad_d=((8, WIDTH), F32),
            gain_two_out_d=((1, 8), F32),
            router_out_d=((8, 32), F32),
            gu_out_d=((2, ROWS, WIDTH), F32),
            down_out_d=((2, UNITS, ROWS), F32),
        ),
        dict(
            gu_own=V((PAIR, WIDTH), BF),
            grads_t=V((2 * HEAD, LENGTH), BF),
            kv_full=V((WIDTH, WIDTH), BF),
            code=V((PADDED, ROWS), F32),
            starts=V((1, LENGTH), F32),
            kv_sum=V((PADDED, 2 * HEAD), F32),
            tail_left=V((3 * HEAD, LENGTH), BF),
            query_src=V((TENSOR, HEAD, ROWS), BF),
            query_all=V((TENSOR, HEAD, ROWS), BF),
            back_src=V((TENSOR, ROWS, ROWS), BF),
            back_all=V((TENSOR, ROWS, ROWS), BF),
            out_terms=V((CHIPS, ROWS, WIDTH), BF),
            out_twins=V((CHIPS, HEAD, WIDTH), BF),
            out_sums=V((CHIPS, HEAD, WIDTH), BF),
            out_landed=V((4, 2, HEAD, WIDTH), BF),
            out_joined=V((HEAD, WIDTH), BF),
            out_crossed=V((HEAD, WIDTH), BF),
            out_rows=V((HEAD, WIDTH), F32),
            out_in=V((DP, 8, WIDTH), F32),
            m_landed=V((2, PAIR, WIDTH), BF),
            m_joined=V((ROWS, WIDTH), BF),
            m_crossed=V((ROWS, WIDTH), BF),
            tail=V((TAIL, WIDTH), BF),
            tail_in=V((DP, TAIL, ROWS), BF),
            pieces=V((TENSOR, 8, PAIR), F32),
            last=V((TENSOR, 8, PAIR), F32),
            yx_gu0=V((ROWS, WIDTH), BF),
            y_gu=V((4, PAIR, WIDTH), BF),
            s_gu=V((ROWS, WIDTH), BF),
            yx_gu=V((ROWS, WIDTH), BF),
            yx_down=V((2, UNITS, ROWS), BF),
        )
        | sems(
            g_send=1,
            g_recv=1,
            q_send=1,
            q_recv=1,
            b_send=1,
            b_recv=1,
            x_send=4,
            x_recv=4,
            gu_send=4,
            gu_recv=4,
            ot_send=1,
            ot_recv=1,
            o_send=8,
            o_recv=8,
            m_send=3,
            m_recv=3,
            t_send=1,
            t_recv=1,
            od_send=1,
            od_recv=1,
            l_send=1,
            l_recv=1,
            local=8,
        ),
    )
    values = {name: getattr(c, name) for name in STORED}
    done = call(
        store_kernel,
        0,
        values,
        {name + "_done": (value.shape, value.dtype) for name, value in values.items()},
        {name + "_kept": V(value.shape, value.dtype) for name, value in values.items()}
        | sems(local=2 * len(STORED)),
        reaches=False,
    )
    return (
        done.output_done[None],
        done.hidden_grad_done[None],
        done.gain_one_out_done.reshape(8),
        done.query_out_done.T,
        done.kv_out_done,
        done.out_grad_done.T,
        done.gain_two_out_done.reshape(8),
        done.router_out_done,
        done.gu_out_done,
        done.down_out_done,
    )


def solution(mesh):
    return jax.shard_map(
        body,
        mesh=mesh,
        in_specs=(
            P("dp", "tensor", None),
            P("dp", None),
            P("dp", None),
            P("dp", None, None),
            P(("dp", "tensor")),
            P("dp", "tensor"),
            P(("dp", "tensor"), None),
            P(None, ("dp", "tensor")),
            P(("dp", "tensor")),
            P(("dp", "tensor"), None),
            P("tensor", "dp", None),
            P("tensor", None, "dp"),
            P("dp", "tensor", None),
        ),
        out_specs=(
            P("dp", "tensor", None),
            P("dp", "tensor", None),
            P(("dp", "tensor")),
            P("dp", "tensor"),
            P(("dp", "tensor"), None),
            P(None, ("dp", "tensor")),
            P(("dp", "tensor")),
            P(("dp", "tensor"), None),
            P("tensor", "dp", None),
            P("tensor", None, "dp"),
        ),
        check_vma=False,
    )
```

time: 261 us -> 207 us (0.79)
  Pallas kernels: 260 us -> 206 us
    pallas_call x4 -> x3, Pallas kernels: 260 us -> 206 us  [call(): pl.pallas_call(lambda *refs: kernel(Refs(names, refs, loads, saves)), out...]
where the time goes in v3:
time: 207 us
  Pallas kernels  206 us (100%)
    pallas_call x3, Pallas kernels, call(): pl.pallas_call(lambda *refs: kernel(Refs(names, refs, loads, saves)), out...  206 us

profile of v3, /device:TPU:1, one launch (start us, length us, event | category | flops | bytes accessed | tf_op | source)
XLA Modules:
  0.0 206.5 jit_solution(5462433198500434638)
XLA Ops:
  0.6 144.9 %layer_kernel.1 = (bf16[2048,1024]{1,0:T(8,128)(2,1)}, bf16[2048,128]{1,0:T(8,128)(2,1)}, bf16[2944,128]{1,0:T(8,128)(2,1)}, bf16[128,2944]{1,0:T(8,128)(2,1)}, ...) custom-call(bf16[128,1024]{1,0:T(8,128)(2,1)} %bitcast.15, ...), custom_call_target="tpu_custom_call" | custom-call | tf_op jit(solution)/shard_map/layer_kernel/pallas_call | solution.py:1520
  145.6 58.0 %back_kernel.1 = (bf16[128,1024]{1,0:T(8,128)(2,1)}, bf16[128,1024]{1,0:T(8,128)(2,1)}, f32[1,8]{1,0:T(1,128)}, f32[64,128]{1,0:T(8,128)}, f32[8,1024]{1,0:T(8,1...) custom-call(bf16[1024,128]{1,0:T(8,128)(2,1)} %get-tuple-element.50., ...), custom_call_target="tpu_custom_call" | custom-call | tf_op jit(solution)/shard_map/back_kernel/pallas_call | solution.py:1520
  203.6 2.8 %store_kernel.1 = (bf16[128,1024]{1,0:T(8,128)(2,1)}, bf16[128,1024]{1,0:T(8,128)(2,1)}, f32[1,8]{1,0:T(1,128)}, f32[64,128]{1,0:T(8,128)}, f32[8,1024]{1,0:T(8,...) custom-call(bf16[128,1024]{1,0:T(8,128)(2,1)} %get-tuple-element.70., ...), custom_call_target="tpu_custom_call" | custom-call | tf_op jit(solution)/shard_map/store_kernel/pallas_call | solution.py:1520

commit v4 on v3

--- a/solution.py
+++ b/solution.py
@@ -173,14 +173,13 @@
 
 
 class Ring:
-    SENDS = 17
-
-    def __init__(self, place, block, half, send, recv, source=None, most=None):
+    def __init__(self, place, block, half, send, recv, most, source=None, source_half=None):
         self.place, self.block, self.half = place, block, half
-        self.send, self.recv, self.source, self.most = send, recv, source, most
+        self.send, self.recv, self.most = send, recv, most
+        self.source, self.source_half = source, source_half
 
     def send_sem(self, number):
-        return self.send.at[number if self.most is None else 0]
+        return self.send.at[0]
 
     def copy(self, number, index, dest, source=None):
         src = self.block(index) if source is None else source
@@ -188,10 +187,17 @@
             src, self.block(index), self.send_sem(number), self.recv.at[index], TP, dest
         )
 
-    def piece(self, number, index, part, dest):
+    def piece(self, number, index, part, dest, source=None):
         ref = self.half(index, part)
-        place = TENSOR + lax.rem(index // 2, 2) if part else index
-        return remote(ref, ref, self.send_sem(number), self.recv.at[place], TP, dest)
+        place = TENSOR + index // 2 if part else index
+        return remote(
+            ref if source is None else source,
+            ref,
+            self.send_sem(number),
+            self.recv.at[place],
+            TP,
+            dest,
+        )
 
     def sent(self, number):
         at = self.place
@@ -208,18 +214,38 @@
         return self.copy(number, at.step_core(number - 9), at.twin)
 
     def start(self):
-        for number in (1, 2, 3, 0):
+        at = self.place
+        for part in range(2):
+            src = None if self.source_half is None else self.source_half(part)
+            self.piece(1, at.t, part, at.step_core(1), src).start()
+        for number in (2, 3, 0):
             self.sent(number).start()
 
+    def piece_arrived(self, index, part):
+        self.piece(0, index, part, self.place.twin).wait_recv()
+
     def pass_on(self, i):
-        index = self.place.step_core(i)
-        if i < 6:
-            self.copy(0, index, self.place.twin).wait_recv()
+        at = self.place
+        index = at.step_core(i)
+        if i in (2, 3):
+            self.copy(0, index, at.twin).wait_recv()
+            self.sent(8 if i == 2 else 6).start()
+        elif i == 1:
+            for part in range(2):
+                self.piece_arrived(index, part)
+                self.piece(4, index, part, at.step_core(2)).start()
+                self.piece(5, index, part, at.step_core(3)).start()
+        elif i == 4:
+            self.piece_arrived(index, 1)
+            self.sent(9).start()
+            self.piece_arrived(index, 0)
+        elif i == 5:
+            self.piece_arrived(index, 0)
+            self.sent(7).start()
+            self.piece_arrived(index, 1)
         else:
-            self.piece(0, index, 0, self.place.twin).wait_recv()
-            self.piece(0, index, 1, self.place.twin).wait_recv()
-        for number in {1: (4, 5), 2: (8,), 3: (6,), 4: (9,), 5: (7,)}.get(i, ()):
-            self.sent(number).start()
+            self.piece_arrived(index, 0)
+            self.piece_arrived(index, 1)
         self.sent(9 + i).start()
 
     def pass_on_at(self, i):
@@ -233,11 +259,7 @@
         self.copy(0, 2 * self.place.step(i) + 1 - self.place.core, self.place.twin).wait_recv()
 
     def end(self):
-        if self.most is not None:
-            all_sent(self.most, self.send.at[0], self.place)
-            return
-        for number in range(self.SENDS):
-            self.sent(number).wait_send()
+        all_sent(self.most, self.send.at[0], self.place)
 
 
 def whole_ring(place, ref, send, recv, source=None):
@@ -247,25 +269,33 @@
         lambda b, part: ref.at[pl.ds(pl.multiple_of(b * ROWS + part * HEAD, HEAD), HEAD)],
         send,
         recv,
+        ref.at[pl.ds(0, 15 * ROWS)],
         source,
-        ref.at[pl.ds(0, 15 * ROWS)],
+        None if source is None else lambda part: source.at[pl.ds(part * HEAD, HEAD)],
     )
 
 
 class Copies:
     def __init__(self, sems):
-        self.sems, self.all, self.done = sems, [], 0
+        self.sems, self.pending, self.used = sems, [], 0
 
     def start(self, src, dst):
-        copy = pltpu.make_async_copy(src, dst, self.sems.at[len(self.all)])
+        copy = pltpu.make_async_copy(src, dst, self.sems.at[self.used])
         copy.start()
-        self.all.append(copy)
+        self.used += 1
+        self.pending.append(copy)
+        return copy
 
     def wait(self, count=None):
-        end = len(self.all) if count is None else self.done + count
-        for copy in self.all[self.done : end]:
+        count = len(self.pending) if count is None else count
+        for copy in self.pending[:count]:
             copy.wait()
-        self.done = end
+        self.pending = self.pending[count:]
+
+    def need(self, *copies):
+        for copy in copies:
+            copy.wait()
+            self.pending = [other for other in self.pending if other is not copy]
 
 
 def lanes(shape):
@@ -321,17 +351,17 @@
 
 
 class Halves:
-    def __init__(self, place, parts, twins, sums, send, recv):
+    def __init__(self, place, parts, twins, sums, send, recv, credit):
         self.place, self.parts, self.twins, self.sums = place, parts, twins, sums
-        self.send, self.recv = send, recv
+        self.send, self.recv, self.credit = send, recv, credit
 
     def half(self, k):
-        at = self.place
-        return remote(
-            self.parts.at[lax.rem(k, SLOTS), aligned(1 - at.core, ROWS), :],
-            self.twins.at[k],
-            self.send.at[lax.rem(k, SLOTS)],
-            self.recv.at[k],
+        at, slot = self.place, lax.rem(k, SLOTS)
+        return remote(
+            self.parts.at[slot, aligned(1 - at.core, ROWS), :],
+            self.twins.at[slot],
+            self.send.at[slot],
+            self.recv.at[slot],
             TP,
             at.twin,
         )
@@ -340,14 +370,22 @@
         @pl.when(k >= SLOTS)
         def _():
             self.half(k - SLOTS).wait_send()
+            pl.semaphore_wait(self.credit, 1)
 
         self.parts[lax.rem(k, SLOTS)] = value.astype(BF)
         self.half(k).start()
 
     def add(self, k):
+        slot = lax.rem(k, SLOTS)
         self.half(k).wait_recv()
-        own = self.parts[lax.rem(k, SLOTS), aligned(self.place.core, ROWS), :].astype(F32)
-        self.sums(k)[...] = (own + self.twins[k].astype(F32)).astype(BF)
+        own = self.parts[slot, aligned(self.place.core, ROWS), :].astype(F32)
+        self.sums(k)[...] = (own + self.twins[slot].astype(F32)).astype(BF)
+
+        @pl.when(k < CHIPS - SLOTS)
+        def _():
+            pl.semaphore_signal(
+                self.credit, inc=1, device_id={TP: self.place.twin}, device_id_type=MESH
+            )
 
     def end(self):
         for k in range(CHIPS - SLOTS, CHIPS):
@@ -610,13 +648,14 @@
     columns = r.small[...].astype(F32).T
     gain_one = columns[32:33, :]
     gain_two = columns[33:34, :]
-    r.need("cosine", "sine")
+    r.need("turns")
     ring_o = Ring(
         at,
         lambda b: r.out_all.at[b // 2, aligned(lax.rem(b, 2), HEAD)],
         lambda b, part: r.out_all.at[b // 2, aligned(2 * lax.rem(b, 2) + part, 32)],
         r.o_send,
         r.o_recv,
+        r.nm_all.at[pl.ds(0, 15 * HEAD)],
     )
 
     ring_c = whole_ring(at, r.cots, r.c_send, r.c_recv, r.cot)
@@ -654,7 +693,10 @@
         inverse = lax.rsqrt(jnp.mean(hidden * hidden, axis=1, keepdims=True) + 1e-6)
         unit = (hidden * inverse * gain_one).astype(BF)
         r.normed[here, :] = unit
-        cos, sin = r.cosine[here, :], r.sine[here, :]
+        table = r.turns[here, :]
+        turned = lanes(table.shape) < HEAD
+        cos = jnp.where(turned, table, 1.0)
+        sin = jnp.where(turned, pltpu.roll(table, HEAD, 1), 0.0)
         projected = dot(unit, r.wqk[...])
         query, keyval = projected[:, 0:ROWS], projected[:, ROWS:PAIR]
         query = (query * cos + swapped(query) * sin).astype(BF)
@@ -664,14 +706,8 @@
         r.keyvals[later, :] = keyval.astype(BF)
         r.keyvals_t[:, later] = keyval.T.astype(BF)
 
-    r.save("normed", "queries", "keyvals", "keyvals_t", "small")
+    r.save("normed")
     ring_o.pass_on(1)
-    for stream in first_expert:
-        stream.from_across()
-    for stream in first_expert:
-        stream.from_y()
-    for stream in second_expert:
-        stream.start_x()
 
     def att_copy(dest, src):
         return remote(
@@ -694,6 +730,13 @@
             def _(ring=ring, chips=chips):
                 for k in chips:
                     ring.pass_on(k)
+
+        @pl.when(i == 2)
+        def _():
+            for stream in first_expert:
+                stream.from_across()
+            for stream in first_expert:
+                stream.from_y()
 
         block = at.chip_at(i + 1)
         here = aligned(block, PAIR)
@@ -711,9 +754,9 @@
             place = slice(chunk * CHUNK, (chunk + 1) * CHUNK)
             weight = jnp.exp(r.scores[place, :] - top)
             total = total + jnp.sum(weight, axis=0, keepdims=True)
-            r.probs[place, :] = weight.astype(BF)
+            r.weighted[place, 0:PAIR] = weight.astype(BF)
         window = pl.ds(pl.multiple_of(block * PAIR, ROWS), SPAN)
-        head = dot(r.keyvals_t[HEAD : 2 * HEAD, window], r.probs[...]) / total
+        head = dot(r.keyvals_t[HEAD : 2 * HEAD, window], r.weighted[0:SPAN, 0:PAIR]) / total
         r.heads_t[:, here] = head
         r.stats[:, here] = top + jnp.log(total)
         r.att_src[2 * block] = head[:, 0:ROWS].astype(BF)
@@ -728,8 +771,9 @@
         def _():
             att_copy(at.twin, t).start()
 
-    r.save("stats", "heads_t")
     ring_c.pass_on(1)
+    for stream in second_expert:
+        stream.start_x()
     r.att_t[aligned(t, HEAD), :] = r.att_src[t]
     ring_o.pass_on(6)
     ring_o.pass_on(7)
@@ -758,13 +802,10 @@
     r.nm_all[aligned(t, ROWS), :] = (middle * inverse * gain_two).astype(BF)
     ring = whole_ring(at, r.nm_all, r.g_send, r.g_recv)
     ring.start()
-    r.save("att_rows")
     for stream in second_expert:
         stream.start_y()
     ring_c.pass_on(2)
     ring_c.pass_on(3)
-    for stream in second_expert:
-        stream.from_across()
     for stream in first_expert:
         stream.finish()
     copies.wait()
@@ -772,15 +813,15 @@
     ring_o.end()
     r.finish("normed")
     r.finish("out_t")
-    r.proj_grads, r.n_first, r.gates, r.n_sums = r.hidden_all, r.normed, r.cosine, r.out_all
+    r.proj_grads, r.n_first, r.gates, r.n_sums = r.hidden_all, r.normed, r.turns, r.out_all
     r.m_sums = r.out_t
 
 
     def moe_sums(k, count=1):
         return r.m_sums.at[pl.ds(pl.multiple_of(k * ROWS, ROWS), count * ROWS)]
 
-    halves_n = Halves(at, r.n_parts, r.n_twins, lambda k: r.n_sums.at[k], r.ntw_send, r.ntw_recv)
-    halves_m = Halves(at, r.m_parts, r.m_twins, moe_sums, r.mtw_send, r.mtw_recv)
+    halves_n = Halves(at, r.n_parts, r.n_twins, lambda k: r.n_sums.at[k], r.ntw_send, r.ntw_recv, r.n_credit)
+    halves_m = Halves(at, r.m_parts, r.m_twins, moe_sums, r.mtw_send, r.mtw_recv, r.m_credit)
     joined = Joined(
         at,
         r.n_sums,
@@ -788,34 +829,26 @@
         r.n_landed,
         (r.nc_send, r.nc_recv, r.n_send, r.n_recv),
     )
-    ring_w = Ring(
-        at,
-        lambda b: r.wqkv.at[b],
-        lambda b, part: r.wqkv.at[b, pl.ds(part * HEAD, HEAD)],
-        r.h_send,
-        r.h_recv,
-        r.wqkv_own,
-        r.wqkv.at[pl.ds(0, 15)],
-    )
-    copies.start(r.wqkv_own, r.wqkv.at[t])
-
-    def moe_along():
-        return remote(
-            moe_sums(0, 2),
-            r.m_landed,
-            r.m_send.at[0],
-            r.m_recv.at[0],
+    ring_w = whole_ring(at, r.wqkv, r.h_send, r.h_recv, r.wqkv_own)
+    copies.start(r.wqkv_own, r.wqkv.at[aligned(t, ROWS)])
+
+    def moe_along(j):
+        return remote(
+            moe_sums(2 * j, 2),
+            r.m_landed.at[j],
+            r.m_send.at[j],
+            r.m_recv.at[j],
             TP,
-            at.near_core(SUM_Z[0], 0),
-        )
-
-    def gu_over_y(k):
+            at.near_core(SUM_Z[2 * j], 0),
+        )
+
+    def gu_over_y(e, k):
         y = at.y_at(k)
         return remote(
-            r.gus.at[0, aligned(y, PAIR), :],
-            r.y_gu.at[k - 1],
-            r.x_send.at[k],
-            r.x_recv.at[k],
+            r.gus.at[e, aligned(y, PAIR), :],
+            r.y_gu.at[e, k - 1],
+            r.x_send.at[4 * e + k],
+            r.x_recv.at[4 * e + k],
             SP,
             2 * y + at.x,
         )
@@ -831,6 +864,15 @@
             2 * y + at.x,
         )
 
+    def across_x(number, src, dst):
+        return remote(src, dst, r.tx_send.at[number], r.tx_recv.at[number], SP, at.across)
+
+    def gu_across(e):
+        return across_x(e, r.ys_gu.at[e, 1 - at.x], r.yx_gu.at[e])
+
+    def down_across(e):
+        return across_x(2 + e, r.ys_down.at[e, 1 - at.x], r.yx_down.at[e])
+
     def gate_copy(dest, src):
         return remote(
             r.gate_src.at[dest],
@@ -857,6 +899,11 @@
                 def _():
                     ring_c.pass_on(4)
                     ring_c.pass_on(5)
+
+                @pl.when(i == 2)
+                def _():
+                    for stream in second_expert:
+                        stream.from_across()
 
                 @pl.when(i == 4)
                 def _():
@@ -956,9 +1003,9 @@
                 def _(j=j):
                     joined.join(j)
 
-            @pl.when(i == 3)
+            @pl.when(i == 2)
             def _():
-                moe_along().start()
+                moe_along(0).start()
 
             for step, chips in ((0, (2, 3)), (2, (4, 5))):
 
@@ -990,7 +1037,7 @@
     gate_up_gradients(0)
     ring_w.pass_on(1)
     for k in range(1, 4):
-        gu_over_y(k).start()
+        gu_over_y(0, k).start()
     for stream in second_expert:
         stream.finish()
     one_pass(1)
@@ -1005,7 +1052,8 @@
     for k in range(1, 4):
         down_over_y(1, k).start()
     gate_up_gradients(1)
-    copies.start(r.gus.at[1], r.gu_grad)
+    for k in range(1, 4):
+        gu_over_y(1, k).start()
     r.gate_all[t] = r.gate_src[t]
     all_landed(r.gate_all.at[pl.ds(0, 15)], r.gg_recv.at[0], at)
     groups = r.gate_all[...].reshape(4, 4, 8, ROWS)
@@ -1030,129 +1078,44 @@
     )
     r.mid_grad[...] = grad
     turned = grad.T.reshape(DP, TENSOR, 8, ROWS).transpose(1, 0, 2, 3)
+    r.att_grad_t, r.mid_t = r.att_t, r.wqk.at[:, pl.ds(0, ROWS)]
     r.mid_t[...] = turned.reshape(WIDTH, ROWS).astype(BF)
     copies.wait()
     r.att_grad_t[...] = dot(grad.astype(BF), out_rows[...]).T.astype(BF)
-    r.save("att_grad_t", "mid_grad", "mid_t", "gain_grad", "router_t")
-    across, own = moe_sums(6)[...].astype(F32), middle + moe_sums(7)[...].astype(F32)
-    moe_along().wait_recv()
-    r.moe_across[...] = across + r.m_landed[0:ROWS, :].astype(F32)
-    r.mid[...] = own + r.m_landed[ROWS:PAIR, :].astype(F32)
-    copies.start(moe_sums(2, 4), r.moe_last)
-    r.save("moe_across", "mid")
-    gu = r.gus[0, aligned(at.y, PAIR), :].astype(F32)
-    for k in range(1, 4):
-        gu_over_y(k).wait_recv()
-        gu = gu + r.y_gu[k - 1].astype(F32)
-    r.ys_gu[0] = gu[0:ROWS].astype(BF)
-    r.ys_gu[1] = gu[ROWS:PAIR].astype(BF)
-    for e in range(2):
-        down = r.down_grads[e, :, aligned(at.y, PAIR)].astype(F32)
-        for k in range(1, 4):
-            down_over_y(e, k).wait_recv()
-            down = down + r.y_down[e, k - 1].astype(F32)
-        r.ys_down[0, e] = down[:, 0:ROWS].astype(BF)
-        r.ys_down[1, e] = down[:, ROWS:PAIR].astype(BF)
-    r.save("ys_gu", "ys_down")
-    for k in range(1, 4):
-        gu_over_y(k).wait_send()
-        for e in range(2):
-            down_over_y(e, k).wait_send()
-    ring_w.pass_on(6)
-    ring_w.pass_on(7)
-    all_sent(r.tiles.at[pl.ds(0, 15)], r.t1_send.at[0], at)
-    all_sent(r.tile_all.at[pl.ds(0, 7)], r.t2_send.at[0], at)
-    all_sent(r.row_dp.at[pl.ds(0, 7)], r.rd_send.at[0], at)
-    all_sent(seven_wq, r.wq_send.at[0], at)
-    all_sent(r.att_src.at[pl.ds(0, 15)], r.a_send.at[0], at)
-    all_sent(r.gate_src.at[pl.ds(0, 15)], r.gg_send.at[0], at)
-    ring.end()
-    ring_c.end()
-    moe_along().wait_send()
+
+    def back_copy(k, src):
+        dest = at.tensor_at(k)
+        return remote(
+            r.att_grad_t.at[aligned(dest, HEAD), :],
+            r.grads.at[:, aligned(src, ROWS)],
+            r.b_send.at[0],
+            r.b_recv.at[0],
+            TP,
+            dest,
+        )
+
+    for k in range(1, TENSOR):
+        back_copy(k, t).start()
+    own_grads = copies.start(
+        r.att_grad_t.at[aligned(t, HEAD), :], r.grads.at[:, aligned(t, ROWS)]
+    )
+    moe_along(1).start()
+    moe_along(2).start()
+    normed_load = copies.start(r.normed_d, r.normed)
+    for number in (6, 7):
+        ring_w.pass_on(number)
     for i in range(CHIPS):
         ring_w.second(i)
-    ring_w.end()
-    halves_n.end()
-    halves_m.end()
+    ring_c.end()
+    weights_load = copies.start(r.wqkv, r.cots)
     joined.end()
-    copies.wait()
-    r.end()
-
-
-def back_kernel(r):
-    at = Place()
-    t, d = at.t, at.d
-    copies = Copies(r.local)
-    r.load()
-    copies.start(r.gu_grad.at[aligned(at.y, PAIR), :], r.gu_own)
-    r.need("att_grad_t")
-    r.grads_t[0:HEAD, :] = jnp.zeros((HEAD, LENGTH), BF)
-    r.grads_t[HEAD : 2 * HEAD, aligned(t, ROWS)] = r.att_grad_t[aligned(t, HEAD), :]
-    at.enter()
-
-    def back_copy(k, src):
-        dest = at.tensor_at(k)
-        return remote(
-            r.att_grad_t.at[aligned(dest, HEAD), :],
-            r.grads_t.at[pl.ds(HEAD, HEAD), aligned(src, ROWS)],
-            r.g_send.at[0],
-            r.g_recv.at[0],
-            TP,
-            dest,
-        )
-
-    def then_across():
-        return (
-            remote(
-                r.ys_gu.at[1 - at.x], r.yx_gu0, r.x_send.at[0], r.x_recv.at[0], SP, at.across
-            ),
-            remote(
-                r.ys_down.at[1 - at.x], r.yx_down, r.x_send.at[1], r.x_recv.at[1], SP, at.across
-            ),
-        )
-
-    def over_y(k):
-        y = at.y_at(k)
-        return remote(
-            r.gu_grad.at[aligned(y, PAIR), :],
-            r.y_gu.at[k],
-            r.gu_send.at[k],
-            r.gu_recv.at[k],
-            SP,
-            2 * y + at.x,
-        )
-
-    def then_x():
-        return remote(r.s_gu, r.yx_gu, r.gu_send.at[0], r.gu_recv.at[0], SP, at.across)
-
-    def moe_along(j):
-        return remote(
-            r.moe_last.at[aligned(j, PAIR)],
-            r.m_landed.at[j],
-            r.m_send.at[j],
-            r.m_recv.at[j],
-            TP,
-            at.near_core(SUM_Z[2 * j + 2], 0),
-        )
-
-    for k in range(1, TENSOR):
-        back_copy(k, t).start()
-    for j in range(2):
-        moe_along(j).start()
-    for k in range(1, 4):
-        over_y(k).start()
-    r.need("ys_gu", "ys_down")
-    for copy in then_across():
-        copy.start()
-
-    r.need("mid_t", "att_rows")
-    r.out_terms[...] = (
+    r.n_sums[...] = (
         dot(r.mid_t[...], r.att_rows[...]).reshape(CHIPS, ROWS, WIDTH).astype(BF)
     )
 
     def out_half():
         return remote(
-            r.out_terms.at[:, aligned(1 - at.core, HEAD), :],
+            r.n_sums.at[:, aligned(1 - at.core, HEAD), :],
             r.out_twins,
             r.ot_send.at[0],
             r.ot_recv.at[0],
@@ -1161,50 +1124,80 @@
         )
 
     out_half().start()
-    key_codes(r.mask, r.code)
-    r.starts[...] = document_starts(r.seg[...])
-    r.kv_sum[...] = jnp.zeros((PADDED, 2 * HEAD), F32)
+    r.kv_sum, r.query_src = r.gates, r.att_src
+    r.tail_left, r.grads_t = r.weighted_t.at[pl.ds(PAIR, 3 * HEAD)], r.weighted_t
+    r.kv_sum[...] = jnp.zeros((LENGTH, 2 * HEAD), F32)
+    r.grads_t[0:HEAD, :] = jnp.zeros((HEAD, LENGTH), BF)
+    all_sent(r.att_src.at[pl.ds(0, 15)], r.a_send.at[0], at)
+    halves_n.end()
+    halves_m.end()
+    r.tail = r.n_parts.at[0]
+    r.s_gu, r.m_joined = r.m_parts.at[0, pl.ds(0, ROWS)], r.m_parts.at[0, pl.ds(ROWS, ROWS)]
+
+    def gu_sums(e):
+        places = [r.proj_grads.at[pl.ds((3 * e + k) * PAIR, PAIR)] for k in range(3)]
+        loads = []
+        for k in range(3):
+            gu_over_y(e, k + 1).wait_recv()
+            loads.append(copies.start(r.y_gu.at[e, k], places[k]))
+        copies.need(*loads)
+        total = r.gus[e, aligned(at.y, PAIR), :].astype(F32)
+        for place in places:
+            total = total + place[...].astype(F32)
+        r.ys_gu[e, 0] = total[0:ROWS].astype(BF)
+        r.ys_gu[e, 1] = total[ROWS:PAIR].astype(BF)
+        gu_across(e).start()
+
+    def down_sums(e):
+        places = [
+            r.weighted.at[pl.ds(k * UNITS, UNITS), pl.ds(e * PAIR, PAIR)] for k in range(3)
+        ]
+        loads = []
+        for k in range(3):
+            down_over_y(e, k + 1).wait_recv()
+            loads.append(copies.start(r.y_down.at[e, k], places[k]))
+        copies.need(*loads)
+        total = r.down_grads[e, :, aligned(at.y, PAIR)].astype(F32)
+        for place in places:
+            total = total + place[...].astype(F32)
+        r.ys_down[e, 0] = total[:, 0:ROWS].astype(BF)
+        r.ys_down[e, 1] = total[:, ROWS:PAIR].astype(BF)
+        down_across(e).start()
+
+    down_sums(0)
+    gu_sums(0)
 
     def out_along(k):
         return remote(
-            r.out_sums.at[pl.ds(2 * lax.rem(at.z + k, 4), 2)],
-            r.out_landed.at[k],
-            r.o_send.at[k],
-            r.o_recv.at[k],
+            r.out_twins.at[pl.ds(2 * lax.rem(at.z + k, 4), 2)],
+            r.out_landed.at[k - 1],
+            r.oz_send.at[k],
+            r.oz_recv.at[k],
             TP,
             at.near_core(k, 0),
         )
 
     def out_across():
         return remote(
-            r.out_joined, r.out_crossed, r.o_send.at[0], r.o_recv.at[0], TP, at.near_core(0, 1)
-        )
-
-    def out_total(x):
-        total = r.out_sums[2 * at.z + x].astype(F32)
-        for k in range(1, 4):
-            total = total + r.out_landed[k, x].astype(F32)
-        return total
-
-
-    def moe_across():
-        return remote(
-            r.m_joined, r.m_crossed, r.m_send.at[2], r.m_recv.at[2], TP, at.near_core(0, 1)
+            r.out_joined, r.out_crossed, r.oz_send.at[0], r.oz_recv.at[0], TP, at.near_core(0, 1)
         )
 
     out_half().wait_recv()
-    r.out_sums[...] = (
-        r.out_terms[:, aligned(at.core, HEAD), :].astype(F32) + r.out_twins[...].astype(F32)
+    r.out_twins[...] = (
+        r.n_sums[:, aligned(at.core, HEAD), :].astype(F32) + r.out_twins[...].astype(F32)
     ).astype(BF)
-    r.need("queries", "keyvals", "keyvals_t", "stats", "heads_t", "cosine_t", "sine_t")
-    all_landed(r.grads_t.at[pl.ds(HEAD, HEAD), pl.ds(0, 15 * ROWS)], r.g_recv.at[0], at)
+    out_along(1).start()
+    all_landed(r.grads.at[:, pl.ds(0, 15 * ROWS)], r.b_recv.at[0], at)
+    copies.need(own_grads)
+    copies.need(copies.start(r.grads, r.grads_t.at[pl.ds(HEAD, HEAD)]))
+    r.need("cosine_t", "sine_t")
 
     def query_copy(dest, src):
         return remote(
             r.query_src.at[dest],
             r.query_all.at[src],
-            r.b_send.at[0],
-            r.b_recv.at[0],
+            r.qb_send.at[0],
+            r.qb_recv.at[0],
             TP,
             dest,
         )
@@ -1216,7 +1209,7 @@
         query = r.queries[here, :]
         start_row = r.starts[:, here]
         stat = r.stats[:, here]
-        grad_t = r.grads_t[:, here]
+        grad_t = r.grads_t[0 : 2 * HEAD, here]
         grad_rows = grad_t.astype(F32).T.astype(BF)
         head = r.heads_t[:, here]
         delta = jnp.sum(head * grad_t[HEAD : 2 * HEAD, :].astype(F32), axis=0, keepdims=True)
@@ -1229,7 +1222,12 @@
             prob = jnp.exp(jnp.where(ok, score - stat, LOWEST))
             prob_grad = dot(both, grad_t)
             score_grad = (prob * (prob_grad - delta)).astype(BF)
-            r.kv_sum[keys, :] += dot(score_grad, query) + dot(prob.astype(BF), grad_rows)
+            update = dot(score_grad, query) + dot(prob.astype(BF), grad_rows)
+            for part in range(CHUNK // ROWS):
+                row = jnp.maximum(block * PAIR + (chunk * CHUNK + part * ROWS - REACH), 0)
+                place = pl.ds(pl.multiple_of(row, ROWS), ROWS)
+                r.kv_sum[place, :] += update[part * ROWS : (part + 1) * ROWS]
+
             query_grad = query_grad + dot(r.keyvals_t[0:HEAD, keys], score_grad)
         turned = turned_back(query_grad * (1.0 / math.sqrt(HEAD)), r, here).astype(BF)
         r.tail_left[0:HEAD, here] = turned
@@ -1248,7 +1246,7 @@
     @pl.loop(0, CHIPS)
     def _(i):
         here = aligned(i, PAIR)
-        grad = r.kv_sum[pl.ds(pl.multiple_of(REACH + i * PAIR, ROWS), PAIR), :].T
+        grad = r.kv_sum[here, :].T
         grad = jnp.concatenate(
             [turned_back(grad[0:HEAD], r, here), grad[HEAD : 2 * HEAD]], axis=0
         ).astype(BF)
@@ -1261,8 +1259,8 @@
         return remote(
             r.back_src.at[dest],
             r.back_all.at[src],
-            r.q_send.at[0],
-            r.q_recv.at[0],
+            r.kb_send.at[0],
+            r.kb_recv.at[0],
             TP,
             dest,
         )
@@ -1271,37 +1269,45 @@
         grad_copy(k, t).start()
     r.back_all[t] = r.back_src[t]
     r.query_all[t] = r.query_src[t]
-    for k in range(1, 4):
+    for k in (2, 3):
         out_along(k).start()
-    r.need("moe_across", "moe_own")
-    across = r.moe_across[...]
-    for j in range(2):
+    down_sums(1)
+    across, own = moe_sums(6)[...].astype(F32), middle + moe_sums(7)[...].astype(F32)
+    for j in range(3):
         moe_along(j).wait_recv()
         across = across + r.m_landed[j, 0:ROWS].astype(F32)
+        own = own + r.m_landed[j, ROWS:PAIR].astype(F32)
     r.m_joined[...] = across.astype(BF)
+    r.mid[...] = own
+
+    def moe_across():
+        return remote(
+            r.m_joined, r.m_crossed, r.mx_send.at[0], r.mx_recv.at[0], TP, at.near_core(0, 1)
+        )
+
     moe_across().start()
-
-    copies.wait()
-    r.need("normed")
+    copies.need(normed_load)
     r.tail[0 : 3 * HEAD, :] = dot(r.tail_left[...], r.normed[...]).astype(BF)
 
-    r.need("wqkv")
-
-    @pl.loop(0, 4)
-    def _(j):
-        rows = pl.ds(pl.multiple_of(HEAD + j * 16, 16), 16)
-        first, second = unpacked(r.wqkv[:, rows, :].astype(F32))
-        r.kv_full[aligned(2 * j, ROWS), :] = first.astype(BF)
-        r.kv_full[aligned(2 * j + 1, ROWS), :] = second.astype(BF)
-
-    all_landed(r.query_all.at[pl.ds(0, 15)], r.b_recv.at[0], at)
-    all_landed(r.back_all.at[pl.ds(0, 15)], r.q_recv.at[0], at)
-    r.need("hid", "small", "mid_grad", "router_t", "gain_grad")
+    copies.need(weights_load)
+    whole = r.cots
+    for j in range(4):
+        rows = [
+            whole[i * ROWS + HEAD + j * 16 : i * ROWS + HEAD + (j + 1) * 16, :].astype(F32)
+            for i in range(TENSOR)
+        ]
+        first, second = unpacked(jnp.stack(rows, axis=0))
+        r.downs[2 * j * ROWS : (2 * j + 1) * ROWS, :] = first.astype(BF)
+        r.downs[(2 * j + 1) * ROWS : (2 * j + 2) * ROWS, :] = second.astype(BF)
+    all_landed(r.query_all.at[pl.ds(0, 15)], r.qb_recv.at[0], at)
+    all_landed(r.back_all.at[pl.ds(0, 15)], r.kb_recv.at[0], at)
     query_rows = r.query_all[...].astype(F32).reshape(WIDTH, ROWS).T.astype(BF)
     pairs = r.back_all[...].astype(F32).reshape(CHIPS, 2, ROWS, ROWS)
     kv_rows = (pairs[:, 0] + pairs[:, 1]).reshape(WIDTH, ROWS).T.astype(BF)
-    wq_full = r.wqkv[:, 0:HEAD, :].reshape(WIDTH, WIDTH)
-    normed_grad = dot(query_rows, wq_full) + dot(kv_rows, r.kv_full[...], NT)
+    wq_full = jnp.concatenate(
+        [whole[i * ROWS : i * ROWS + HEAD, :] for i in range(TENSOR)], axis=0
+    )
+    normed_grad = dot(query_rows, wq_full) + dot(kv_rows, r.downs[...], NT)
     hidden = r.hid[...].astype(F32)
     inverse = lax.rsqrt(jnp.mean(hidden * hidden, axis=1, keepdims=True) + 1e-6)
     unit = hidden * inverse
@@ -1312,6 +1318,7 @@
         r.mid_grad[...]
         + inverse * (scaled - unit * jnp.mean(scaled * unit, axis=1, keepdims=True))
     ).astype(BF)
+    r.save("hidden_grad")
     r.tail[3 * HEAD : 3 * HEAD + 32, :] = r.router_t[...].astype(BF)
     row = sublanes((16, WIDTH))
     r.tail[3 * HEAD + 32 : TAIL, :] = jnp.where(
@@ -1321,7 +1328,7 @@
     def tail_copy(k):
         dest = at.dp_at(k)
         return remote(
-            r.tail.at[:, aligned(dest, ROWS)],
+            r.tail.at[pl.ds(0, TAIL), aligned(dest, ROWS)],
             r.tail_in.at[k],
             r.t_send.at[0],
             r.t_recv.at[0],
@@ -1332,31 +1339,31 @@
     for k in range(1, DP):
         tail_copy(k).start()
 
-    for k in range(1, 4):
-        over_y(k).wait_recv()
-
-    def y_total(x):
-        here = aligned(x, ROWS)
-        gu = r.gu_own[here, :].astype(F32)
-        for k in range(1, 4):
-            gu = gu + r.y_gu[k, here, :].astype(F32)
-        return gu
-
-    r.s_gu[...] = y_total(1 - at.x).astype(BF)
-    then_x().start()
-
-    for k in range(1, 4):
-        out_along(k).wait_recv()
+    landed = [
+        [r.nm_all.at[pl.ds((2 * k + x) * HEAD, HEAD)] for x in range(2)] for k in range(3)
+    ]
+    ring.end()
+    loads = []
+    for k in range(3):
+        out_along(k + 1).wait_recv()
+        for x in range(2):
+            loads.append(copies.start(r.out_landed.at[k, x], landed[k][x]))
+    copies.need(*loads)
+
+    def out_total(x):
+        total = r.out_twins[2 * at.z + x].astype(F32)
+        for k in range(3):
+            rows = aligned(2 * k + x, HEAD)
+            total = total + r.nm_all[rows, :].astype(F32)
+        return total
+
     r.out_joined[...] = out_total(1 - at.x_far).astype(BF)
     out_across().start()
-    moe_across().wait_recv()
-    own = r.moe_own[...] + r.m_crossed[...].astype(F32)
-    for j in range(2):
-        own = own + r.m_landed[j, ROWS:PAIR].astype(F32)
-    r.output[...] = own.astype(BF)
-    r.save("output")
+    gu_sums(1)
     out_across().wait_recv()
-    r.out_rows[...] = out_total(at.x_far) + r.out_crossed[...].astype(F32)
+    crossed = r.proj_grads.at[pl.ds(6 * PAIR, HEAD)]
+    copies.need(copies.start(r.out_crossed, crossed))
+    r.out_rows[...] = out_total(at.x_far) + crossed[...].astype(F32)
 
     def out_copy(k):
         dest = at.dp_at(k)
@@ -1371,13 +1378,12 @@
 
     for k in range(1, DP):
         out_copy(k).start()
-
-    total = r.tail[:, aligned(d, ROWS)].astype(F32)
+    total = r.tail[0:TAIL, aligned(d, ROWS)].astype(F32)
     all_landed(r.tail_in.at[pl.ds(0, 7)], r.t_recv.at[0], at)
     for k in range(1, DP):
         total = total + r.tail_in[k].astype(F32)
     r.query_out[...] = total[0:HEAD, :]
-    r.save("hidden_grad", "query_out")
+    r.save("query_out")
     turned = jnp.concatenate(
         [total[HEAD:TAIL], jnp.zeros((256 + HEAD - TAIL, ROWS), F32)], axis=0
     ).T
@@ -1394,13 +1400,26 @@
         last_copy(k, t).start()
     r.last[t] = r.pieces[t]
 
-    for copy in then_across():
-        copy.wait_recv()
-    r.gu_out[0] = r.ys_gu[at.x].astype(F32) + r.yx_gu0[...].astype(F32)
-    r.down_out[...] = r.ys_down[at.x].astype(F32) + r.yx_down[...].astype(F32)
-    then_x().wait_recv()
-    r.gu_out[1] = y_total(at.x) + r.yx_gu[...].astype(F32)
-    r.save("gu_out", "down_out")
+    moe_across().wait_recv()
+    crossed = r.proj_grads.at[pl.ds(7 * PAIR, ROWS)]
+    copies.need(copies.start(r.m_crossed, crossed))
+    r.output[...] = (r.mid[...] + crossed[...].astype(F32)).astype(BF)
+    r.save("output")
+    loads, crossed = [], []
+    for e in range(2):
+        down_across(e).wait_recv()
+        crossed.append(r.weighted.at[pl.ds(3 * UNITS, UNITS), pl.ds(e * ROWS, ROWS)])
+        loads.append(copies.start(r.yx_down.at[e], crossed[-1]))
+    for e in range(2):
+        gu_across(e).wait_recv()
+        crossed.append(r.nm_all.at[pl.ds(WIDTH + e * ROWS, ROWS)])
+        loads.append(copies.start(r.yx_gu.at[e], crossed[-1]))
+    copies.need(*loads)
+    for e, total in ((0, r.mid_grad), (1, r.mid)):
+        total[...] = r.ys_gu[e, at.x].astype(F32) + crossed[2 + e][...].astype(F32)
+        copies.start(total, r.gu_out.at[e])
+        r.down_out[e] = r.ys_down[e, at.x].astype(F32) + crossed[e][...].astype(F32)
+    r.save("down_out")
     total = r.out_rows[aligned(d, 8), :]
     all_landed(r.out_in.at[pl.ds(0, 7)], r.od_recv.at[0], at)
     for k in range(1, DP):
@@ -1419,24 +1438,32 @@
     r.gain_two_out[...] = wide[33:34, 0:8]
     r.save("out_grad", "kv_out", "router_out", "gain_one_out", "gain_two_out")
 
-    all_sent(r.att_grad_t.at[pl.ds(0, 15 * HEAD)], r.g_send.at[0], at)
-    all_sent(r.query_src.at[pl.ds(0, 15)], r.b_send.at[0], at)
-    all_sent(r.back_src.at[pl.ds(0, 15)], r.q_send.at[0], at)
+    all_sent(r.tiles.at[pl.ds(0, 15)], r.t1_send.at[0], at)
+    all_sent(r.tile_all.at[pl.ds(0, 7)], r.t2_send.at[0], at)
+    all_sent(r.row_dp.at[pl.ds(0, 7)], r.rd_send.at[0], at)
+    all_sent(seven_wq, r.wq_send.at[0], at)
+    all_sent(r.gate_src.at[pl.ds(0, 15)], r.gg_send.at[0], at)
+    all_sent(r.att_grad_t.at[pl.ds(0, 15 * HEAD)], r.b_send.at[0], at)
+    all_sent(r.query_src.at[pl.ds(0, 15)], r.qb_send.at[0], at)
+    all_sent(r.back_src.at[pl.ds(0, 15)], r.kb_send.at[0], at)
     all_sent(r.pieces.at[pl.ds(0, 15)], r.l_send.at[0], at)
     all_sent(r.tail_in.at[pl.ds(0, 7)], r.t_send.at[0], at)
     all_sent(r.out_in.at[pl.ds(0, 7)], r.od_send.at[0], at)
-    for k in range(1, 4):
-        over_y(k).wait_send()
-    for copy in then_across():
-        copy.wait_send()
-    then_x().wait_send()
-    out_half().wait_send()
+    for j in range(3):
+        moe_along(j).wait_send()
+    moe_across().wait_send()
     for k in range(1, 4):
         out_along(k).wait_send()
     out_across().wait_send()
-    for j in range(2):
-        moe_along(j).wait_send()
-    moe_across().wait_send()
+    out_half().wait_send()
+    for e in range(2):
+        for k in range(1, 4):
+            gu_over_y(e, k).wait_send()
+            down_over_y(e, k).wait_send()
+        gu_across(e).wait_send()
+        down_across(e).wait_send()
+    ring_w.end()
+    copies.wait()
     r.end()
 
 
@@ -1540,10 +1567,8 @@
     ).astype(np.float32)
     angles = np.arange(LENGTH, dtype=np.float32)[:, None] * freqs[None, :]
     cos, sin = np.cos(angles).astype(np.float32), np.sin(angles).astype(np.float32)
-    ones, zeros = np.ones((LENGTH, HEAD), np.float32), np.zeros((LENGTH, HEAD), np.float32)
     return (
-        np.concatenate([cos, cos, ones], axis=1),
-        np.concatenate([-sin, sin, zeros], axis=1),
+        np.concatenate([cos, cos, -sin, sin], axis=1),
         np.ascontiguousarray(cos.T),
         np.ascontiguousarray(sin.T),
     )
@@ -1565,9 +1590,9 @@
     cotangent,
 ):
     V = pltpu.VMEM
-    cosine, sine, cosine_t, sine_t = rope_tables()
+    turns, cosine_t, sine_t = rope_tables()
     hid, cot = hidden[0], cotangent[0]
-    a = call(
+    c = call(
         layer_kernel,
         1,
         dict(
@@ -1581,34 +1606,35 @@
             gain_two_v=gain_mlp.reshape(1, 8),
             gu=w_gate_up,
             down=w_down,
-            cosine_d=cosine,
-            sine_d=sine,
+            turns_d=turns,
+            cosine_t_d=cosine_t,
+            sine_t_d=sine_t,
             mask_v=key_mask,
             seg_v=seg_ids,
             routes_t_v=routes[0].T,
         ),
         dict(
+            output_d=((ROWS, WIDTH), BF),
+            hidden_grad_d=((ROWS, WIDTH), BF),
+            gain_one_out_d=((1, 8), F32),
+            query_out_d=((HEAD, ROWS), F32),
+            kv_out_d=((8, WIDTH), F32),
+            out_grad_d=((8, WIDTH), F32),
+            gain_two_out_d=((1, 8), F32),
+            router_out_d=((8, 32), F32),
+            gu_out=((2, ROWS, WIDTH), F32),
+            down_out_d=((2, UNITS, ROWS), F32),
             normed_d=((LENGTH, WIDTH), BF),
-            queries_d=((LENGTH, 2 * HEAD), BF),
-            keyvals_d=((PADDED, 2 * HEAD), BF),
-            keyvals_t_d=((2 * HEAD, PADDED), BF),
-            stats_d=((1, LENGTH), F32),
-            heads_t_d=((HEAD, LENGTH), F32),
-            att_rows_d=((ROWS, WIDTH), BF),
-            small_d=((WIDTH, ROWS), BF),
             out_t_d=((WIDTH, WIDTH), BF),
-            wqkv=((TENSOR, ROWS, WIDTH), BF),
-            moe_across_d=((ROWS, WIDTH), F32),
-            mid_d=((ROWS, WIDTH), F32),
-            moe_last=((2 * PAIR, WIDTH), BF),
-            mid_grad_d=((ROWS, WIDTH), F32),
-            mid_t_d=((WIDTH, ROWS), BF),
-            att_grad_t_d=((WIDTH, ROWS), BF),
-            gu_grad=((WIDTH, WIDTH), BF),
-            ys_gu_d=((2, ROWS, WIDTH), BF),
-            ys_down_d=((2, 2, UNITS, ROWS), BF),
-            router_t_d=((32, WIDTH), F32),
-            gain_grad_d=((1, WIDTH), F32),
+            wqkv=((LENGTH, WIDTH), BF),
+            grads=((HEAD, LENGTH), BF),
+            y_gu=((2, 3, PAIR, WIDTH), BF),
+            y_down=((2, 3, UNITS, PAIR), BF),
+            yx_gu=((2, ROWS, WIDTH), BF),
+            yx_down=((2, UNITS, ROWS), BF),
+            out_landed=((3, 2, HEAD, WIDTH), BF),
+            out_crossed=((HEAD, WIDTH), BF),
+            m_crossed=((ROWS, WIDTH), BF),
         ),
         dict(
             hidden_all=V((LENGTH, WIDTH), BF),
@@ -1619,6 +1645,16 @@
             down_grads=V((2, UNITS, WIDTH), BF),
             weighted=V((LENGTH, UNITS), BF),
             weighted_t=V((UNITS, LENGTH), BF),
+            queries=V((LENGTH, 2 * HEAD), BF),
+            keyvals=V((PADDED, 2 * HEAD), BF),
+            keyvals_t=V((2 * HEAD, PADDED), BF),
+            stats=V((1, LENGTH), F32),
+            heads_t=V((HEAD, LENGTH), F32),
+            small=V((WIDTH, ROWS), BF),
+            mid=V((ROWS, WIDTH), F32),
+            mid_grad=V((ROWS, WIDTH), F32),
+            router_t=V((32, WIDTH), F32),
+            gain_grad=V((1, WIDTH), F32),
             wqkv_own=V((ROWS, WIDTH), BF),
             rows=V((16, WIDTH), BF),
             row_dp=V((DP, 16, WIDTH), BF),
@@ -1629,32 +1665,44 @@
             wq_all=V((2 * HEAD, WIDTH), BF),
             code=V((PADDED, ROWS), F32),
             scores=V((SPAN, PAIR), F32),
-            probs=V((SPAN, PAIR), BF),
             starts=V((1, LENGTH), F32),
             wqk=V((WIDTH, PAIR), BF),
             att_src=V((TENSOR, HEAD, ROWS), BF),
             att_t=V((WIDTH, ROWS), BF),
-            y_gu=V((3, PAIR, WIDTH), BF),
-            y_down=V((2, 3, UNITS, PAIR), BF),
+            att_rows=V((ROWS, WIDTH), BF),
+            ys_gu=V((2, 2, ROWS, WIDTH), BF),
+            ys_down=V((2, 2, UNITS, ROWS), BF),
             n_parts=V((SLOTS, PAIR, WIDTH), BF),
-            n_twins=V((CHIPS, ROWS, WIDTH), BF),
+            n_twins=V((SLOTS, ROWS, WIDTH), BF),
+            n_credit=pltpu.SemaphoreType.REGULAR,
             n_crossed=V((4, ROWS, WIDTH), BF),
             n_landed=V((3, ROWS, WIDTH), BF),
             m_parts=V((SLOTS, PAIR, WIDTH), BF),
-            m_twins=V((CHIPS, ROWS, WIDTH), BF),
-            m_landed=V((PAIR, WIDTH), BF),
+            m_twins=V((SLOTS, ROWS, WIDTH), BF),
+            m_credit=pltpu.SemaphoreType.REGULAR,
+            m_landed=V((3, PAIR, WIDTH), BF),
             gate_src=V((TENSOR, 8, ROWS), F32),
             gate_all=V((TENSOR, 8, ROWS), F32),
+            query_all=V((TENSOR, HEAD, ROWS), BF),
+            back_src=V((TENSOR, ROWS, ROWS), BF),
+            back_all=V((TENSOR, ROWS, ROWS), BF),
+            out_twins=V((CHIPS, HEAD, WIDTH), BF),
+            out_joined=V((HEAD, WIDTH), BF),
+            out_rows=V((HEAD, WIDTH), F32),
+            out_in=V((DP, 8, WIDTH), F32),
+            tail_in=V((DP, TAIL, ROWS), BF),
+            pieces=V((TENSOR, 8, PAIR), F32),
+            last=V((TENSOR, 8, PAIR), F32),
         )
         | sems(
             h_send=1,
-            h_recv=18,
+            h_recv=24,
             c_send=1,
-            c_recv=18,
-            o_send=17,
-            o_recv=18,
+            c_recv=24,
+            o_send=1,
+            o_recv=24,
             g_send=1,
-            g_recv=18,
+            g_recv=24,
             t1_send=1,
             t1_recv=1,
             t2_send=1,
@@ -1668,123 +1716,42 @@
             a_send=1,
             a_recv=1,
             ntw_send=SLOTS,
-            ntw_recv=8,
+            ntw_recv=SLOTS,
             nc_send=4,
             nc_recv=4,
             n_send=3,
             n_recv=3,
             mtw_send=SLOTS,
-            mtw_recv=8,
-            m_send=1,
-            m_recv=1,
+            mtw_recv=SLOTS,
+            m_send=3,
+            m_recv=3,
+            mx_send=1,
+            mx_recv=1,
             gg_send=1,
             gg_recv=1,
-            x_send=4,
-            x_recv=4,
+            b_send=1,
+            b_recv=1,
+            ot_send=1,
+            ot_recv=1,
+            oz_send=4,
+            oz_recv=4,
+            qb_send=1,
+            qb_recv=1,
+            kb_send=1,
+            kb_recv=1,
+            x_send=8,
+            x_recv=8,
             y_send=8,
             y_recv=8,
-            local=12,
-        ),
-    )
-    c = call(
-        back_kernel,
-        3,
-        dict(
-            att_grad_t_d=a.att_grad_t,
-            mid_t_d=a.mid_t,
-            mid_grad_d=a.mid_grad,
-            moe_across_d=a.moe_across,
-            moe_own_d=a.mid,
-            moe_last=a.moe_last,
-            wqkv_d=a.wqkv,
-            gu_grad=a.gu_grad,
-            ys_gu_d=a.ys_gu,
-            ys_down_d=a.ys_down,
-            router_t_d=a.router_t,
-            gain_grad_d=a.gain_grad,
-            queries_d=a.queries,
-            keyvals_d=a.keyvals,
-            keyvals_t_d=a.keyvals_t,
-            stats_d=a.stats,
-            heads_t_d=a.heads_t,
-            mask_v=key_mask,
-            seg_v=seg_ids,
-            cosine_t_d=cosine_t,
-            sine_t_d=sine_t,
-            att_rows_d=a.att_rows,
-            normed_d=a.normed,
-            hid_d=hid,
-            small_d=a.small,
-        ),
-        dict(
-            output_d=((ROWS, WIDTH), BF),
-            hidden_grad_d=((ROWS, WIDTH), BF),
-            gain_one_out_d=((1, 8), F32),
-            query_out_d=((HEAD, ROWS), F32),
-            kv_out_d=((8, WIDTH), F32),
-            out_grad_d=((8, WIDTH), F32),
-            gain_two_out_d=((1, 8), F32),
-            router_out_d=((8, 32), F32),
-            gu_out_d=((2, ROWS, WIDTH), F32),
-            down_out_d=((2, UNITS, ROWS), F32),
-        ),
-        dict(
-            gu_own=V((PAIR, WIDTH), BF),
-            grads_t=V((2 * HEAD, LENGTH), BF),
-            kv_full=V((WIDTH, WIDTH), BF),
-            code=V((PADDED, ROWS), F32),
-            starts=V((1, LENGTH), F32),
-            kv_sum=V((PADDED, 2 * HEAD), F32),
-            tail_left=V((3 * HEAD, LENGTH), BF),
-            query_src=V((TENSOR, HEAD, ROWS), BF),
-            query_all=V((TENSOR, HEAD, ROWS), BF),
-            back_src=V((TENSOR, ROWS, ROWS), BF),
-            back_all=V((TENSOR, ROWS, ROWS), BF),
-            out_terms=V((CHIPS, ROWS, WIDTH), BF),
-            out_twins=V((CHIPS, HEAD, WIDTH), BF),
-            out_sums=V((CHIPS, HEAD, WIDTH), BF),
-            out_landed=V((4, 2, HEAD, WIDTH), BF),
-            out_joined=V((HEAD, WIDTH), BF),
-            out_crossed=V((HEAD, WIDTH), BF),
-            out_rows=V((HEAD, WIDTH), F32),
-            out_in=V((DP, 8, WIDTH), F32),
-            m_landed=V((2, PAIR, WIDTH), BF),
-            m_joined=V((ROWS, WIDTH), BF),
-            m_crossed=V((ROWS, WIDTH), BF),
-            tail=V((TAIL, WIDTH), BF),
-            tail_in=V((DP, TAIL, ROWS), BF),
-            pieces=V((TENSOR, 8, PAIR), F32),
-            last=V((TENSOR, 8, PAIR), F32),
-            yx_gu0=V((ROWS, WIDTH), BF),
-            y_gu=V((4, PAIR, WIDTH), BF),
-            s_gu=V((ROWS, WIDTH), BF),
-            yx_gu=V((ROWS, WIDTH), BF),
-            yx_down=V((2, UNITS, ROWS), BF),
-        )
-        | sems(
-            g_send=1,
-            g_recv=1,
-            q_send=1,
-            q_recv=1,
-            b_send=1,
-            b_recv=1,
-            x_send=4,
-            x_recv=4,
-            gu_send=4,
-            gu_recv=4,
-            ot_send=1,
-            ot_recv=1,
-            o_send=8,
-            o_recv=8,
-            m_send=3,
-            m_recv=3,
+            tx_send=4,
+            tx_recv=4,
             t_send=1,
             t_recv=1,
             od_send=1,
             od_recv=1,
             l_send=1,
             l_recv=1,
-            local=8,
+            local=48,
         ),
     )
     values = {name: getattr(c, name) for name in STORED}

time: 207 us -> 194 us (0.937)
  Pallas kernels: 206 us -> 193 us
    pallas_call x3 -> x2, Pallas kernels: 206 us -> 193 us  [call(): pl.pallas_call(lambda *refs: kernel(Refs(names, refs, loads, saves)), out...]
where the time goes in v4:
time: 194 us
  Pallas kernels  193 us (99%)
    pallas_call x2, Pallas kernels, call(): pl.pallas_call(lambda *refs: kernel(Refs(names, refs, loads, saves)), out...  193 us

profile of v4, /device:TPU:1, one launch (start us, length us, event | category | flops | bytes accessed | tf_op | source)
XLA Modules:
  0.0 193.9 jit_solution(16734149915393137107)
XLA Ops:
  0.6 190.3 %layer_kernel.1 = (bf16[128,1024]{1,0:T(8,128)(2,1)}, bf16[128,1024]{1,0:T(8,128)(2,1)}, f32[1,8]{1,0:T(1,128)}, f32[64,128]{1,0:T(8,128)}, f32[8,1024]{1,0:T(8,...) custom-call(bf16[128,1024]{1,0:T(8,128)(2,1)} %bitcast.15, ...), custom_call_target="tpu_custom_call" | custom-call | tf_op jit(solution)/shard_map/layer_kernel/pallas_call | solution.py:1547
  190.9 2.8 %store_kernel.1 = (bf16[128,1024]{1,0:T(8,128)(2,1)}, bf16[128,1024]{1,0:T(8,128)(2,1)}, f32[1,8]{1,0:T(1,128)}, f32[64,128]{1,0:T(8,128)}, f32[8,1024]{1,0:T(8,...) custom-call(bf16[128,1024]{1,0:T(8,128)(2,1)} %get-tuple-element.30., ...), custom_call_target="tpu_custom_call" | custom-call | tf_op jit(solution)/shard_map/store_kernel/pallas_call | solution.py:1547

commit v5 on v4

--- a/solution.py
+++ b/solution.py
@@ -132,46 +132,6 @@
         pl.semaphore_wait(barrier, TENSOR + DP - 2)
 
 
-class Spread:
-    def __init__(self, place, block, send, recv, source=None):
-        self.place, self.block, self.send, self.recv = place, block, send, recv
-        self.source = source
-
-    def copy(self, number, index, dest, source=None):
-        src = self.block(index) if source is None else source
-        return remote(
-            src, self.block(index), self.send.at[number], self.recv.at[index], TP, dest
-        )
-
-    def own(self, k):
-        dest = self.place.twin if k == 0 else self.place.same_core(k)
-        return self.copy(k, self.place.t, dest, self.source)
-
-    def start(self):
-        for k in range(1, CHIPS):
-            self.own(k).start()
-        self.own(0).start()
-
-    def passed(self, k):
-        return self.copy(CHIPS + k, self.place.same_core(k), self.place.twin)
-
-    def arrived(self, index):
-        self.copy(0, index, self.place.twin).wait_recv()
-
-    def first(self, k):
-        self.arrived(self.place.same_core(k))
-        self.passed(k).start()
-
-    def second(self, k):
-        self.arrived(2 * self.place.chip_at(k) + 1 - self.place.core)
-
-    def end(self):
-        for k in range(CHIPS):
-            self.own(k).wait_send()
-        for k in range(1, CHIPS):
-            self.passed(k).wait_send()
-
-
 class Ring:
     def __init__(self, place, block, half, send, recv, most, source=None, source_half=None):
         self.place, self.block, self.half = place, block, half
@@ -277,25 +237,30 @@
 
 class Copies:
     def __init__(self, sems):
-        self.sems, self.pending, self.used = sems, [], 0
+        self.sems, self.pending, self.free, self.used = sems, [], [], 0
 
     def start(self, src, dst):
-        copy = pltpu.make_async_copy(src, dst, self.sems.at[self.used])
+        if self.free:
+            number = self.free.pop()
+        else:
+            number, self.used = self.used, self.used + 1
+        copy = pltpu.make_async_copy(src, dst, self.sems.at[number])
         copy.start()
-        self.used += 1
-        self.pending.append(copy)
+        self.pending.append((copy, number))
         return copy
 
     def wait(self, count=None):
         count = len(self.pending) if count is None else count
-        for copy in self.pending[:count]:
+        for copy, number in self.pending[:count]:
             copy.wait()
+            self.free.append(number)
         self.pending = self.pending[count:]
 
     def need(self, *copies):
         for copy in copies:
             copy.wait()
-            self.pending = [other for other in self.pending if other is not copy]
+            self.free += [number for other, number in self.pending if other is copy]
+            self.pending = [pair for pair in self.pending if pair[0] is not copy]
 
 
 def lanes(shape):
@@ -590,13 +555,17 @@
             dest,
         )
 
-    def tile_two(k, src):
+    def y_peer(k):
+        return 2 * at.y_at(k) + at.x
+
+    def tile_two(src, dest, recv):
         ref = r.tile_all.at[src]
-        return remote(ref, ref, r.t2_send.at[0], r.t2_recv.at[0], SP, at.dp_at(k))
-
-    def rows_dp(k, src):
-        return remote(
-            r.rows, r.row_dp.at[src], r.rd_send.at[0], r.rd_recv.at[0], SP, at.dp_at(k)
+        return remote(ref, ref, r.t2_send.at[0], recv.at[0], SP, dest)
+
+    def rows_dp(src, dest, recv, source=None):
+        ref = r.row_dp.at[src]
+        return remote(
+            ref if source is None else source, ref, r.rd_send.at[0], recv.at[0], SP, dest
         )
 
     def wq_dp(k, src):
@@ -628,18 +597,26 @@
     r.keyvals_t[:, 0:REACH] = jnp.zeros((2 * HEAD, REACH), BF)
 
     all_landed(r.tile_all.at[0, pl.ds(0, 15)], r.t1_recv.at[0], at)
-    for k in range(1, DP):
-        tile_two(k, d).start()
-    for k in range(1, DP):
-        rows_dp(k, d).start()
+    tile_two(d, at.across, r.t2x_recv).start()
+    rows_dp(d, at.across, r.rdx_recv, r.rows).start()
+    for k in range(1, 4):
+        tile_two(d, y_peer(k), r.t2_recv).start()
+        rows_dp(d, y_peer(k), r.rd_recv, r.rows).start()
     for stream in first_expert:
         stream.start_x()
-        stream.start_y()
     for i in range(1, 4):
         ring_h.pass_on(i)
+    tile_two(at.across, at.across, r.t2x_recv).wait_recv()
+    for k in range(1, 4):
+        tile_two(at.across, y_peer(k), r.t2_recv).start()
+    rows_dp(at.across, at.across, r.rdx_recv).wait_recv()
+    for k in range(1, 4):
+        rows_dp(at.across, y_peer(k), r.rd_recv).start()
+    for stream in first_expert:
+        stream.start_y()
     seven_wq = r.wq_all.at[pl.ds(0, HEAD), pl.ds(0, 7 * ROWS)]
     all_landed(seven_wq, r.wq_recv.at[0], at)
-    all_landed(r.tile_all.at[pl.ds(0, 7)], r.t2_recv.at[0], at)
+    all_landed(r.tile_all.at[pl.ds(0, 6)], r.t2_recv.at[0], at)
     for j in range(DP):
         both = r.tile_all[j].astype(F32)
         r.wqk[j * ROWS : (j + 1) * ROWS, ROWS:PAIR] = both[:, 0:8].reshape(ROWS, ROWS).astype(BF)
@@ -668,7 +645,7 @@
 
         @pl.when(i == 2)
         def _():
-            all_landed(r.row_dp.at[pl.ds(0, 7)], r.rd_recv.at[0], at)
+            all_landed(r.row_dp.at[pl.ds(0, 6)], r.rd_recv.at[0], at)
             both = r.row_dp[...].astype(F32)
             r.wqkv_own[0:HEAD, :] = r.wq_all[0:HEAD, :]
             r.wqkv_own[HEAD : 2 * HEAD, :] = both[:, 0:8].reshape(HEAD, WIDTH).astype(BF)
@@ -707,7 +684,6 @@
         r.keyvals_t[:, later] = keyval.T.astype(BF)
 
     r.save("normed")
-    ring_o.pass_on(1)
 
     def att_copy(dest, src):
         return remote(
@@ -721,22 +697,25 @@
 
     @pl.loop(0, CHIPS)
     def _(i):
-        for step, ring, chips in (
-            (0, ring_o, (2, 3)),
-            (4, ring_o, (4, 5)),
-        ):
-
-            @pl.when(i == step)
-            def _(ring=ring, chips=chips):
-                for k in chips:
-                    ring.pass_on(k)
-
-        @pl.when(i == 2)
+        @pl.when(i == 0)
         def _():
             for stream in first_expert:
                 stream.from_across()
+
+        @pl.when(i == 1)
+        def _():
+            for k in range(1, 4):
+                ring_o.pass_on(k)
+
+        @pl.when(i == 3)
+        def _():
             for stream in first_expert:
                 stream.from_y()
+
+        @pl.when(i == 5)
+        def _():
+            ring_o.pass_on(4)
+            ring_o.pass_on(5)
 
         block = at.chip_at(i + 1)
         here = aligned(block, PAIR)
@@ -772,11 +751,11 @@
             att_copy(at.twin, t).start()
 
     ring_c.pass_on(1)
-    for stream in second_expert:
-        stream.start_x()
     r.att_t[aligned(t, HEAD), :] = r.att_src[t]
     ring_o.pass_on(6)
     ring_o.pass_on(7)
+    for stream in first_expert:
+        stream.from_y_across()
     for i in range(CHIPS):
         ring_o.second(i)
 
@@ -791,8 +770,6 @@
         r.out_t[aligned(2 * j + 1, ROWS), :] = second.astype(BF)
 
     r.save("out_t")
-    for stream in first_expert:
-        stream.from_y_across()
     all_landed(r.att_t.at[pl.ds(0, 15 * HEAD)], r.a_recv.at[0], at)
     attended = r.att_t[...].astype(F32).T.astype(BF)
     r.att_rows[...] = attended
@@ -803,6 +780,7 @@
     ring = whole_ring(at, r.nm_all, r.g_send, r.g_recv)
     ring.start()
     for stream in second_expert:
+        stream.start_x()
         stream.start_y()
     ring_c.pass_on(2)
     ring_c.pass_on(3)
@@ -830,14 +808,25 @@
         (r.nc_send, r.nc_recv, r.n_send, r.n_recv),
     )
     ring_w = whole_ring(at, r.wqkv, r.h_send, r.h_recv, r.wqkv_own)
-    copies.start(r.wqkv_own, r.wqkv.at[aligned(t, ROWS)])
-
-    def moe_along(j):
-        return remote(
-            moe_sums(2 * j, 2),
-            r.m_landed.at[j],
-            r.m_send.at[j],
-            r.m_recv.at[j],
+    own_weights = copies.start(r.wqkv_own, r.wqkv.at[aligned(t, ROWS)])
+
+    def moe_first():
+        return remote(
+            moe_sums(0, 2),
+            r.m_landed.at[0],
+            r.m_send.at[0],
+            r.m_recv.at[0],
+            TP,
+            at.near_core(SUM_Z[0], 0),
+        )
+
+    def moe_along(j, part):
+        number = 2 * j - 1 + part
+        return remote(
+            moe_sums(2 * j + part),
+            r.m_landed.at[j, pl.ds(part * ROWS, ROWS)],
+            r.m_send.at[number],
+            r.m_recv.at[number],
             TP,
             at.near_core(SUM_Z[2 * j], 0),
         )
@@ -1005,7 +994,7 @@
 
             @pl.when(i == 2)
             def _():
-                moe_along(0).start()
+                moe_first().start()
 
             for step, chips in ((0, (2, 3)), (2, (4, 5))):
 
@@ -1044,14 +1033,54 @@
     joined.join(2)
     halves_n.add(CHIPS - 1)
     halves_m.add(CHIPS - 1)
+    for j in (1, 2):
+        moe_along(j, 0).start()
+    def gu_loads(e):
+        ref, first = (r.n_first, WIDTH) if e == 0 else (r.proj_grads, 0)
+        places = [ref.at[pl.ds(first + k * PAIR, PAIR)] for k in range(3)]
+        loads = []
+        for k in range(3):
+            gu_over_y(e, k + 1).wait_recv()
+            loads.append(copies.start(r.y_gu.at[e, k], places[k]))
+        return places, loads
+
+    def gu_sums(e, places, loads):
+        copies.need(*loads)
+        total = r.gus[e, aligned(at.y, PAIR), :].astype(F32)
+        for place in places:
+            total = total + place[...].astype(F32)
+        r.ys_gu[e, 0] = total[0:ROWS].astype(BF)
+        r.ys_gu[e, 1] = total[ROWS:PAIR].astype(BF)
+        gu_across(e).start()
+
+    def down_loads(e):
+        places = [
+            r.weighted.at[pl.ds(k * UNITS, UNITS), pl.ds(e * PAIR, PAIR)] for k in range(3)
+        ]
+        loads = []
+        for k in range(3):
+            down_over_y(e, k + 1).wait_recv()
+            loads.append(copies.start(r.y_down.at[e, k], places[k]))
+        return places, loads
+
+    def down_sums(e, places, loads):
+        copies.need(*loads)
+        total = r.down_grads[e, :, aligned(at.y, PAIR)].astype(F32)
+        for place in places:
+            total = total + place[...].astype(F32)
+        r.ys_down[e, 0] = total[:, 0:ROWS].astype(BF)
+        r.ys_down[e, 1] = total[:, ROWS:PAIR].astype(BF)
+        down_across(e).start()
+
     out_rows = r.n_first.at[pl.ds(0, WIDTH)]
-    copies.start(r.out_t_d, out_rows)
+    out_load = copies.start(r.out_t_d, out_rows)
     for stream in second_expert:
         stream.end()
     down_gradients(1)
     for k in range(1, 4):
         down_over_y(1, k).start()
     gate_up_gradients(1)
+    first_down, first_gu = down_loads(0), gu_loads(0)
     for k in range(1, 4):
         gu_over_y(1, k).start()
     r.gate_all[t] = r.gate_src[t]
@@ -1080,7 +1109,7 @@
     turned = grad.T.reshape(DP, TENSOR, 8, ROWS).transpose(1, 0, 2, 3)
     r.att_grad_t, r.mid_t = r.att_t, r.wqk.at[:, pl.ds(0, ROWS)]
     r.mid_t[...] = turned.reshape(WIDTH, ROWS).astype(BF)
-    copies.wait()
+    copies.need(out_load)
     r.att_grad_t[...] = dot(grad.astype(BF), out_rows[...]).T.astype(BF)
 
     def back_copy(k, src):
@@ -1099,15 +1128,6 @@
     own_grads = copies.start(
         r.att_grad_t.at[aligned(t, HEAD), :], r.grads.at[:, aligned(t, ROWS)]
     )
-    moe_along(1).start()
-    moe_along(2).start()
-    normed_load = copies.start(r.normed_d, r.normed)
-    for number in (6, 7):
-        ring_w.pass_on(number)
-    for i in range(CHIPS):
-        ring_w.second(i)
-    ring_c.end()
-    weights_load = copies.start(r.wqkv, r.cots)
     joined.end()
     r.n_sums[...] = (
         dot(r.mid_t[...], r.att_rows[...]).reshape(CHIPS, ROWS, WIDTH).astype(BF)
@@ -1134,38 +1154,9 @@
     r.tail = r.n_parts.at[0]
     r.s_gu, r.m_joined = r.m_parts.at[0, pl.ds(0, ROWS)], r.m_parts.at[0, pl.ds(ROWS, ROWS)]
 
-    def gu_sums(e):
-        places = [r.proj_grads.at[pl.ds((3 * e + k) * PAIR, PAIR)] for k in range(3)]
-        loads = []
-        for k in range(3):
-            gu_over_y(e, k + 1).wait_recv()
-            loads.append(copies.start(r.y_gu.at[e, k], places[k]))
-        copies.need(*loads)
-        total = r.gus[e, aligned(at.y, PAIR), :].astype(F32)
-        for place in places:
-            total = total + place[...].astype(F32)
-        r.ys_gu[e, 0] = total[0:ROWS].astype(BF)
-        r.ys_gu[e, 1] = total[ROWS:PAIR].astype(BF)
-        gu_across(e).start()
-
-    def down_sums(e):
-        places = [
-            r.weighted.at[pl.ds(k * UNITS, UNITS), pl.ds(e * PAIR, PAIR)] for k in range(3)
-        ]
-        loads = []
-        for k in range(3):
-            down_over_y(e, k + 1).wait_recv()
-            loads.append(copies.start(r.y_down.at[e, k], places[k]))
-        copies.need(*loads)
-        total = r.down_grads[e, :, aligned(at.y, PAIR)].astype(F32)
-        for place in places:
-            total = total + place[...].astype(F32)
-        r.ys_down[e, 0] = total[:, 0:ROWS].astype(BF)
-        r.ys_down[e, 1] = total[:, ROWS:PAIR].astype(BF)
-        down_across(e).start()
-
-    down_sums(0)
-    gu_sums(0)
+    down_sums(0, *first_down)
+    gu_sums(0, *first_gu)
+    normed_load = copies.start(r.normed_d, r.normed)
 
     def out_along(k):
         return remote(
@@ -1186,7 +1177,20 @@
     r.out_twins[...] = (
         r.n_sums[:, aligned(at.core, HEAD), :].astype(F32) + r.out_twins[...].astype(F32)
     ).astype(BF)
-    out_along(1).start()
+    for k in range(1, 4):
+        out_along(k).start()
+    def moe_across():
+        return remote(
+            r.m_joined, r.m_crossed, r.mx_send.at[0], r.mx_recv.at[0], TP, at.near_core(0, 1)
+        )
+
+    moe_first().wait_recv()
+    across = moe_sums(6)[...].astype(F32) + r.m_landed[0, 0:ROWS].astype(F32)
+    for j in (1, 2):
+        moe_along(j, 0).wait_recv()
+        across = across + r.m_landed[j, 0:ROWS].astype(F32)
+    r.m_joined[...] = across.astype(BF)
+    moe_across().start()
     all_landed(r.grads.at[:, pl.ds(0, 15 * ROWS)], r.b_recv.at[0], at)
     copies.need(own_grads)
     copies.need(copies.start(r.grads, r.grads_t.at[pl.ds(HEAD, HEAD)]))
@@ -1269,23 +1273,36 @@
         grad_copy(k, t).start()
     r.back_all[t] = r.back_src[t]
     r.query_all[t] = r.query_src[t]
-    for k in (2, 3):
-        out_along(k).start()
-    down_sums(1)
-    across, own = moe_sums(6)[...].astype(F32), middle + moe_sums(7)[...].astype(F32)
-    for j in range(3):
-        moe_along(j).wait_recv()
-        across = across + r.m_landed[j, 0:ROWS].astype(F32)
-        own = own + r.m_landed[j, ROWS:PAIR].astype(F32)
-    r.m_joined[...] = across.astype(BF)
-    r.mid[...] = own
-
-    def moe_across():
-        return remote(
-            r.m_joined, r.m_crossed, r.mx_send.at[0], r.mx_recv.at[0], TP, at.near_core(0, 1)
-        )
-
-    moe_across().start()
+    for j in (1, 2):
+        moe_along(j, 1).start()
+    down_sums(1, *down_loads(1))
+    landed = [
+        [r.nm_all.at[pl.ds((2 * k + x) * HEAD, HEAD)] for x in range(2)] for k in range(3)
+    ]
+    ring.end()
+    loads = []
+    for k in range(3):
+        out_along(k + 1).wait_recv()
+        for x in range(2):
+            loads.append(copies.start(r.out_landed.at[k, x], landed[k][x]))
+    copies.need(*loads)
+
+    def out_total(x):
+        total = r.out_twins[2 * at.z + x].astype(F32)
+        for k in range(3):
+            rows = aligned(2 * k + x, HEAD)
+            total = total + r.nm_all[rows, :].astype(F32)
+        return total
+
+    r.out_joined[...] = out_total(1 - at.x_far).astype(BF)
+    out_across().start()
+    for number in (6, 7):
+        ring_w.pass_on(number)
+    for i in range(CHIPS):
+        ring_w.second(i)
+    ring_c.end()
+    copies.need(own_weights)
+    weights_load = copies.start(r.wqkv, r.cots)
     copies.need(normed_load)
     r.tail[0 : 3 * HEAD, :] = dot(r.tail_left[...], r.normed[...]).astype(BF)
 
@@ -1339,27 +1356,7 @@
     for k in range(1, DP):
         tail_copy(k).start()
 
-    landed = [
-        [r.nm_all.at[pl.ds((2 * k + x) * HEAD, HEAD)] for x in range(2)] for k in range(3)
-    ]
-    ring.end()
-    loads = []
-    for k in range(3):
-        out_along(k + 1).wait_recv()
-        for x in range(2):
-            loads.append(copies.start(r.out_landed.at[k, x], landed[k][x]))
-    copies.need(*loads)
-
-    def out_total(x):
-        total = r.out_twins[2 * at.z + x].astype(F32)
-        for k in range(3):
-            rows = aligned(2 * k + x, HEAD)
-            total = total + r.nm_all[rows, :].astype(F32)
-        return total
-
-    r.out_joined[...] = out_total(1 - at.x_far).astype(BF)
-    out_across().start()
-    gu_sums(1)
+    gu_sums(1, *gu_loads(1))
     out_across().wait_recv()
     crossed = r.proj_grads.at[pl.ds(6 * PAIR, HEAD)]
     copies.need(copies.start(r.out_crossed, crossed))
@@ -1401,9 +1398,14 @@
     r.last[t] = r.pieces[t]
 
     moe_across().wait_recv()
-    crossed = r.proj_grads.at[pl.ds(7 * PAIR, ROWS)]
-    copies.need(copies.start(r.m_crossed, crossed))
-    r.output[...] = (r.mid[...] + crossed[...].astype(F32)).astype(BF)
+    crossed = r.nm_all.at[pl.ds(WIDTH + PAIR, ROWS)]
+    load = copies.start(r.m_crossed, crossed)
+    own = r.mid[...] + moe_sums(7)[...].astype(F32) + r.m_landed[0, ROWS:PAIR].astype(F32)
+    for j in (1, 2):
+        moe_along(j, 1).wait_recv()
+        own = own + r.m_landed[j, ROWS:PAIR].astype(F32)
+    copies.need(load)
+    r.output[...] = (own + crossed[...].astype(F32)).astype(BF)
     r.save("output")
     loads, crossed = [], []
     for e in range(2):
@@ -1449,8 +1451,10 @@
     all_sent(r.pieces.at[pl.ds(0, 15)], r.l_send.at[0], at)
     all_sent(r.tail_in.at[pl.ds(0, 7)], r.t_send.at[0], at)
     all_sent(r.out_in.at[pl.ds(0, 7)], r.od_send.at[0], at)
-    for j in range(3):
-        moe_along(j).wait_send()
+    moe_first().wait_send()
+    for j in (1, 2):
+        for part in range(2):
+            moe_along(j, part).wait_send()
     moe_across().wait_send()
     for k in range(1, 4):
         out_along(k).wait_send()
@@ -1707,6 +1711,8 @@
             t1_recv=1,
             t2_send=1,
             t2_recv=1,
+            t2x_recv=1,
+            rdx_recv=1,
             rd_send=1,
             rd_recv=1,
             wq_send=1,
@@ -1723,8 +1729,8 @@
             n_recv=3,
             mtw_send=SLOTS,
             mtw_recv=SLOTS,
-            m_send=3,
-            m_recv=3,
+            m_send=5,
+            m_recv=5,
             mx_send=1,
             mx_recv=1,
             gg_send=1,
@@ -1751,7 +1757,7 @@
             od_recv=1,
             l_send=1,
             l_recv=1,
-            local=48,
+            local=20,
         ),
     )
     values = {name: getattr(c, name) for name in STORED}

time: 194 us -> 189 us (0.974)
  Pallas kernels: 193 us -> 188 us
    pallas_call x2, Pallas kernels: 193 us -> 188 us  [call(): pl.pallas_call(lambda *refs: kernel(Refs(names, refs, loads, saves)), out...]
where the time goes in v5:
time: 189 us
  Pallas kernels  188 us (99%)
    pallas_call x2, Pallas kernels, call(): pl.pallas_call(lambda *refs: kernel(Refs(names, refs, loads, saves)), out...  188 us

profile of v5, /device:TPU:1, one launch (start us, length us, event | category | flops | bytes accessed | tf_op | source)
XLA Modules:
  0.0 189.0 jit_solution(11687368028508962626)
XLA Ops:
  0.6 185.3 %layer_kernel.1 = (bf16[128,1024]{1,0:T(8,128)(2,1)}, bf16[128,1024]{1,0:T(8,128)(2,1)}, f32[1,8]{1,0:T(1,128)}, f32[64,128]{1,0:T(8,128)}, f32[8,1024]{1,0:T(8,...) custom-call(bf16[128,1024]{1,0:T(8,128)(2,1)} %bitcast.15, ...), custom_call_target="tpu_custom_call" | custom-call | tf_op jit(solution)/shard_map/layer_kernel/pallas_call | solution.py:1551
  186.0 2.8 %store_kernel.1 = (bf16[128,1024]{1,0:T(8,128)(2,1)}, bf16[128,1024]{1,0:T(8,128)(2,1)}, f32[1,8]{1,0:T(1,128)}, f32[64,128]{1,0:T(8,128)}, f32[8,1024]{1,0:T(8,...) custom-call(bf16[128,1024]{1,0:T(8,128)(2,1)} %get-tuple-element.30., ...), custom_call_target="tpu_custom_call" | custom-call | tf_op jit(solution)/shard_map/store_kernel/pallas_call | solution.py:1551

commit v6 on v5

--- a/solution.py
+++ b/solution.py
@@ -856,6 +856,17 @@
     def across_x(number, src, dst):
         return remote(src, dst, r.tx_send.at[number], r.tx_recv.at[number], SP, at.across)
 
+    def gu_half(part):
+        rows = pl.ds(part * HEAD, HEAD)
+        return remote(
+            r.ys_gu.at[1, 1 - at.x, rows],
+            r.yx_gu.at[1, rows],
+            r.tx_send.at[1 + 3 * part],
+            r.tx_recv.at[1 + 3 * part],
+            SP,
+            at.across,
+        )
+
     def gu_across(e):
         return across_x(e, r.ys_gu.at[e, 1 - at.x], r.yx_gu.at[e])
 
@@ -1033,8 +1044,6 @@
     joined.join(2)
     halves_n.add(CHIPS - 1)
     halves_m.add(CHIPS - 1)
-    for j in (1, 2):
-        moe_along(j, 0).start()
     def gu_loads(e):
         ref, first = (r.n_first, WIDTH) if e == 0 else (r.proj_grads, 0)
         places = [ref.at[pl.ds(first + k * PAIR, PAIR)] for k in range(3)]
@@ -1051,7 +1060,7 @@
             total = total + place[...].astype(F32)
         r.ys_gu[e, 0] = total[0:ROWS].astype(BF)
         r.ys_gu[e, 1] = total[ROWS:PAIR].astype(BF)
-        gu_across(e).start()
+        (gu_half(0) if e else gu_across(0)).start()
 
     def down_loads(e):
         places = [
@@ -1125,9 +1134,7 @@
 
     for k in range(1, TENSOR):
         back_copy(k, t).start()
-    own_grads = copies.start(
-        r.att_grad_t.at[aligned(t, HEAD), :], r.grads.at[:, aligned(t, ROWS)]
-    )
+    r.grads[:, aligned(t, ROWS)] = r.att_grad_t[aligned(t, HEAD), :]
     joined.end()
     r.n_sums[...] = (
         dot(r.mid_t[...], r.att_rows[...]).reshape(CHIPS, ROWS, WIDTH).astype(BF)
@@ -1145,9 +1152,8 @@
 
     out_half().start()
     r.kv_sum, r.query_src = r.gates, r.att_src
-    r.tail_left, r.grads_t = r.weighted_t.at[pl.ds(PAIR, 3 * HEAD)], r.weighted_t
+    r.tail_left = r.weighted_t.at[pl.ds(0, 3 * HEAD)]
     r.kv_sum[...] = jnp.zeros((LENGTH, 2 * HEAD), F32)
-    r.grads_t[0:HEAD, :] = jnp.zeros((HEAD, LENGTH), BF)
     all_sent(r.att_src.at[pl.ds(0, 15)], r.a_send.at[0], at)
     halves_n.end()
     halves_m.end()
@@ -1179,21 +1185,7 @@
     ).astype(BF)
     for k in range(1, 4):
         out_along(k).start()
-    def moe_across():
-        return remote(
-            r.m_joined, r.m_crossed, r.mx_send.at[0], r.mx_recv.at[0], TP, at.near_core(0, 1)
-        )
-
-    moe_first().wait_recv()
-    across = moe_sums(6)[...].astype(F32) + r.m_landed[0, 0:ROWS].astype(F32)
-    for j in (1, 2):
-        moe_along(j, 0).wait_recv()
-        across = across + r.m_landed[j, 0:ROWS].astype(F32)
-    r.m_joined[...] = across.astype(BF)
-    moe_across().start()
     all_landed(r.grads.at[:, pl.ds(0, 15 * ROWS)], r.b_recv.at[0], at)
-    copies.need(own_grads)
-    copies.need(copies.start(r.grads, r.grads_t.at[pl.ds(HEAD, HEAD)]))
     r.need("cosine_t", "sine_t")
 
     def query_copy(dest, src):
@@ -1213,7 +1205,7 @@
         query = r.queries[here, :]
         start_row = r.starts[:, here]
         stat = r.stats[:, here]
-        grad_t = r.grads_t[0 : 2 * HEAD, here]
+        grad_t = jnp.concatenate([jnp.zeros((HEAD, PAIR), BF), r.grads[:, here]], axis=0)
         grad_rows = grad_t.astype(F32).T.astype(BF)
         head = r.heads_t[:, here]
         delta = jnp.sum(head * grad_t[HEAD : 2 * HEAD, :].astype(F32), axis=0, keepdims=True)
@@ -1273,8 +1265,9 @@
         grad_copy(k, t).start()
     r.back_all[t] = r.back_src[t]
     r.query_all[t] = r.query_src[t]
-    for j in (1, 2):
-        moe_along(j, 1).start()
+    for part in range(2):
+        for j in (1, 2):
+            moe_along(j, part).start()
     down_sums(1, *down_loads(1))
     landed = [
         [r.nm_all.at[pl.ds((2 * k + x) * HEAD, HEAD)] for x in range(2)] for k in range(3)
@@ -1342,19 +1335,22 @@
         row == 0, gain_one_grad, jnp.where(row == 1, r.gain_grad[...], 0.0)
     ).astype(BF)
 
-    def tail_copy(k):
-        dest = at.dp_at(k)
-        return remote(
-            r.tail.at[pl.ds(0, TAIL), aligned(dest, ROWS)],
-            r.tail_in.at[k],
-            r.t_send.at[0],
-            r.t_recv.at[0],
+    def tail_along(k):
+        y = at.y_at(k)
+        return remote(
+            r.tail.at[pl.ds(0, TAIL), aligned(y, PAIR)],
+            r.tail_in.at[k - 1],
+            r.t_send.at[k],
+            r.t_recv.at[k],
             SP,
-            dest,
-        )
-
-    for k in range(1, DP):
-        tail_copy(k).start()
+            2 * y + at.x,
+        )
+
+    def tail_across():
+        return remote(r.tail_src, r.tail_x, r.t_send.at[0], r.t_recv.at[0], SP, at.across)
+
+    for k in range(1, 4):
+        tail_along(k).start()
 
     gu_sums(1, *gu_loads(1))
     out_across().wait_recv()
@@ -1362,23 +1358,71 @@
     copies.need(copies.start(r.out_crossed, crossed))
     r.out_rows[...] = out_total(at.x_far) + crossed[...].astype(F32)
 
-    def out_copy(k):
-        dest = at.dp_at(k)
-        return remote(
-            r.out_rows.at[aligned(dest, 8), :],
-            r.out_in.at[k],
+    def out_dp_along(k):
+        y = at.y_at(k)
+        return remote(
+            r.out_rows.at[aligned(y, 16), :],
+            r.out_in.at[k - 1],
+            r.od_send.at[k],
+            r.od_recv.at[k],
+            SP,
+            2 * y + at.x,
+        )
+
+    def out_dp_across():
+        return remote(
+            r.out_sum.at[aligned(1 - at.x, 8), :],
+            r.out_x,
             r.od_send.at[0],
             r.od_recv.at[0],
             SP,
-            dest,
-        )
-
-    for k in range(1, DP):
-        out_copy(k).start()
-    total = r.tail[0:TAIL, aligned(d, ROWS)].astype(F32)
-    all_landed(r.tail_in.at[pl.ds(0, 7)], r.t_recv.at[0], at)
-    for k in range(1, DP):
-        total = total + r.tail_in[k].astype(F32)
+            at.across,
+        )
+
+    for k in range(1, 4):
+        out_dp_along(k).start()
+    def moe_across():
+        return remote(
+            r.m_joined, r.m_crossed, r.mx_send.at[0], r.mx_recv.at[0], TP, at.near_core(0, 1)
+        )
+
+    moe_first().wait_recv()
+    across = moe_sums(6)[...].astype(F32) + r.m_landed[0, 0:ROWS].astype(F32)
+    for j in (1, 2):
+        moe_along(j, 0).wait_recv()
+        across = across + r.m_landed[j, 0:ROWS].astype(F32)
+    r.m_joined[...] = across.astype(BF)
+    moe_across().start()
+    loads, crossed = [], []
+    for e in range(2):
+        down_across(e).wait_recv()
+        crossed.append(r.weighted.at[pl.ds(3 * UNITS, UNITS), pl.ds(e * ROWS, ROWS)])
+        loads.append(copies.start(r.yx_down.at[e], crossed[-1]))
+    gu_across(0).wait_recv()
+    crossed.append(r.nm_all.at[pl.ds(WIDTH, ROWS)])
+    loads.append(copies.start(r.yx_gu.at[0], crossed[-1]))
+    copies.need(*loads)
+    for e in range(2):
+        r.down_out[e] = r.ys_down[e, at.x].astype(F32) + crossed[e][...].astype(F32)
+    r.mid_grad[...] = r.ys_gu[0, at.x].astype(F32) + crossed[2][...].astype(F32)
+    copies.start(r.mid_grad, r.gu_out.at[0])
+    r.save("down_out")
+    total = r.tail[0:TAIL, aligned(at.y, PAIR)].astype(F32)
+    for k in range(1, 4):
+        tail_along(k).wait_recv()
+        total = total + r.tail_in[k - 1].astype(F32)
+    r.scores[0:TAIL, :] = total
+    r.tail_src[...] = r.scores[0:TAIL, aligned(1 - at.x, ROWS)].astype(BF)
+    tail_across().start()
+    gu_half(1).start()
+    total = r.out_rows[aligned(at.y, 16), :]
+    for k in range(1, 4):
+        out_dp_along(k).wait_recv()
+        total = total + r.out_in[k - 1]
+    r.out_sum[...] = total
+    out_dp_across().start()
+    tail_across().wait_recv()
+    total = r.scores[0:TAIL, aligned(at.x, ROWS)] + r.tail_x[...].astype(F32)
     r.query_out[...] = total[0:HEAD, :]
     r.save("query_out")
     turned = jnp.concatenate(
@@ -1397,36 +1441,23 @@
         last_copy(k, t).start()
     r.last[t] = r.pieces[t]
 
-    moe_across().wait_recv()
-    crossed = r.nm_all.at[pl.ds(WIDTH + PAIR, ROWS)]
-    load = copies.start(r.m_crossed, crossed)
     own = r.mid[...] + moe_sums(7)[...].astype(F32) + r.m_landed[0, ROWS:PAIR].astype(F32)
     for j in (1, 2):
         moe_along(j, 1).wait_recv()
         own = own + r.m_landed[j, ROWS:PAIR].astype(F32)
-    copies.need(load)
-    r.output[...] = (own + crossed[...].astype(F32)).astype(BF)
+    place = r.nm_all.at[pl.ds(WIDTH + PAIR, ROWS)]
+    moe_across().wait_recv()
+    copies.need(copies.start(r.m_crossed, place))
+    r.output[...] = (own + place[...].astype(F32)).astype(BF)
     r.save("output")
-    loads, crossed = [], []
-    for e in range(2):
-        down_across(e).wait_recv()
-        crossed.append(r.weighted.at[pl.ds(3 * UNITS, UNITS), pl.ds(e * ROWS, ROWS)])
-        loads.append(copies.start(r.yx_down.at[e], crossed[-1]))
-    for e in range(2):
-        gu_across(e).wait_recv()
-        crossed.append(r.nm_all.at[pl.ds(WIDTH + e * ROWS, ROWS)])
-        loads.append(copies.start(r.yx_gu.at[e], crossed[-1]))
-    copies.need(*loads)
-    for e, total in ((0, r.mid_grad), (1, r.mid)):
-        total[...] = r.ys_gu[e, at.x].astype(F32) + crossed[2 + e][...].astype(F32)
-        copies.start(total, r.gu_out.at[e])
-        r.down_out[e] = r.ys_down[e, at.x].astype(F32) + crossed[e][...].astype(F32)
-    r.save("down_out")
-    total = r.out_rows[aligned(d, 8), :]
-    all_landed(r.out_in.at[pl.ds(0, 7)], r.od_recv.at[0], at)
-    for k in range(1, DP):
-        total = total + r.out_in[k]
-    r.out_grad[...] = total
+    for part in range(2):
+        gu_half(part).wait_recv()
+    place = r.nm_all.at[pl.ds(WIDTH + ROWS, ROWS)]
+    copies.need(copies.start(r.yx_gu.at[1], place))
+    r.mid[...] = r.ys_gu[1, at.x].astype(F32) + place[...].astype(F32)
+    copies.start(r.mid, r.gu_out.at[1])
+    out_dp_across().wait_recv()
+    r.out_grad[...] = r.out_sum[aligned(at.x, 8), :] + r.out_x[...]
     all_landed(r.last.at[pl.ds(0, 15)], r.l_recv.at[0], at)
     r.kv_out[...] = jnp.concatenate(
         [r.last[2 * j, :, 0:ROWS] + r.last[2 * j + 1, :, 0:ROWS] for j in range(CHIPS)], axis=1
@@ -1449,8 +1480,11 @@
     all_sent(r.query_src.at[pl.ds(0, 15)], r.qb_send.at[0], at)
     all_sent(r.back_src.at[pl.ds(0, 15)], r.kb_send.at[0], at)
     all_sent(r.pieces.at[pl.ds(0, 15)], r.l_send.at[0], at)
-    all_sent(r.tail_in.at[pl.ds(0, 7)], r.t_send.at[0], at)
-    all_sent(r.out_in.at[pl.ds(0, 7)], r.od_send.at[0], at)
+    for k in range(1, 4):
+        tail_along(k).wait_send()
+        out_dp_along(k).wait_send()
+    tail_across().wait_send()
+    out_dp_across().wait_send()
     moe_first().wait_send()
     for j in (1, 2):
         for part in range(2):
@@ -1464,8 +1498,9 @@
         for k in range(1, 4):
             gu_over_y(e, k).wait_send()
             down_over_y(e, k).wait_send()
-        gu_across(e).wait_send()
+        gu_half(e).wait_send()
         down_across(e).wait_send()
+    gu_across(0).wait_send()
     ring_w.end()
     copies.wait()
     r.end()
@@ -1631,7 +1666,6 @@
             normed_d=((LENGTH, WIDTH), BF),
             out_t_d=((WIDTH, WIDTH), BF),
             wqkv=((LENGTH, WIDTH), BF),
-            grads=((HEAD, LENGTH), BF),
             y_gu=((2, 3, PAIR, WIDTH), BF),
             y_down=((2, 3, UNITS, PAIR), BF),
             yx_gu=((2, ROWS, WIDTH), BF),
@@ -1687,14 +1721,19 @@
             m_landed=V((3, PAIR, WIDTH), BF),
             gate_src=V((TENSOR, 8, ROWS), F32),
             gate_all=V((TENSOR, 8, ROWS), F32),
+            grads=V((HEAD, LENGTH), BF),
             query_all=V((TENSOR, HEAD, ROWS), BF),
             back_src=V((TENSOR, ROWS, ROWS), BF),
             back_all=V((TENSOR, ROWS, ROWS), BF),
             out_twins=V((CHIPS, HEAD, WIDTH), BF),
             out_joined=V((HEAD, WIDTH), BF),
             out_rows=V((HEAD, WIDTH), F32),
-            out_in=V((DP, 8, WIDTH), F32),
-            tail_in=V((DP, TAIL, ROWS), BF),
+            out_in=V((3, 16, WIDTH), F32),
+            out_sum=V((16, WIDTH), F32),
+            out_x=V((8, WIDTH), F32),
+            tail_in=V((3, TAIL, PAIR), BF),
+            tail_src=V((TAIL, ROWS), BF),
+            tail_x=V((TAIL, ROWS), BF),
             pieces=V((TENSOR, 8, PAIR), F32),
             last=V((TENSOR, 8, PAIR), F32),
         )
@@ -1749,12 +1788,12 @@
             x_recv=8,
             y_send=8,
             y_recv=8,
-            tx_send=4,
-            tx_recv=4,
-            t_send=1,
-            t_recv=1,
-            od_send=1,
-            od_recv=1,
+            tx_send=5,
+            tx_recv=5,
+            t_send=4,
+            t_recv=4,
+            od_send=4,
+            od_recv=4,
             l_send=1,
             l_recv=1,
             local=20,

time: 189 us -> 185 us (0.979)
  Pallas kernels: 188 us -> 184 us
    pallas_call x2, Pallas kernels: 188 us -> 184 us  [call(): pl.pallas_call(lambda *refs: kernel(Refs(names, refs, loads, saves)), out...]
where the time goes in v6:
time: 185 us
  Pallas kernels  184 us (99%)
    pallas_call x2, Pallas kernels, call(): pl.pallas_call(lambda *refs: kernel(Refs(names, refs, loads, saves)), out...  184 us

profile of v6, /device:TPU:1, one launch (start us, length us, event | category | flops | bytes accessed | tf_op | source)
XLA Modules:
  0.0 184.9 jit_solution(11861327883715715805)
XLA Ops:
  0.6 181.3 %layer_kernel.1 = (bf16[128,1024]{1,0:T(8,128)(2,1)}, bf16[128,1024]{1,0:T(8,128)(2,1)}, f32[1,8]{1,0:T(1,128)}, f32[64,128]{1,0:T(8,128)}, f32[8,1024]{1,0:T(8,...) custom-call(bf16[128,1024]{1,0:T(8,128)(2,1)} %bitcast.15, ...), custom_call_target="tpu_custom_call" | custom-call | tf_op jit(solution)/shard_map/layer_kernel/pallas_call | solution.py:1586
  182.0 2.8 %store_kernel.1 = (bf16[128,1024]{1,0:T(8,128)(2,1)}, bf16[128,1024]{1,0:T(8,128)(2,1)}, f32[1,8]{1,0:T(1,128)}, f32[64,128]{1,0:T(8,128)}, f32[8,1024]{1,0:T(8,...) custom-call(bf16[128,1024]{1,0:T(8,128)(2,1)} %get-tuple-element.30., ...), custom_call_target="tpu_custom_call" | custom-call | tf_op jit(solution)/shard_map/store_kernel/pallas_call | solution.py:1586

commit v7 on v6

--- a/solution.py
+++ b/solution.py
@@ -921,6 +921,11 @@
                 def _():
                     ring_w.start()
 
+                @pl.when(i == 7)
+                def _():
+                    for stream in second_expert:
+                        stream.from_y_across()
+
             here = aligned(at.step(i) if e == 0 else at.sum_step(i), PAIR)
             nm = r.nm_all[here, :]
             place = lanes((PAIR, ROWS))
@@ -1015,20 +1020,15 @@
                         ring_w.pass_on(k)
 
     def down_gradients(e):
+        r.down_grads[e] = dot(r.weighted_t[...], r.cots[...]).astype(BF)
+
+    def gate_up_gradients(e):
         @pl.loop(0, 2)
         def _(j):
-            strip = aligned(j, PAIR)
-            r.down_grads[e, strip, :] = dot(r.weighted_t[strip, :], r.cots[...]).astype(BF)
-
-    def gate_up_gradients(e):
-        @pl.loop(0, 4)
-        def _(j):
-            strip = aligned(j, PAIR)
+            strip = aligned(j, 2 * PAIR)
             r.gus[e, strip, :] = dot(r.nm_all[:, strip], r.proj_grads[...], TN).astype(BF)
 
     one_pass(0)
-    for stream in second_expert:
-        stream.from_y_across()
     for stream in first_expert:
         stream.end()
     down_gradients(0)

time: 185 us -> 183 us (0.989)
  Pallas kernels: 184 us -> 182 us
    pallas_call x2, Pallas kernels: 184 us -> 182 us  [call(): pl.pallas_call(lambda *refs: kernel(Refs(names, refs, loads, saves)), out...]
where the time goes in v7:
time: 183 us
  Pallas kernels  182 us (99%)
    pallas_call x2, Pallas kernels, call(): pl.pallas_call(lambda *refs: kernel(Refs(names, refs, loads, saves)), out...  182 us

profile of v7, /device:TPU:1, one launch (start us, length us, event | category | flops | bytes accessed | tf_op | source)
XLA Modules:
  0.0 182.7 jit_solution(2415211669184613993)
XLA Ops:
  0.6 179.1 %layer_kernel.1 = (bf16[128,1024]{1,0:T(8,128)(2,1)}, bf16[128,1024]{1,0:T(8,128)(2,1)}, f32[1,8]{1,0:T(1,128)}, f32[64,128]{1,0:T(8,128)}, f32[8,1024]{1,0:T(8,...) custom-call(bf16[128,1024]{1,0:T(8,128)(2,1)} %bitcast.15, ...), custom_call_target="tpu_custom_call" | custom-call | tf_op jit(solution)/shard_map/layer_kernel/pallas_call | solution.py:1586
  179.7 2.8 %store_kernel.1 = (bf16[128,1024]{1,0:T(8,128)(2,1)}, bf16[128,1024]{1,0:T(8,128)(2,1)}, f32[1,8]{1,0:T(1,128)}, f32[64,128]{1,0:T(8,128)}, f32[8,1024]{1,0:T(8,...) custom-call(bf16[128,1024]{1,0:T(8,128)(2,1)} %get-tuple-element.30., ...), custom_call_target="tpu_custom_call" | custom-call | tf_op jit(solution)/shard_map/store_kernel/pallas_call | solution.py:1586

commit v8 on v7

--- a/solution.py
+++ b/solution.py
@@ -663,6 +663,11 @@
             ring_h.pass_on(6)
             ring_h.pass_on(7)
 
+        @pl.when(i == 7)
+        def _():
+            for stream in first_expert:
+                stream.from_across()
+
         ring_h.second(i)
         block = at.step(i)
         here = aligned(block, PAIR)
@@ -697,11 +702,6 @@
 
     @pl.loop(0, CHIPS)
     def _(i):
-        @pl.when(i == 0)
-        def _():
-            for stream in first_expert:
-                stream.from_across()
-
         @pl.when(i == 1)
         def _():
             for k in range(1, 4):

time: 183 us -> 183 us (level)
  no operation moved by 1% of the time
where the time goes in v8:
time: 183 us
  Pallas kernels  182 us (99%)
    pallas_call x2, Pallas kernels, call(): pl.pallas_call(lambda *refs: kernel(Refs(names, refs, loads, saves)), out...  182 us

profile of v8, /device:TPU:1, one launch (start us, length us, event | category | flops | bytes accessed | tf_op | source)
XLA Modules:
  0.0 182.7 jit_solution(15044343165406167110)
XLA Ops:
  0.6 179.1 %layer_kernel.1 = (bf16[128,1024]{1,0:T(8,128)(2,1)}, bf16[128,1024]{1,0:T(8,128)(2,1)}, f32[1,8]{1,0:T(1,128)}, f32[64,128]{1,0:T(8,128)}, f32[8,1024]{1,0:T(8,...) custom-call(bf16[128,1024]{1,0:T(8,128)(2,1)} %bitcast.15, ...), custom_call_target="tpu_custom_call" | custom-call | tf_op jit(solution)/shard_map/layer_kernel/pallas_call | solution.py:1586
  179.7 2.8 %store_kernel.1 = (bf16[128,1024]{1,0:T(8,128)(2,1)}, bf16[128,1024]{1,0:T(8,128)(2,1)}, f32[1,8]{1,0:T(1,128)}, f32[64,128]{1,0:T(8,128)}, f32[8,1024]{1,0:T(8,...) custom-call(bf16[128,1024]{1,0:T(8,128)(2,1)} %get-tuple-element.30., ...), custom_call_target="tpu_custom_call" | custom-call | tf_op jit(solution)/shard_map/store_kernel/pallas_call | solution.py:1586
